TPU v7x, 32 devices: a whole 2x2x4 slice. The times are simulated.
32 devices in a mesh: fsdp: 4 (over z), ctx: 4 (over x, core), tp: 2 (over y).
Axes of the slice: x: 2, y: 2, z: 4, core: 2. Of those that a mesh axis runs over, the one named last changes fastest.
Arguments:
- tokens: bfloat16 [4096, 1536], P(('fsdp', 'ctx')), may hold values from -6 to 6
- cotangent: bfloat16 [4096, 1536], P(('fsdp', 'ctx')), may hold values from -6 to 6
- norm_in: float32 [1, 1536], replicated, may hold values from 0.25 to 1.75
- w_qkv: bfloat16 [1, 1536, 2, 1024], P(None, ('fsdp', 'ctx'), 'tp'), may hold values from -0.15625 to 0.15625
- b_qkv: float32 [1, 2, 1024], P(None, 'tp'), may hold values from -3 to 3
- w_out: bfloat16 [1, 1536, 1536], P(None, ('fsdp', 'ctx'), 'tp'), may hold values from -0.625 to 0.625
- norm_mid: float32 [1, 1536], replicated, may hold values from 0.25 to 1.75
- w_gate_up: bfloat16 [1, 1536, 2, 8960], P(None, ('fsdp', 'ctx'), None, 'tp'), may hold values from -0.15625 to 0.15625
- w_down: bfloat16 [1, 1536, 8960], P(None, ('fsdp', 'ctx'), 'tp'), may hold values from -0.09375 to 0.09375
- segments: int32 [4096], P(('fsdp', 'ctx')), may hold values from 0 to 5, as said below
- positions: int32 [4096], P(('fsdp', 'ctx')), may hold values from 0 to 1023, as said below
Outputs:
- output: bfloat16 [4096, 1536], P(('fsdp', 'ctx'))
- grad_tokens: float32 [4096, 1536], P(('fsdp', 'ctx'))
- grad_norm_in: float32 [1, 1536], replicated
- grad_qkv: float32 [1, 1536, 2, 1024], P(None, ('fsdp', 'ctx'), 'tp')
- grad_qkv_bias: float32 [1, 2, 1024], P(None, 'tp')
- grad_out: float32 [1, 1536, 1536], P(None, ('fsdp', 'ctx'), 'tp')
- grad_norm_mid: float32 [1, 1536], replicated
- grad_gate_up: float32 [1, 1536, 2, 8960], P(None, ('fsdp', 'ctx'), None, 'tp')
- grad_down: float32 [1, 1536, 8960], P(None, ('fsdp', 'ctx'), 'tp')
Inputs may be any that keep to these rules, and one draw needn't show every extreme that they name: `segments`: within each sequence of 1024 tokens the segment number starts at 0 and rises by one at each document start; every document but a sequence's last has 200 to 2000 tokens, the last is cut off by the sequence's end; the most is reached in some sequence. `positions`: A token's index within its document: 0 at each document start, rising by one along the sequence; the most is reached in some sequence.
All inputs are finite; a program needn't handle non-finite values.
Results may differ from a plain program's by a relative error of at most 0.014.
Values may be sent and summed in bfloat16 or wider, within the bound.
No kernel may reach another device: no remote copies, remote signals or barrier semaphores. Data moves between devices by JAX's collectives and lax.ppermute only.
A program may use at most 256 MiB of HBM per device.

v0:
```python
import jax
import jax.numpy as jnp
from jax import lax
from jax.sharding import PartitionSpec as P

HD = 128


EPS = 1e-06
THETA = 1000000.0


def angle_tables(positions):
    exponent = jnp.arange(HD // 2, dtype=jnp.float32) * (2.0 / HD)
    inverse = THETA ** (-exponent)
    phase_angle = positions.astype(jnp.float32)[:, None] * inverse[None, :]
    phase_angle = jnp.concatenate([phase_angle, phase_angle], axis=-1)
    return (jnp.cos(phase_angle), jnp.sin(phase_angle))


def rotary(vectors, cos_table, sin_table):
    half_width = vectors.shape[-1] // 2
    turned = jnp.concatenate([-vectors[..., half_width:], vectors[..., :half_width]], axis=-1)
    return vectors * cos_table + turned * sin_table


def rotary_back(gradient, cos_table, sin_table):
    scaled = gradient * sin_table
    half_width = gradient.shape[-1] // 2
    turned = jnp.concatenate([scaled[..., half_width:], -scaled[..., :half_width]], axis=-1)
    return gradient * cos_table + turned


def norm_forward(residual, gain):
    inverse = lax.rsqrt(jnp.mean(residual * residual, axis=-1, keepdims=True) + EPS)
    return ((residual * inverse * gain).astype(jnp.bfloat16), inverse)


def norm_backward(grad_normed, residual, inverse, gain):
    scaled = grad_normed * gain
    gain_grad = jnp.sum(grad_normed * residual * inverse, axis=0)
    grad_input = inverse * scaled - residual * inverse**3 * jnp.mean(
        scaled * residual, axis=-1, keepdims=True
    )
    return (grad_input, gain_grad)


def rows_fold(weight, left):
    return jnp.dot(
        left,
        lax.all_gather(weight, ("fsdp", "ctx"), axis=0, tiled=True),
        preferred_element_type=jnp.float32,
    )


def columns_map(weight, right):

    def project(piece, start):
        return lax.dot_general(
            right, piece, (((1,), (1,)), ((), ())), preferred_element_type=jnp.float32
        )

    return project(lax.all_gather(weight, ("fsdp", "ctx"), axis=0, tiled=True), jnp.int32(0))


def outer_term(left, right):
    return lax.dot_general(
        left, right, (((0,), (0,)), ((), ())), preferred_element_type=jnp.float32
    )


def weight_grads(left, right):
    return lax.psum_scatter(
        outer_term(left, right), ("fsdp", "ctx"), scatter_dimension=0, tiled=True
    )


def tensor_sum(partial_sum):
    return lax.psum(partial_sum, "tp")


def body(
    tokens,
    cotangent,
    norm_in,
    w_qkv,
    b_qkv,
    w_out,
    norm_mid,
    w_gate_up,
    w_down,
    segments,
    positions,
):
    tok_rows = tokens.shape[0]
    layer_count = norm_in.shape[0]
    local_rows = w_qkv.shape[1]
    group_heads = w_qkv.shape[3] // HD - 2
    seq_len = tok_rows * lax.axis_size("ctx")
    scale = HD ** (-0.5)
    cos_table, sin_table = angle_tables(positions)
    key_segments = lax.all_gather(segments, "ctx", axis=0, tiled=True)
    query_index = lax.axis_index("ctx") * tok_rows + jnp.arange(tok_rows, dtype=jnp.int32)
    key_index = jnp.arange(seq_len, dtype=jnp.int32)
    allowed = (segments[:, None] == key_segments[None, :]) & (
        key_index[None, :] <= query_index[:, None]
    )

    def attention_scores(queries, key_rows):
        scores = (
            jnp.einsum("tgd,kd->gtk", queries, key_rows, preferred_element_type=jnp.float32) * scale
        )
        return jnp.where(allowed[None], scores, -1e30)

    residual = tokens.astype(jnp.float32)
    layer_idx = 0
    qkv_rows = w_qkv[layer_idx].reshape(local_rows, -1)
    out_rows = w_out[layer_idx]
    pair_rows = w_gate_up[layer_idx].reshape(local_rows, -1)
    down_rows = w_down[layer_idx]
    normed_one, inverse_one = norm_forward(residual, norm_in[layer_idx])
    qkv_whole = qkv_rows
    out_whole = out_rows
    project = rows_fold(qkv_rows, normed_one)
    project = project + b_qkv[layer_idx].reshape(-1)
    project = project.reshape(tok_rows, group_heads + 2, HD)
    queries = rotary(project[:, :group_heads], cos_table[:, None], sin_table[:, None]).astype(
        jnp.bfloat16
    )
    key_local = rotary(project[:, group_heads], cos_table, sin_table).astype(jnp.bfloat16)
    value_local = project[:, group_heads + 1].astype(jnp.bfloat16)
    key_rows = lax.all_gather(key_local, "ctx", axis=0, tiled=True)
    value_rows = lax.all_gather(value_local, "ctx", axis=0, tiled=True)
    scores = attention_scores(queries, key_rows)
    peak = jnp.max(scores, axis=-1, keepdims=True)
    shifted = jnp.exp(scores - peak)
    total = jnp.sum(shifted, axis=-1, keepdims=True)
    probabilities = (shifted / total).astype(jnp.bfloat16)
    log_total = peak + jnp.log(total)
    attended = jnp.einsum(
        "gtk,kd->tgd", probabilities, value_rows, preferred_element_type=jnp.float32
    )
    attended = attended.astype(jnp.bfloat16).reshape(tok_rows, -1)
    branch = columns_map(out_rows, attended)
    middle = residual + tensor_sum(branch)
    normed_two, inverse_two = norm_forward(middle, norm_mid[layer_idx])
    gate_up = rows_fold(pair_rows, normed_two).reshape(tok_rows, 2, -1)
    activated = (jax.nn.silu(gate_up[:, 0]) * gate_up[:, 1]).astype(jnp.bfloat16)
    saved = [
        (
            residual,
            normed_one,
            inverse_one,
            qkv_whole,
            out_whole,
            queries,
            key_rows,
            value_rows,
            log_total,
            attended,
            middle,
            normed_two,
            inverse_two,
            gate_up,
            activated,
        )
    ]
    residual = middle + tensor_sum(columns_map(down_rows, activated))
    output = residual.astype(jnp.bfloat16)
    grad_residual = cotangent.astype(jnp.float32)
    layer_grads = [None] * layer_count
    for layer_idx in reversed(range(layer_count)):
        (
            residual_in,
            normed_one,
            inverse_one,
            qkv_whole,
            out_whole,
            queries,
            key_rows,
            value_rows,
            log_total,
            attended,
            middle,
            normed_two,
            inverse_two,
            gate_up,
            activated,
        ) = saved[layer_idx]
        qkv_rows = w_qkv[layer_idx].reshape(local_rows, -1)
        out_rows = w_out[layer_idx]
        pair_rows = w_gate_up[layer_idx].reshape(local_rows, -1)
        down_rows = w_down[layer_idx]
        down_in = grad_residual.astype(jnp.bfloat16)
        grad_activated = rows_fold(down_rows, down_in)
        gate = gate_up[:, 0]
        upward = gate_up[:, 1]
        sigma = jax.nn.sigmoid(gate)
        grad_gate = grad_activated * upward * sigma * (1.0 + gate * (1.0 - sigma))
        grad_upward = grad_activated * (gate * sigma)
        grad_pair = (
            jnp.stack([grad_gate, grad_upward], axis=1).astype(jnp.bfloat16).reshape(tok_rows, -1)
        )
        grad_normed_two = tensor_sum(columns_map(pair_rows, grad_pair))
        grad_middle, gain_two_grad = norm_backward(
            grad_normed_two, middle, inverse_two, norm_mid[layer_idx]
        )
        grad_middle = grad_middle + grad_residual
        out_in = grad_middle.astype(jnp.bfloat16)
        grad_attended = rows_fold(out_rows, out_in)
        grad_heads = grad_attended.astype(jnp.bfloat16).reshape(tok_rows, group_heads, HD)
        exact = jnp.exp(attention_scores(queries, key_rows) - log_total)
        grad_probs = jnp.einsum(
            "tgd,kd->gtk", grad_heads, value_rows, preferred_element_type=jnp.float32
        )
        grad_scores = exact * (grad_probs - jnp.sum(exact * grad_probs, axis=-1, keepdims=True))
        grad_scores = grad_scores.astype(jnp.bfloat16)
        grad_queries = (
            jnp.einsum("gtk,kd->tgd", grad_scores, key_rows, preferred_element_type=jnp.float32)
            * scale
        )
        grad_key_rows = (
            jnp.einsum("gtk,tgd->kd", grad_scores, queries, preferred_element_type=jnp.float32)
            * scale
        )
        grad_value_rows = jnp.einsum(
            "gtk,tgd->kd",
            exact.astype(jnp.bfloat16),
            grad_heads,
            preferred_element_type=jnp.float32,
        )
        grad_keys, grad_values = (
            lax.psum_scatter(grad_key_rows, "ctx", scatter_dimension=0, tiled=True),
            lax.psum_scatter(grad_value_rows, "ctx", scatter_dimension=0, tiled=True),
        )
        grad_project = (
            jnp.concatenate(
                [
                    rotary_back(grad_queries, cos_table[:, None], sin_table[:, None]),
                    rotary_back(grad_keys, cos_table, sin_table)[:, None],
                    grad_values[:, None],
                ],
                axis=1,
            )
            .astype(jnp.bfloat16)
            .reshape(tok_rows, -1)
        )
        bias_grad = jnp.sum(grad_project, axis=0, dtype=jnp.float32)
        grad_normed_one = columns_map(qkv_rows, grad_project)
        grad_normed_one = tensor_sum(grad_normed_one)
        grad_input, gain_one_grad = norm_backward(
            grad_normed_one, residual_in, inverse_one, norm_in[layer_idx]
        )
        grad_residual = grad_input + grad_middle
        pairs = [
            (down_in, activated),
            (normed_two, grad_pair),
            (out_in, attended),
            (normed_one, grad_project),
        ]
        grad_down, grad_gate_up, grad_out, grad_qkv = [
            weight_grads(left, right) for left, right in pairs
        ]
        layer_grads[layer_idx] = (
            gain_one_grad,
            gain_two_grad,
            bias_grad,
            grad_qkv,
            grad_out,
            grad_gate_up,
            grad_down,
        )
    gains_one = jnp.stack([entry[0] for entry in layer_grads])
    gains_two = jnp.stack([entry[1] for entry in layer_grads])
    biases_all = jnp.stack([entry[2] for entry in layer_grads])
    gains_one, gains_two, biases_all = lax.psum((gains_one, gains_two, biases_all), ("fsdp", "ctx"))
    qkv_all = jnp.stack([entry[3] for entry in layer_grads]).reshape(layer_count, local_rows, 1, -1)
    out_all = jnp.stack([entry[4] for entry in layer_grads])
    pair_all = jnp.stack([entry[5] for entry in layer_grads]).reshape(
        layer_count, local_rows, 2, -1
    )
    down_all = jnp.stack([entry[6] for entry in layer_grads])
    return (
        output,
        grad_residual,
        gains_one,
        qkv_all,
        biases_all.reshape(layer_count, 1, -1),
        out_all,
        gains_two,
        pair_all,
        down_all,
    )


def solution(mesh):
    in_specs = (
        P(("fsdp", "ctx"), None),
        P(("fsdp", "ctx"), None),
        P(),
        P(None, ("fsdp", "ctx"), "tp", None),
        P(None, "tp", None),
        P(None, ("fsdp", "ctx"), "tp"),
        P(),
        P(None, ("fsdp", "ctx"), None, "tp"),
        P(None, ("fsdp", "ctx"), "tp"),
        P(("fsdp", "ctx")),
        P(("fsdp", "ctx")),
    )
    out_specs = (
        P(("fsdp", "ctx"), None),
        P(("fsdp", "ctx"), None),
        P(),
        P(None, ("fsdp", "ctx"), "tp", None),
        P(None, "tp", None),
        P(None, ("fsdp", "ctx"), "tp"),
        P(),
        P(None, ("fsdp", "ctx"), None, "tp"),
        P(None, ("fsdp", "ctx"), "tp"),
    )
    return jax.shard_map(body, mesh=mesh, in_specs=in_specs, out_specs=out_specs, check_vma=False)
```

profile of v0, /device:TPU:0, one launch (start us, length us, event | category | flops | bytes accessed | tf_op | source)
XLA Modules:
  0.0 1601.1 jit_solution(874932013832554639)
XLA Ops:
  10.1 6.3 all-gather.4
  16.4 1.4 fusion.24
  18.3 1.6 fusion.47
  20.0 38.2 %all-gather.12.cloned.1.call-done = bf16[1,1536,1,1024]{3,1,2,0:T(8,128)(2,1)} async-done(((bf16[1,96,1,1024]{3,1,2,0:T(8,128)(2,1)}), bf16[1,1536,1,1024]{3,1,2,0:T(8,128)(2,1)}) %all-gather.12.cloned.1.call-update) | async-done | bytes 3145744 | tf_op jit(solution)/shard_map/all_gather | solution.py:51
  58.2 3.1 fusion.36
  63.8 5.8 all_gather.28
  69.6 6.1 all-gather.1
  76.2 1.1 fusion.73
  77.4 0.8 fusion.7
  78.2 1.8 copy-done
  80.0 1.3 fusion.39
  81.3 20.4 %all-gather.14.cloned.1.call-done = bf16[1,1536,768]{2,1,0:T(8,128)(2,1)} async-done(((bf16[1,96,768]{2,1,0:T(8,128)(2,1)}), bf16[1,1536,768]{2,1,0:T(8,128)(2,1)}) %all-gather.14.cloned.1.call-update) | async-done | bytes 2359312 | tf_op jit(solution)/shard_map/all_gather | solution.py:63
  101.7 3.6 fusion.20
  105.4 1.4 copy.101
  107.5 48.3 %all-reduce.6.cloned.1.call-done = f32[256,1536]{1,0:T(8,128)} async-done(((f32[256,1536]{1,0:T(8,128)}), f32[256,1536]{1,0:T(8,128)}) %all-reduce.6.cloned.1.call-update) | async-done | bytes 1572880 | tf_op jit(solution)/shard_map/psum | solution.py:79
  155.8 1.7 multiply_reduce_fusion.2
  157.5 140.1 %all-gather.10.cloned.1.call-done = bf16[1536,8960]{1,0:T(8,128)(2,1)} async-done(((bf16[96,8960]{1,0:T(8,128)(2,1)}), bf16[1536,8960]{1,0:T(8,128)(2,1)}) %all-gather.10.cloned.1.call-update) | async-done | bytes 27525136 | tf_op jit(solution)/shard_map/all_gather | solution.py:51
  297.6 15.3 fusion.68
  312.9 11.3 reshape.200
  324.1 12.6 fusion.69
  336.7 71.5 %all-gather.16.cloned.1.call-done = bf16[1,1536,4480]{2,1,0:T(8,128)(2,1)} async-done(((bf16[1,96,4480]{2,1,0:T(8,128)(2,1)}), bf16[1,1536,4480]{2,1,0:T(8,128)(2,1)}) %all-gather.16.cloned.1.call-update) | async-done | bytes 13762576 | tf_op jit(solution)/shard_map/all_gather | solution.py:63
  408.2 11.6 fusion.23
  419.8 2.5 pad_maximum_fusion
  422.3 6.5 copy.68
  428.8 14.8 fusion.76
  443.9 49.5 %all-reduce.8.cloned.1.call-done = f32[256,1536]{1,0:T(8,128)} async-done(((f32[256,1536]{1,0:T(8,128)}), f32[256,1536]{1,0:T(8,128)}) %all-reduce.8.cloned.1.call-update) | async-done | bytes 1572880 | tf_op jit(solution)/shard_map/psum | solution.py:79
  493.4 2.5 multiply_reduce_fusion
  495.9 1.8 convert_add_fusion.1
  497.7 1.1 copy-done.5
  498.9 0.8 fusion.40
  499.9 4.2 fusion.4
  504.5 1.3 fusion.6
  505.9 1.7 copy-done.3
  507.5 3.0 fusion.46
  510.6 10.8 fusion.2
  521.4 2.0 fusion.43
  523.5 8.8 reduce-scatter.9.cloned.1.call-done
  532.3 1.6 broadcast_multiply_fusion.2
  534.0 1.6 fusion.63
  535.9 2.5 broadcast_multiply_fusion
  538.6 18.6 %reduce-scatter.11.cloned.1.call-done = f32[256,128]{0,1:T(8,128)} async-done(((f32[1024,128]{0,1:T(8,128)}), f32[256,128]{0,1:T(8,128)}) %reduce-scatter.11.cloned.1.call-update) | async-done | bytes 131088 | tf_op jit(solution)/shard_map/reduce_scatter | solution.py:234
  557.2 1.1 convert_reduce_fusion
  558.3 4.1 fusion.12
  562.7 3.8 fusion.58
  566.6 1.1 copy-done.11
  567.6 13.7 convolution_bitcast_fusion
  581.3 27.4 %copy.91 = f32[1536,4480]{1,0:T(8,128)} copy(f32[1536,4480]{0,1:T(8,128)} %convolution_bitcast_fusion) | data formatting | bytes 55050240
  608.8 1.3 copy-done.2
  610.1 22.7 %fusion.67 = f32[1536,8960]{1,0:T(8,128)} fusion(bf16[256,8960]{0,1:T(8,128)(2,1)} %bitcast.142, f32[256,1536]{1,0:T(8,128)S(1)} %copy-done.2, f32[1536]{0:T(1024)S(1)} %reduce.2, f32[256]{0:T(256)S(1)} %copy-done.22), kind=kOutput, calls=%fused_computation.110 | convolution fusion | flops 7047610368 | bytes 61217792 | tf_op jit(solution)/shard_map/dot_general | solution.py:67
  632.9 0.9 copy-done.15
  633.8 4.4 fusion.50
  638.9 9.7 all-reduce.10.cloned.1.call-done
  648.5 1.8 fusion.32
  650.4 63.2 %all-reduce = (f32[1,1536]{1,0:T(1,128)}, f32[1,1,1024]{2,1,0:T(1,128)}, f32[1,1536]{1,0:T(1,128)}) all-reduce(f32[1,1536]{1,0:T(1,128)S(1)} %stack.30, f32[1,1,1024]{2,1,0:T(1,128)S(1)} %bitcast.157, f32[1,1536]{1,0:T(1,128)S(1)} %stack.33), channel_id=1, replica_groups=mesh['fsdp'=4,'ctx'=4,'tp'=2] {'fsdp','ctx'}, use_global_device_ids=true, to_apply=%region_14.15 | all-reduce | flops 4096 | bytes 32768 | tf_op jit(solution)/shard_map/psum | solution.py:276
  713.6 2.6 add_convert_fusion
  716.2 1.6 fusion.29
  717.8 20.7 %reduce-scatter.13.cloned.1.call-done = f32[96,1024]{1,0:T(8,128)} async-done(((f32[1536,1024]{1,0:T(8,128)}), f32[96,1024]{1,0:T(8,128)}) %reduce-scatter.13.cloned.1.call-update) | async-done | bytes 393232 | tf_op jit(solution)/shard_map/reduce_scatter | solution.py:73
  738.5 2.1 copy.79
  740.7 264.0 %reduce-scatter.19.cloned.1.call-done = f32[96,4480]{1,0:T(8,128)} async-done(((f32[1536,4480]{1,0:T(8,128)}), f32[96,4480]{1,0:T(8,128)}) %reduce-scatter.19.cloned.1.call-update) | async-done | bytes 1720336
  1004.7 2.3 copy.92
  1007.0 2.1 copy.80
  1009.1 505.9 %reduce-scatter.17.cloned.1.call-done = f32[96,8960]{1,0:T(8,128)} async-done(((f32[1536,8960]{1,0:T(8,128)}), f32[96,8960]{1,0:T(8,128)}) %reduce-scatter.17.cloned.1.call-update) | async-done | bytes 3440656 | tf_op jit(solution)/shard_map/reduce_scatter | solution.py:73
  1515.0 5.4 reshape_stack.7
  1520.5 73.7 %reduce-scatter.15.cloned.1.call-done = f32[96,768]{1,0:T(8,128)} async-done(((f32[1536,768]{1,0:T(8,128)}), f32[96,768]{1,0:T(8,128)}) %reduce-scatter.15.cloned.1.call-update) | async-done | bytes 294928 | tf_op jit(solution)/shard_map/reduce_scatter | solution.py:73
  (115 shorter events, 10.0 us)
Async XLA Ops:
  7.2 51.0 %all-gather.12.cloned.1.call-start = ((), (), s32[]{:S(2)}) async-start(), calls=%async_computation.14 | async-start | bytes 3342336 | tf_op jit(solution)/shard_map/all_gather | solution.py:51
  7.9 93.8 %all-gather.14.cloned.1.call-start = ((), (), s32[]{:S(2)}) async-start(), calls=%async_computation.15 | async-start | bytes 2506752 | tf_op jit(solution)/shard_map/all_gather | solution.py:63
  8.7 147.1 %all-reduce.6.cloned.1.call-start = ((), (), s32[]{:S(2)}) async-start(), calls=%async_computation.6 | async-start | bytes 3145728 | tf_op jit(solution)/shard_map/psum | solution.py:79
  18.3 39.9 %copy-start.24 = (f32[256]{0:T(256)}, f32[256]{0:T(256)S(1)}, u32[]{:S(2)}) copy-start(f32[256]{0:T(256)S(1)} %get-tuple-element.69) | copy-start | bytes 3076
  63.2 12.5 copy-start.12
  63.2 13.0 copy-start.18
  75.6 2.6 copy-start.16
  76.2 1.1 copy-start.10
  77.4 2.6 copy-start
  81.3 24.0 %copy-start.14 = (bf16[128,6,256]{2,0,1:T(8,128)(2,1)}, bf16[128,6,256]{2,0,1:T(8,128)(2,1)S(1)}, u32[]{:S(2)}) copy-start(bf16[128,6,256]{2,0,1:T(8,128)(2,1)S(1)} %fusion.39) | copy-start | bytes 1179652
  81.3 24.1 %copy-start.13 = (bf16[1,96,2,4480]{3,2,1,0:T(2,128)(2,1)S(1)}, bf16[1,96,2,4480]{3,2,1,0:T(2,128)(2,1)}, u32[]{:S(2)}) copy-start(bf16[1,96,2,4480]{3,2,1,0:T(2,128)(2,1)} %param.18) | copy-start | bytes 5160964
  105.3 2.1 copy-start.26
  105.3 50.4 %copy-start.4 = (bf16[256,1536]{1,0:T(8,128)(2,1)S(1)}, bf16[256,1536]{1,0:T(8,128)(2,1)}, u32[]{:S(2)}) copy-start(bf16[256,1536]{1,0:T(8,128)(2,1)} %param.11) | copy-start | bytes 2359300
  105.4 192.2 %all-gather.10.cloned.1.call-start = ((), (), s32[]{:S(2)}) async-start(), calls=%async_computation.7 | async-start | bytes 29245440 | tf_op jit(solution)/shard_map/all_gather | solution.py:51
  106.8 301.4 %all-gather.16.cloned.1.call-start = ((), (), s32[]{:S(2)}) async-start(), calls=%async_computation.16 | async-start | bytes 14622720 | tf_op jit(solution)/shard_map/all_gather | solution.py:63
  107.4 386.0 %all-reduce.8.cloned.1.call-start = ((), (), s32[]{:S(2)}) async-start(), calls=%async_computation.8 | async-start | bytes 3145728 | tf_op jit(solution)/shard_map/psum | solution.py:79
  157.4 338.5 %copy-start.1 = (f32[256,1536]{1,0:T(8,128)}, f32[256,1536]{1,0:T(8,128)S(1)}, u32[]{:S(2)}) copy-start(f32[256,1536]{1,0:T(8,128)S(1)} %get-tuple-element.48) | copy-start | bytes 4718596
  157.5 338.5 %copy-start.21 = (f32[256]{0:T(256)}, f32[256]{0:T(256)S(1)}, u32[]{:S(2)}) copy-start(f32[256]{0:T(256)S(1)} %get-tuple-element.71) | copy-start | bytes 3076
  443.6 88.7 %reduce-scatter.9.cloned.1.call-start = ((), (), s32[]{:S(2)}) async-start(), calls=%async_computation.9 | async-start | bytes 655360 | tf_op jit(solution)/shard_map/reduce_scatter | solution.py:233
  443.9 60.2 %copy-start.19 = (f32[6,256]{1,0:T(8,128)}, f32[6,256]{1,0:T(8,128)S(1)}, u32[]{:S(2)}) copy-start(f32[6,256]{1,0:T(8,128)S(1)} %log_add_fusion) | copy-start | bytes 18436
  493.4 2.5 copy-start.9
  495.9 3.0 copy-start.7
  497.7 1.1 copy-start.5
  498.9 1.0 copy-start.17
  499.8 4.3 slice-start
  499.9 4.7 slice-start.1
  505.9 1.7 copy-start.3
  507.5 13.9 slice-start.2
  510.5 46.7 %reduce-scatter.11.cloned.1.call-start = ((), (), s32[]{:S(2)}) async-start(), calls=%async_computation.10 | async-start | bytes 655360 | tf_op jit(solution)/shard_map/reduce_scatter | solution.py:234
  510.6 10.8 slice-start.3
  510.6 10.8 copy-start.20
  523.4 125.1 %all-reduce.10.cloned.1.call-start = ((), (), s32[]{:S(2)}) async-start(), calls=%async_computation.18 | async-start | bytes 6291456 | tf_op jit(solution)/shard_map/psum | solution.py:79
  558.3 4.4 copy-start.25
  562.4 176.1 %reduce-scatter.13.cloned.1.call-start = ((), (), s32[]{:S(2)}) async-start(), calls=%async_computation.11 | async-start | bytes 6684672 | tf_op jit(solution)/shard_map/reduce_scatter | solution.py:73
  566.5 1.1 copy-start.11
  566.5 438.1 %reduce-scatter.19.cloned.1.call-start = ((), (), s32[]{:S(2)}) async-start(), calls=%async_computation.17 | async-start | bytes 29245440
  608.7 1.4 copy-start.2
  608.7 1.4 copy-start.22
  608.7 906.3 %reduce-scatter.17.cloned.1.call-start = ((), (), s32[]{:S(2)}) async-start(), calls=%async_computation.13 | async-start | bytes 58490880 | tf_op jit(solution)/shard_map/reduce_scatter | solution.py:73
  632.8 1.0 copy-start.15
  632.8 961.3 %reduce-scatter.15.cloned.1.call-start = ((), (), s32[]{:S(2)}) async-start(), calls=%async_computation.12 | async-start | bytes 5013504 | tf_op jit(solution)/shard_map/reduce_scatter | solution.py:73
  638.2 0.7 copy-start.23
  648.5 67.7 %copy-start.27 = (f32[256]{0:T(256)S(1)}, f32[256]{0:T(256)}, u32[]{:S(2)}) copy-start(f32[256]{0:T(256)} %get-tuple-element.68) | copy-start | bytes 3076
  713.6 2.6 copy-start.6
  713.6 2.6 copy-start.8
Sparse Core Ops, SparseCore 0:
  10.3 47.8 all-gather.11
  60.5 41.1 all-gather.13
  105.5 50.2 all-reduce.5
  157.9 139.6 all-gather.9
  300.0 108.1 all-gather.15
  443.7 49.6 all-reduce.7
  510.6 21.6 reduce-scatter.8
  535.5 21.6 reduce-scatter.10
  562.5 85.9 all-reduce.9
  652.8 85.6 reduce-scatter.12
  742.7 261.9 reduce-scatter.18
  1009.3 505.6 reduce-scatter.16
  1519.5 74.6 reduce-scatter.14
where the time goes:
time: 1610 us; the launch traced here: 1600 us
  waiting for transfers between devices  1270 us (79%)
  matrix products  123 us (8%)
  local copies, waits for them, and re-layouts  82.4 us (5%)
  blocking collectives  81.3 us (5%)
  other arithmetic  27.6 us (2%)
    reduce_scatter x3, waiting for transfers between devices, weight_grads(): lax.psum_scatter(outer_term(left, right), ('fsdp', 'ctx'), scatter_dimens...  600 us
    unnamed x14, waiting for transfers between devices  266 us
    all_gather x2, waiting for transfers between devices, rows_fold(): lax.all_gather(weight, ('fsdp', 'ctx'), axis=0, tiled=True)  178 us
    psum x3, waiting for transfers between devices, tensor_sum(): return lax.psum(partial_sum, 'tp')  107 us
    all_gather x2, waiting for transfers between devices, columns_map(): lax.all_gather(weight, ('fsdp', 'ctx'), axis=0, tiled=True)  91.8 us
    psum x1, blocking collectives, body(): lax.psum((gains_one, gains_two, biases_all), ('fsdp', 'ctx'))  63.2 us
    unnamed x72, local copies, waits for them, and re-layouts  45.5 us
    dot_general x4, matrix products, outer_term(): lax.dot_general(left, right, (((0,), (0,)), ((), ())), preferred_element_...  44.5 us
  transfers between devices with their start and end apart: 13, of which 13 were waited for; matrix products, arithmetic and copies ran while one was open for 10% of the time, Pallas kernels for 0%

commit v1 on v0

v1 whole, which is shorter than its diff:
```python
import jax
import jax.numpy as jnp
from jax import lax
from jax.sharding import PartitionSpec as P

HD = 128
EPS = 1e-06
THETA = 1000000.0
BF = jnp.bfloat16
F32 = jnp.float32


def angle_tables(positions):
    exponent = jnp.arange(HD // 2, dtype=F32) * (2.0 / HD)
    inverse = THETA ** (-exponent)
    phase_angle = positions.astype(F32)[:, None] * inverse[None, :]
    phase_angle = jnp.concatenate([phase_angle, phase_angle], axis=-1)
    return (jnp.cos(phase_angle), jnp.sin(phase_angle))


def rotary(vectors, cos_table, sin_table):
    half_width = vectors.shape[-1] // 2
    turned = jnp.concatenate([-vectors[..., half_width:], vectors[..., :half_width]], axis=-1)
    return vectors * cos_table + turned * sin_table


def rotary_back(gradient, cos_table, sin_table):
    scaled = gradient * sin_table
    half_width = gradient.shape[-1] // 2
    turned = jnp.concatenate([scaled[..., half_width:], -scaled[..., :half_width]], axis=-1)
    return gradient * cos_table + turned


def dot(left, right):
    return jnp.dot(left, right, preferred_element_type=F32)


def dot_nt(left, right):
    return lax.dot_general(left, right, (((1,), (1,)), ((), ())), preferred_element_type=F32)


def dot_tn(left, right):
    return lax.dot_general(left, right, (((0,), (0,)), ((), ())), preferred_element_type=F32)


def rotate(block, axis, distance):
    n = lax.axis_size(axis)
    return lax.ppermute(block, axis, [(i, (i + distance) % n) for i in range(n)])


def flip(block, axis, bit):
    n = lax.axis_size(axis)
    return lax.ppermute(block, axis, [(i, i ^ bit) for i in range(n)])


def pick(pieces, index):
    return lax.dynamic_index_in_dim(pieces, index, axis=0, keepdims=False)


def in_order(slots):
    n = len(slots)
    z = lax.axis_index("fsdp")
    whole = jnp.zeros((n,) + slots[0].shape, slots[0].dtype)
    for k, slot in enumerate(slots):
        whole = lax.dynamic_update_index_in_dim(whole, slot, (z - k) % n, axis=0)
    return whole


def over_ctx(block):
    n = lax.axis_size("ctx")
    bit = n // 2
    while bit:
        block = jnp.concatenate([block, flip(block, "ctx", bit)], axis=0)
        bit //= 2
    return block


def whole_weight(rows):
    n = lax.axis_size("fsdp")
    slots = [rows] + [rotate(rows, "fsdp", k) for k in range(1, n)]
    stacked = in_order(slots)
    return over_ctx(stacked.reshape(-1, rows.shape[1]))


def gather_tokens(block):
    n = lax.axis_size("fsdp")
    z = lax.axis_index("fsdp")
    up = down = block
    ups, downs = {}, {}
    other_up, other_down = {}, {}
    other_own = flip(block, "tp", 1)

    def cross(piece, first, last):
        pairs = []
        for i in range(first, last + 1):
            pairs += [(2 * i, 2 * i + 1), (2 * i + 1, 2 * i)]
        return lax.ppermute(piece, ("fsdp", "tp"), pairs)

    for s in range(1, n):
        up = lax.ppermute(up, "fsdp", [(i, i + 1) for i in range(s - 1, n - 1)])
        down = lax.ppermute(down, "fsdp", [(i, i - 1) for i in range(1, n - s + 1)])
        ups[s], downs[s] = up, down
        other_up[s] = cross(up, s, n - 1)
        other_down[s] = cross(down, 0, n - 1 - s)
    own = [block] + [jnp.where(z >= k, ups[k], downs[n - k]) for k in range(1, n)]
    other = [other_own] + [jnp.where(z >= k, other_up[k], other_down[n - k]) for k in range(1, n)]
    return jnp.concatenate(own + other, axis=0)


def scatter_tokens(partial):
    n = lax.axis_size("fsdp")
    rows = partial.shape[0] // (2 * n)
    parts = partial.reshape(2, n, rows, partial.shape[1])
    sums = [parts[0, k] + flip(parts[1, k].astype(BF), "tp", 1).astype(F32) for k in range(n)]
    up = down = None
    for s in range(1, n):
        up_acc = sums[s] if up is None else sums[s] + up.astype(F32)
        down_acc = sums[n - s] if down is None else sums[n - s] + down.astype(F32)
        up = lax.ppermute(up_acc.astype(BF), "fsdp", [(i, i + 1) for i in range(s)])
        down = lax.ppermute(down_acc.astype(BF), "fsdp", [(i, i - 1) for i in range(n - s, n)])
    return sums[0] + up.astype(F32) + down.astype(F32)


def reduce_ctx(left, right):
    n = lax.axis_size("ctx")
    half = left.shape[1] // 2
    total = dot_tn(left[:, :half], right)
    arrived = flip(dot_tn(left[:, half:], right).astype(BF), "ctx", 1)
    total = total + arrived.astype(F32)
    bit = 2
    while bit < n:
        half //= 2
        total = total[:half] + flip(total[half:].astype(BF), "ctx", bit).astype(F32)
        bit *= 2
    return total


def reduce_weight(left, right):
    n = lax.axis_size("fsdp")
    z = lax.axis_index("fsdp")
    total = reduce_ctx(left, right)
    parts = total.reshape(n, total.shape[0] // n, total.shape[1])
    out = pick(parts, z)
    for k in range(1, n):
        out = out + rotate(pick(parts, (z + k) % n).astype(BF), "fsdp", k).astype(F32)
    return out


def deal_weight(left, right):
    n = lax.axis_size("fsdp")
    z = lax.axis_index("fsdp")
    total = reduce_ctx(left, right).astype(BF)
    parts = total.reshape(n, total.shape[0] // n, total.shape[1])
    return [pick(parts, z)] + [rotate(pick(parts, (z + k) % n), "fsdp", k) for k in range(1, n)]


def sum_everywhere(vector, axes):
    for axis in axes:
        bit = 1
        while bit < lax.axis_size(axis):
            vector = vector + flip(vector, axis, bit)
            bit *= 2
    return vector


def body(
    tokens,
    cotangent,
    norm_in,
    w_qkv,
    b_qkv,
    w_out,
    norm_mid,
    w_gate_up,
    w_down,
    segments,
    positions,
):
    n, ctx_size = lax.axis_size("fsdp"), lax.axis_size("ctx")
    z, ctx, y = lax.axis_index("fsdp"), lax.axis_index("ctx"), lax.axis_index("tp")
    count, width = tokens.shape
    h = count // 2
    rows = w_qkv.shape[1]
    heads = w_qkv.shape[3] // HD - 2
    hidden = w_down.shape[2]
    piece = -(-hidden // (n * HD)) * HD
    scale = HD ** (-0.5)

    order = [0]
    bit = ctx_size // 2
    while bit:
        order = order + [j ^ bit for j in order]
        bit //= 2
    places = [ctx ^ j for j in order]

    def to_relative(values):
        parts = values.reshape(values.shape[0], n, ctx_size, rows)
        picked = [lax.dynamic_index_in_dim(parts, place, axis=2, keepdims=False) for place in places]
        return jnp.stack(picked, axis=1).reshape(values.shape)

    def to_natural(values):
        parts = values.reshape(values.shape[0], ctx_size, n, rows)
        where = [order.index(j) for j in range(ctx_size)]
        relative = [parts[:, place] for place in where]
        stacked = jnp.stack(relative, axis=1)
        natural = [lax.dynamic_index_in_dim(stacked, ctx ^ j, axis=1, keepdims=False) for j in range(ctx_size)]
        return jnp.stack(natural, axis=2).reshape(values.shape)

    def own_half(values):
        return lax.dynamic_slice_in_dim(values, y * h, h, axis=0)

    def other_half(values):
        return lax.dynamic_slice_in_dim(values, (1 - y) * h, h, axis=0)

    def both_halves(own):
        other = flip(own, "tp", 1)
        return jnp.where(
            y == 0, jnp.concatenate([own, other], axis=0), jnp.concatenate([other, own], axis=0)
        )

    qkv_whole = whole_weight(w_qkv[0].reshape(rows, -1))
    out_whole = whole_weight(w_out[0])

    pad = n * piece - hidden
    gate_rows = jnp.pad(w_gate_up[0, :, 0], ((0, 0), (0, pad)))
    up_rows = jnp.pad(w_gate_up[0, :, 1], ((0, 0), (0, pad)))
    down_rows = jnp.pad(w_down[0], ((0, 0), (0, pad)))

    def columns(values, index):
        return lax.dynamic_slice_in_dim(values, index * piece, piece, axis=1)

    pair_slots, down_slots = [], []
    for k in range(n):
        index = (z + k) % n
        pair = jnp.concatenate([columns(gate_rows, index), columns(up_rows, index)], axis=1)
        pair_slots.append(rotate(pair, "fsdp", k) if k else pair)
    for k in range(n):
        down = columns(down_rows, (z + k) % n)
        down_slots.append(rotate(down, "fsdp", k) if k else down)
    pair_whole = over_ctx(in_order(pair_slots).reshape(n * rows, -1))
    down_whole = over_ctx(in_order(down_slots).reshape(n * rows, -1))

    x0 = to_relative(tokens).astype(F32)
    grad_in = to_relative(cotangent)
    gain_one = to_relative(norm_in)
    gain_two = to_relative(norm_mid)

    cos_table, sin_table = angle_tables(positions)
    inverse_one = lax.rsqrt(jnp.mean(x0 * x0, axis=-1, keepdims=True) + EPS)
    normed_one = (x0 * inverse_one * gain_one).astype(BF)
    project = dot(normed_one, qkv_whole) + b_qkv[0].reshape(-1)
    project = project.reshape(count, heads + 2, HD)
    queries = rotary(project[:, :heads], cos_table[:, None], sin_table[:, None]).astype(BF)
    key_local = rotary(project[:, heads], cos_table, sin_table).astype(BF)
    value_local = project[:, heads + 1].astype(BF)
    local_pair = jnp.stack([key_local, value_local])
    pairs_all = [local_pair] + [flip(local_pair, "ctx", j) for j in range(1, ctx_size)]
    key_rows = jnp.concatenate([p[0] for p in pairs_all], axis=0)
    value_rows = jnp.concatenate([p[1] for p in pairs_all], axis=0)
    query_index = ctx * count + jnp.arange(count, dtype=jnp.int32)
    key_index = jnp.concatenate(
        [(ctx ^ j) * count + jnp.arange(count, dtype=jnp.int32) for j in range(ctx_size)]
    )
    first_key = query_index - positions
    allowed = (key_index[None, :] <= query_index[:, None]) & (
        key_index[None, :] >= first_key[:, None]
    )

    def attention_scores():
        scores = jnp.einsum("tgd,kd->gtk", queries, key_rows, preferred_element_type=F32) * scale
        return jnp.where(allowed[None], scores, -1e30)

    scores = attention_scores()
    peak = jnp.max(scores, axis=-1, keepdims=True)
    shifted = jnp.exp(scores - peak)
    total = jnp.sum(shifted, axis=-1, keepdims=True)
    probabilities = (shifted / total).astype(BF)
    log_total = peak + jnp.log(total)
    attended = jnp.einsum("gtk,kd->tgd", probabilities, value_rows, preferred_element_type=F32)
    attended = attended.astype(BF).reshape(count, -1)
    branch = dot_nt(attended, out_whole)
    arrived = flip(other_half(branch).astype(BF), "tp", 1)
    middle = own_half(x0) + own_half(branch) + arrived.astype(F32)

    inverse_two = lax.rsqrt(jnp.mean(middle * middle, axis=-1, keepdims=True) + EPS)
    normed_two = (middle * inverse_two * gain_two).astype(BF)
    grad_half = own_half(grad_in)
    grad_all = gather_tokens(grad_half)
    normed_all = gather_tokens(normed_two)
    gate_up = dot(normed_all, pair_whole)
    gate, upward = gate_up[:, :piece], gate_up[:, piece:]
    sigma = jax.nn.sigmoid(gate)
    activated = (gate * sigma * upward).astype(BF)
    grad_activated = dot(grad_all, down_whole)
    grad_gate = grad_activated * upward * sigma * (1.0 + gate * (1.0 - sigma))
    grad_upward = grad_activated * (gate * sigma)
    grad_pair = jnp.concatenate([grad_gate.astype(BF), grad_upward.astype(BF)], axis=1)
    grad_normed_two = scatter_tokens(dot_nt(grad_pair, pair_whole))

    scaled = grad_normed_two * gain_two
    gain_two_grad = jnp.sum(grad_normed_two * middle * inverse_two, axis=0)
    grad_middle = (
        inverse_two * scaled
        - middle * inverse_two**3 * jnp.mean(scaled * middle, axis=-1, keepdims=True)
        + grad_half.astype(F32)
    )
    out_in = both_halves(grad_middle.astype(BF))

    grad_heads = dot(out_in, out_whole).astype(BF).reshape(count, heads, HD)
    exact = jnp.exp(attention_scores() - log_total)
    grad_probs = jnp.einsum("tgd,kd->gtk", grad_heads, value_rows, preferred_element_type=F32)
    grad_scores = exact * (grad_probs - jnp.sum(exact * grad_probs, axis=-1, keepdims=True))
    grad_scores = grad_scores.astype(BF)
    grad_queries = (
        jnp.einsum("gtk,kd->tgd", grad_scores, key_rows, preferred_element_type=F32) * scale
    )
    grad_key_rows = (
        jnp.einsum("gtk,tgd->kd", grad_scores, queries, preferred_element_type=F32) * scale
    )
    grad_value_rows = jnp.einsum(
        "gtk,tgd->kd", exact.astype(BF), grad_heads, preferred_element_type=F32
    )
    grad_pairs = jnp.stack([grad_key_rows, grad_value_rows]).reshape(2, ctx_size, count, HD)
    grad_kv = grad_pairs[:, 0]
    for j in range(1, ctx_size):
        grad_kv = grad_kv + flip(grad_pairs[:, j].astype(BF), "ctx", j).astype(F32)
    grad_project = (
        jnp.concatenate(
            [
                rotary_back(grad_queries, cos_table[:, None], sin_table[:, None]),
                rotary_back(grad_kv[0], cos_table, sin_table)[:, None],
                grad_kv[1][:, None],
            ],
            axis=1,
        )
        .astype(BF)
        .reshape(count, -1)
    )
    bias_grad = jnp.sum(grad_project, axis=0, dtype=F32)
    partial_one = dot_nt(grad_project, qkv_whole).astype(BF)
    grad_normed_one = partial_one.astype(F32) + flip(partial_one, "tp", 1).astype(F32)
    scaled = grad_normed_one * gain_one
    gain_one_grad = jnp.sum(grad_normed_one * x0 * inverse_one, axis=0)
    grad_tokens = (
        inverse_one * scaled
        - x0 * inverse_one**3 * jnp.mean(scaled * x0, axis=-1, keepdims=True)
        + out_in.astype(F32)
    )

    residual = middle + scatter_tokens(dot_nt(activated, down_whole))
    output = to_natural(both_halves(residual.astype(BF)))

    def natural_columns(slots):
        whole = jnp.zeros((rows, n * piece), F32)
        for k, slot in enumerate(slots):
            whole = lax.dynamic_update_slice_in_dim(
                whole, slot.astype(F32), ((z - k) % n) * piece, axis=1
            )
        return whole[:, :hidden]

    down_grad = natural_columns(deal_weight(grad_all, activated))
    pair_grads = deal_weight(normed_all, grad_pair)
    pair_grad = jnp.stack(
        [
            natural_columns([slot[:, :piece] for slot in pair_grads]),
            natural_columns([slot[:, piece:] for slot in pair_grads]),
        ],
        axis=1,
    )
    out_grad = reduce_weight(out_in, attended)
    qkv_grad = reduce_weight(normed_one, grad_project)

    gain_two_all = sum_everywhere(to_natural(gain_two_grad[None]), ("tp", "ctx", "fsdp"))
    small = jnp.concatenate([to_natural(gain_one_grad[None]), bias_grad[None]], axis=1)
    small_all = sum_everywhere(small, ("ctx", "fsdp"))
    return (
        output,
        to_natural(grad_tokens),
        small_all[:, :width],
        qkv_grad.reshape(1, rows, 1, -1),
        small_all[:, width:].reshape(1, 1, -1),
        out_grad[None],
        gain_two_all,
        pair_grad[None],
        down_grad[None],
    )


def solution(mesh):
    rows = ("fsdp", "ctx")
    in_specs = (
        P(rows, None),
        P(rows, None),
        P(),
        P(None, rows, "tp", None),
        P(None, "tp", None),
        P(None, rows, "tp"),
        P(),
        P(None, rows, None, "tp"),
        P(None, rows, "tp"),
        P(rows),
        P(rows),
    )
    out_specs = (
        P(rows, None),
        P(rows, None),
        P(),
        P(None, rows, "tp", None),
        P(None, "tp", None),
        P(None, rows, "tp"),
        P(),
        P(None, rows, None, "tp"),
        P(None, rows, "tp"),
    )
    return jax.shard_map(body, mesh=mesh, in_specs=in_specs, out_specs=out_specs, check_vma=False)
```

time: 1610 us -> 722 us (0.45)
  waiting for transfers between devices: 1270 us -> 299 us
  starting transfers between devices: 0.99 us -> 193 us
  blocking collectives: 81.3 us -> 0 us
  matrix products: 123 us -> 85.4 us
  other arithmetic: 27.6 us -> 55.6 us
    reduce_scatter x5 -> x0, waiting for transfers between devices: 628 us -> none  [the longest x3 600 us: weight_grads(): lax.psum_scatter(outer_term(left, right), ('fsdp', 'ctx'), scatter_dimens...]
    ppermute x0 -> x105, waiting for transfers between devices: none -> 299 us  [the longest x45 155 us: flip(): return lax.ppermute(block, axis, [(i, i ^ bit) for i in range(n)])]
    all_gather x4 -> x0, waiting for transfers between devices: 270 us -> none  [the longest x2 178 us: rows_fold(): lax.all_gather(weight, ('fsdp', 'ctx'), axis=0, tiled=True)]
    unnamed x14 -> x0, waiting for transfers between devices: 266 us -> none
    ppermute x0 -> x105, starting transfers between devices: none -> 193 us  [the longest x24 52.3 us: rotate(): lax.ppermute(block, axis, [(i, (i + distance) % n) for i in range(n)])]
    psum x3 -> x0, waiting for transfers between devices: 107 us -> none  [tensor_sum(): return lax.psum(partial_sum, 'tp')]
    psum x1 -> x0, blocking collectives: 63.2 us -> none  [body(): lax.psum((gains_one, gains_two, biases_all), ('fsdp', 'ctx'))]
    dot_general x16 -> x20, matrix products: 117 us -> 77.8 us  [the longest x8 27.8 us: dot_tn(): lax.dot_general(left, right, (((0,), (0,)), ((), ())), preferred_element_...]
  transfers between devices with their start and end apart: 13 -> 105, of which waited for: 13 -> 38; matrix products, arithmetic and copies ran while one was open for 10% -> 26% of each run, Pallas kernels for 0% -> 0%
where the time goes in v1:
time: 722 us; the launch traced here: 708 us
  waiting for transfers between devices  299 us (41%)
  starting transfers between devices  193 us (27%)
  matrix products  85.4 us (12%)
  local copies, waits for them, and re-layouts  71.6 us (10%)
  other arithmetic  55.6 us (8%)
    ppermute x45, waiting for transfers between devices, flip(): return lax.ppermute(block, axis, [(i, i ^ bit) for i in range(n)])  155 us
    ppermute x24, waiting for transfers between devices, rotate(): lax.ppermute(block, axis, [(i, (i + distance) % n) for i in range(n)])  78 us
    ppermute x24, starting transfers between devices, rotate(): lax.ppermute(block, axis, [(i, (i + distance) % n) for i in range(n)])  52.3 us
    ppermute x45, starting transfers between devices, flip(): return lax.ppermute(block, axis, [(i, i ^ bit) for i in range(n)])  52.2 us
    ppermute x12, waiting for transfers between devices, cross(): return lax.ppermute(piece, ('fsdp', 'tp'), pairs)  28.7 us
    dot_general x8, matrix products, dot_tn(): lax.dot_general(left, right, (((0,), (0,)), ((), ())), preferred_element_...  27.8 us
    ppermute x6, starting transfers between devices, scatter_tokens(): up = lax.ppermute(up_acc.astype(BF), 'fsdp', [(i, i + 1) for i in range(s)])  27.2 us
    ppermute x6, starting transfers between devices, gather_tokens(): up = lax.ppermute(up, 'fsdp', [(i, i + 1) for i in range(s - 1, n - 1)])  25 us
  transfers between devices with their start and end apart: 105, of which 38 were waited for; matrix products, arithmetic and copies ran while one was open for 26% of the time, Pallas kernels for 0%

profile of v1, /device:TPU:0, one launch (start us, length us, event | category | flops | bytes accessed | tf_op | source)
XLA Modules:
  0.0 707.8 jit_solution(198753547117930438)
XLA Ops:
  0.6 3.1 collective-permute-start
  3.7 2.6 collective-permute-start.1
  47.1 2.9 collective-permute-start.10
  53.8 5.4 collective-permute-start.48
  63.2 3.8 collective-permute-start.32
  68.6 19.6 %collective-permute-done.32 = bf16[96,1152]{1,0:T(8,128)(2,1)S(1)} collective-permute-done((bf16[96,1152]{1,0:T(8,128)(2,1)}, bf16[96,1152]{1,0:T(8,128)(2,1)S(1)}, u32[]{:S(2)}, u32[]{:S(2)}) %collective-permute-start.32) | collective-permute-done | bytes 221216 | tf_op jit(solution)/shard_map/ppermute | solution.py:48
  88.2 16.6 %collective-permute-start.33 = (bf16[96,1152]{1,0:T(8,128)(2,1)}, bf16[96,1152]{1,0:T(8,128)(2,1)S(1)}, u32[]{:S(2)}, u32[]{:S(2)}) collective-permute-start(bf16[96,1152]{1,0:T(8,128)(2,1)} %get-tuple-element.73), channel_id=1, source_target_pairs={{0,16},{8,24},{16,0},{24,8},{1,17},{9,25},{17,1},{25,9},{2,18},{10... | collective-permute-start | bytes 663560 | tf_op jit(solution)/shard_map/ppermute | solution.py:48
  104.8 7.7 %collective-permute-done.33 = bf16[96,1152]{1,0:T(8,128)(2,1)S(1)} collective-permute-done((bf16[96,1152]{1,0:T(8,128)(2,1)}, bf16[96,1152]{1,0:T(8,128)(2,1)S(1)}, u32[]{:S(2)}, u32[]{:S(2)}) %collective-permute-start.33) | collective-permute-done | bytes 221216 | tf_op jit(solution)/shard_map/ppermute | solution.py:48
  114.2 5.9 collective-permute-done.34
  120.1 4.3 collective-permute-start.29
  132.4 8.3 %collective-permute-done.11 = bf16[384,768]{1,0:T(8,128)(2,1)S(1)} collective-permute-done((bf16[384,768]{1,0:T(8,128)(2,1)S(1)}, bf16[384,768]{1,0:T(8,128)(2,1)S(1)}, u32[]{:S(2)}, u32[]{:S(2)}) %collective-permute-start.11) | collective-permute-done | bytes 589856 | tf_op jit(solution)/shard_map/ppermute | solution.py:53
  143.2 11.1 %collective-permute-done.3 = bf16[384,1024]{1,0:T(8,128)(2,1)S(1)} collective-permute-done((bf16[384,1024]{1,0:T(8,128)(2,1)}, bf16[384,1024]{1,0:T(8,128)(2,1)S(1)}, u32[]{:S(2)}, u32[]{:S(2)}) %collective-permute-start.3) | collective-permute-done | bytes 786464 | tf_op jit(solution)/shard_map/ppermute | solution.py:53
  155.7 3.4 collective-permute-start.60
  159.2 4.6 collective-permute-done.35
  164.9 3.4 collective-permute-start.56
  170.2 8.2 %collective-permute-done.56 = bf16[128,1536]{1,0:T(8,128)(2,1)S(1)} collective-permute-done((bf16[128,1536]{1,0:T(8,128)(2,1)S(1)}, bf16[128,1536]{1,0:T(8,128)(2,1)S(1)}, u32[]{:S(2)}, u32[]{:S(2)}) %collective-permute-start.56) | collective-permute-done | bytes 393248 | tf_op jit(solution)/shard_map/ppermute | solution.py:97
  185.5 26.8 %collective-permute-done.6 = bf16[2,256,128]{2,1,0:T(8,128)(2,1)S(1)} collective-permute-done((bf16[2,256,128]{2,1,0:T(8,128)(2,1)S(1)}, bf16[2,256,128]{2,1,0:T(8,128)(2,1)S(1)}, u32[]{:S(2)}, u32[]{:S(2)}) %collective-permute-start.6) | collective-permute-done | bytes 131104 | tf_op jit(solution)/shard_map/ppermute | solution.py:53
  212.8 5.2 collective-permute-done.7
  226.9 4.2 collective-permute-done.58
  231.7 9.7 %collective-permute-done.13 = bf16[128,1536]{1,0:T(8,128)(2,1)S(1)} collective-permute-done((bf16[128,1536]{1,0:T(8,128)(2,1)S(1)}, bf16[128,1536]{1,0:T(8,128)(2,1)S(1)}, u32[]{:S(2)}, u32[]{:S(2)}) %collective-permute-start.13) | collective-permute-done | bytes 393248 | tf_op jit(solution)/shard_map/ppermute | solution.py:53
  243.7 4.7 collective-permute-start.14
  248.5 5.1 collective-permute-done.15
  258.0 5.9 collective-permute-done.16
  265.2 3.1 fusion.1
  269.5 5.5 collective-permute-done.17
  275.0 12.8 %collective-permute-start.19 = (bf16[128,1536]{1,0:T(8,128)(2,1)S(1)}, bf16[128,1536]{1,0:T(8,128)(2,1)S(1)}, u32[]{:S(2)}, u32[]{:S(2)}) collective-permute-start(bf16[128,1536]{1,0:T(8,128)(2,1)S(1)} %collective-permute-done.18), channel_id=1, source_target_pairs={{16,24},{17,25},{18,26},{19,27},{20,28},{21,29},{22,30},{23,31}} | collective-permute-start | bytes 1179656 | tf_op jit(solution)/shard_map/ppermute | solution.py:100
  288.0 3.4 collective-permute-start.22
  294.7 7.2 %collective-permute-done.22 = bf16[128,1536]{1,0:T(8,128)(2,1)S(1)} collective-permute-done((bf16[128,1536]{1,0:T(8,128)(2,1)S(1)}, bf16[128,1536]{1,0:T(8,128)(2,1)S(1)}, u32[]{:S(2)}, u32[]{:S(2)}) %collective-permute-start.22) | collective-permute-done | bytes 393248 | tf_op jit(solution)/shard_map/ppermute | solution.py:97
  302.0 3.4 collective-permute-start.24
  306.2 9.0 %collective-permute-done.24 = bf16[128,1536]{1,0:T(8,128)(2,1)S(1)} collective-permute-done((bf16[128,1536]{1,0:T(8,128)(2,1)S(1)}, bf16[128,1536]{1,0:T(8,128)(2,1)S(1)}, u32[]{:S(2)}, u32[]{:S(2)}) %collective-permute-start.24) | collective-permute-done | bytes 393248 | tf_op jit(solution)/shard_map/ppermute | solution.py:97
  315.5 11.2 %fusion.11 = f32[1024,2304]{1,0:T(8,128)} fusion(bf16[1024,1536]{1,0:T(8,128)(2,1)S(1)} %select_dynamic-update-slice_fusion.6, bf16[768,2304]{1,0:T(8,128)(2,1)S(1)} %collective-permute-done.31, bf16[384,2304]{1,0:T(8,128)(2,1)S(1)} %collective-permute-done.30, bf16[384,2304]{1,0:T(8,128)(2,1)} %bitcast.50), kind=kOutput, calls=%fused_computation.35 | convolution fusion | flops 7268990976 | bytes 19660800 | tf_op jit(solution)/shard_map/dot_general | solution.py:35
  326.7 10.2 %multiply_convert_fusion.1 = (bf16[1024,1152]{1,0:T(8,128)(2,1)}, bf16[1024,1152]{1,0:T(8,128)(2,1)}, bf16[1024,1152]{1,0:T(8,128)(2,1)S(1)}) fusion(f32[1024,2304]{1,0:T(8,128)} %fusion.11, bf16[1024,1536]{1,0:T(8,128)(2,1)S(1)} %select_dynamic-update-slice_fusion, bf16[768,1152]{1,0:T(8,128)(2,1)} %collective-permute-done.36, ...), kind=kOutput, calls=%fused_computation.18 | convolution fusion | flops 3652190208 | bytes 23199744 | tf_op jit(solution)/shard_map/dot_general | solution.py:35
  336.9 3.5 convolution_convert_fusion.1
  340.5 11.4 %fusion.10 = f32[1024,1536]{1,0:T(8,128)S(1)} fusion(bf16[768,2304]{1,0:T(8,128)(2,1)} %copy-done.86, bf16[384,2304]{1,0:T(8,128)(2,1)S(1)} %copy-done.30, bf16[384,2304]{1,0:T(8,128)(2,1)} %bitcast.50, bf16[1024,1152]{1,0:T(8,128)(2,1)} %get-tuple-element.30, bf16[1024,1152]{1,0:T(8,128)(2,1)} %get-tuple-element.29), kind=kOutput, calls=%fused_computation.34 | convolution fusion | flops 7278428160 | bytes 18087936 | tf_op jit(solution)/shard_map/dot_general | solution.py:39
  356.5 5.7 fusion.19
  365.9 6.9 collective-permute-done.63
  375.8 22.3 %collective-permute-done.40 = bf16[128,1536]{1,0:T(8,128)(2,1)S(1)} collective-permute-done((bf16[128,1536]{1,0:T(8,128)(2,1)S(1)}, bf16[128,1536]{1,0:T(8,128)(2,1)S(1)}, u32[]{:S(2)}, u32[]{:S(2)}) %collective-permute-start.40) | collective-permute-done | bytes 393248 | tf_op jit(solution)/shard_map/ppermute | solution.py:53
  401.3 6.2 collective-permute-done.66
  407.5 4.4 collective-permute-start.41
  413.9 5.3 collective-permute-done.41
  420.0 4.4 collective-permute-start.42
  426.5 7.4 %collective-permute-done.42 = bf16[128,1536]{1,0:T(8,128)(2,1)S(1)} collective-permute-done((bf16[128,1536]{1,0:T(8,128)(2,1)S(1)}, bf16[128,1536]{1,0:T(8,128)(2,1)S(1)}, u32[]{:S(2)}, u32[]{:S(2)}) %collective-permute-start.42) | collective-permute-done | bytes 393248 | tf_op jit(solution)/shard_map/ppermute | solution.py:119
  439.0 13.8 %collective-permute-start.43 = (bf16[128,1536]{1,0:T(8,128)(2,1)}, bf16[128,1536]{1,0:T(8,128)(2,1)}, u32[]{:S(2)}, u32[]{:S(2)}) collective-permute-start(bf16[128,1536]{1,0:T(8,128)(2,1)} %get-tuple-element.34), channel_id=1, source_target_pairs={{0,8},{8,16},{16,24},{1,9},{9,17},{17,25},{2,10},{10,18},{18,26},{... | collective-permute-start | bytes 1179656 | tf_op jit(solution)/shard_map/ppermute | solution.py:119
  457.4 5.2 convolution_add_fusion
  468.4 5.4 convolution_convert_fusion
  473.8 3.5 collective-permute-done.92
  477.3 13.1 %collective-permute-start.93 = (f32[1,1536]{1,0:T(1,128)S(1)}, f32[1,1536]{1,0:T(1,128)S(1)}, u32[]{:S(2)}, u32[]{:S(2)}) collective-permute-start(f32[1,1536]{1,0:T(1,128)S(1)} %add.605), channel_id=1, source_target_pairs={{0,8},{8,0},{16,24},{24,16},{1,9},{9,1},{17,25},{25,17},{2,10},{10... | collective-permute-start | bytes 18440 | tf_op jit(solution)/shard_map/ppermute | solution.py:53
  492.1 3.5 collective-permute-start.94
  495.7 2.5 add_convert_fusion
  507.2 10.8 %collective-permute-done.71 = bf16[128,1536]{1,0:T(8,128)(2,1)S(1)} collective-permute-done((bf16[128,1536]{1,0:T(8,128)(2,1)S(1)}, bf16[128,1536]{1,0:T(8,128)(2,1)S(1)}, u32[]{:S(2)}, u32[]{:S(2)}) %collective-permute-start.71) | collective-permute-done | bytes 393248 | tf_op jit(solution)/shard_map/ppermute | solution.py:53
  521.1 5.7 fusion.2
  538.9 3.0 convolution_bitcast_fusion.1
  565.6 6.2 convert_add_fusion
  571.9 2.9 copy-done.13
  577.6 6.0 collective-permute-done.75
  585.5 2.8 convert_add_fusion.3
  591.9 25.8 %collective-permute-done.77 = f32[1,2560]{1,0:T(1,128)S(1)} collective-permute-done((f32[1,2560]{1,0:T(1,128)S(1)}, f32[1,2560]{1,0:T(1,128)S(1)}, u32[]{:S(2)}, u32[]{:S(2)}) %collective-permute-start.77) | collective-permute-done | bytes 10272 | tf_op jit(solution)/shard_map/ppermute | solution.py:53
  624.6 3.0 copy.68
  631.9 6.2 collective-permute-done.86
  643.8 3.8 collective-permute-done.87
  647.6 3.6 collective-permute-done.88
  665.4 21.1 %collective-permute-done.83 = bf16[96,1024]{1,0:T(8,128)(2,1)S(1)} collective-permute-done((bf16[96,1024]{1,0:T(8,128)(2,1)S(1)}, bf16[96,1024]{1,0:T(8,128)(2,1)S(1)}, u32[]{:S(2)}, u32[]{:S(2)}) %collective-permute-start.83) | collective-permute-done | bytes 196640 | tf_op jit(solution)/shard_map/ppermute | solution.py:48
  687.7 14.7 %collective-permute-done.98 = bf16[96,2304]{1,0:T(8,128)(2,1)S(1)} collective-permute-done((bf16[96,2304]{1,0:T(8,128)(2,1)S(1)}, bf16[96,2304]{1,0:T(8,128)(2,1)S(1)}, u32[]{:S(2)}, u32[]{:S(2)}) %collective-permute-start.98) | collective-permute-done | bytes 442400 | tf_op jit(solution)/shard_map/ppermute | solution.py:48
  703.2 4.4 copy.69
  (578 shorter events, 220.9 us)
Async XLA Ops:
  0.6 58.6 %collective-permute-start = (bf16[96,1024]{1,0:T(8,128)(2,1)}, bf16[96,1024]{1,0:T(8,128)(2,1)}, u32[]{:S(2)}, u32[]{:S(2)}) collective-permute-start(bf16[96,1024]{1,0:T(8,128)(2,1)} %bitcast.468), channel_id=1, source_target_pairs={{0,8},{8,16},{16,24},{24,0},{1,9},{9,17},{17,25},{25,1},{2,10},{10... | collective-permute-start | bytes 589832 | tf_op jit(solution)/shard_map/ppermute | solution.py:48
  3.7 57.4 %collective-permute-start.1 = (bf16[96,1024]{1,0:T(8,128)(2,1)}, bf16[96,1024]{1,0:T(8,128)(2,1)}, u32[]{:S(2)}, u32[]{:S(2)}) collective-permute-start(bf16[96,1024]{1,0:T(8,128)(2,1)} %bitcast.469), channel_id=1, source_target_pairs={{0,16},{8,24},{16,0},{24,8},{1,17},{9,25},{17,1},{25,9},{2,18},{10... | collective-permute-start | bytes 589832 | tf_op jit(solution)/shard_map/ppermute | solution.py:48
  6.3 56.9 %collective-permute-start.2 = (bf16[96,1024]{1,0:T(8,128)(2,1)}, bf16[96,1024]{1,0:T(8,128)(2,1)}, u32[]{:S(2)}, u32[]{:S(2)}) collective-permute-start(bf16[96,1024]{1,0:T(8,128)(2,1)} %bitcast.470), channel_id=1, source_target_pairs={{0,24},{8,0},{16,8},{24,16},{1,25},{9,1},{17,9},{25,17},{2,26},{10... | collective-permute-start | bytes 589832 | tf_op jit(solution)/shard_map/ppermute | solution.py:48
  7.7 39.4 %collective-permute-start.8 = (bf16[96,768]{1,0:T(8,128)(2,1)}, bf16[96,768]{1,0:T(8,128)(2,1)}, u32[]{:S(2)}, u32[]{:S(2)}) collective-permute-start(bf16[96,768]{1,0:T(8,128)(2,1)} %bitcast.471), channel_id=1, source_target_pairs={{0,8},{8,16},{16,24},{24,0},{1,9},{9,17},{17,25},{25,1},{2,10},{10... | collective-permute-start | bytes 442376 | tf_op jit(solution)/shard_map/ppermute | solution.py:48
  8.3 42.6 %collective-permute-start.9 = (bf16[96,768]{1,0:T(8,128)(2,1)}, bf16[96,768]{1,0:T(8,128)(2,1)}, u32[]{:S(2)}, u32[]{:S(2)}) collective-permute-start(bf16[96,768]{1,0:T(8,128)(2,1)} %bitcast.472), channel_id=1, source_target_pairs={{0,16},{8,24},{16,0},{24,8},{1,17},{9,25},{17,1},{25,9},{2,18},{10... | collective-permute-start | bytes 442376 | tf_op jit(solution)/shard_map/ppermute | solution.py:48
  50.9 77.3 %collective-permute-start.49 = (bf16[128,1536]{1,0:T(8,128)(2,1)S(1)}, bf16[128,1536]{1,0:T(8,128)(2,1)S(1)}, u32[]{:S(2)}, u32[]{:S(2)}) collective-permute-start(bf16[128,1536]{1,0:T(8,128)(2,1)S(1)} %copy.88), channel_id=1, source_target_pairs={{8,0},{16,8},{24,16},{9,1},{17,9},{25,17},{10,2},{18,10},{26,18},{... | collective-permute-start | bytes 1179656 | tf_op jit(solution)/shard_map/ppermute | solution.py:101
  53.8 75.8 %collective-permute-start.48 = (bf16[128,1536]{1,0:T(8,128)(2,1)S(1)}, bf16[128,1536]{1,0:T(8,128)(2,1)S(1)}, u32[]{:S(2)}, u32[]{:S(2)}) collective-permute-start(bf16[128,1536]{1,0:T(8,128)(2,1)S(1)} %copy.88), channel_id=1, source_target_pairs={{0,8},{8,16},{16,24},{1,9},{9,17},{17,25},{2,10},{10,18},{18,26},{... | collective-permute-start | bytes 1179656 | tf_op jit(solution)/shard_map/ppermute | solution.py:100
  59.3 65.1 %collective-permute-start.27 = (bf16[96,2304]{1,0:T(8,128)(2,1)}, bf16[96,2304]{1,0:T(8,128)(2,1)S(1)}, u32[]{:S(2)}, u32[]{:S(2)}) collective-permute-start(bf16[96,2304]{1,0:T(8,128)(2,1)} %pad_maximum_fusion.26), channel_id=1, source_target_pairs={{0,8},{8,16},{16,24},{24,0},{1,9},{9,17},{17,25},{25,1},{2,10},{10... | collective-permute-start | bytes 1327112 | tf_op jit(solution)/shard_map/ppermute | solution.py:48
  61.1 65.6 %collective-permute-start.28 = (bf16[96,2304]{1,0:T(8,128)(2,1)}, bf16[96,2304]{1,0:T(8,128)(2,1)S(1)}, u32[]{:S(2)}, u32[]{:S(2)}) collective-permute-start(bf16[96,2304]{1,0:T(8,128)(2,1)} %pad_maximum_fusion.27), channel_id=1, source_target_pairs={{0,16},{8,24},{16,0},{24,8},{1,17},{9,25},{17,1},{25,9},{2,18},{10... | collective-permute-start | bytes 1327112 | tf_op jit(solution)/shard_map/ppermute | solution.py:48
  63.2 25.0 %collective-permute-start.32 = (bf16[96,1152]{1,0:T(8,128)(2,1)}, bf16[96,1152]{1,0:T(8,128)(2,1)S(1)}, u32[]{:S(2)}, u32[]{:S(2)}) collective-permute-start(bf16[96,1152]{1,0:T(8,128)(2,1)} %get-tuple-element.72), channel_id=1, source_target_pairs={{0,8},{8,16},{16,24},{24,0},{1,9},{9,17},{17,25},{25,1},{2,10},{10... | collective-permute-start | bytes 663560 | tf_op jit(solution)/shard_map/ppermute | solution.py:48
  88.2 24.3 %collective-permute-start.33 = (bf16[96,1152]{1,0:T(8,128)(2,1)}, bf16[96,1152]{1,0:T(8,128)(2,1)S(1)}, u32[]{:S(2)}, u32[]{:S(2)}) collective-permute-start(bf16[96,1152]{1,0:T(8,128)(2,1)} %get-tuple-element.73), channel_id=1, source_target_pairs={{0,16},{8,24},{16,0},{24,8},{1,17},{9,25},{17,1},{25,9},{2,18},{10... | collective-permute-start | bytes 663560 | tf_op jit(solution)/shard_map/ppermute | solution.py:48
  124.4 16.3 %collective-permute-start.11 = (bf16[384,768]{1,0:T(8,128)(2,1)S(1)}, bf16[384,768]{1,0:T(8,128)(2,1)S(1)}, u32[]{:S(2)}, u32[]{:S(2)}) collective-permute-start(bf16[384,768]{1,0:T(8,128)(2,1)S(1)} %bitcast.457), channel_id=1, source_target_pairs={{0,4},{2,6},{4,0},{6,2},{1,5},{3,7},{5,1},{7,3},{8,12},{10,14},{12... | collective-permute-start | bytes 1769480 | tf_op jit(solution)/shard_map/ppermute | solution.py:53
  126.8 27.5 %collective-permute-start.3 = (bf16[384,1024]{1,0:T(8,128)(2,1)}, bf16[384,1024]{1,0:T(8,128)(2,1)S(1)}, u32[]{:S(2)}, u32[]{:S(2)}) collective-permute-start(bf16[384,1024]{1,0:T(8,128)(2,1)} %bitcast.451), channel_id=1, source_target_pairs={{0,4},{2,6},{4,0},{6,2},{1,5},{3,7},{5,1},{7,3},{8,12},{10,14},{12... | collective-permute-start | bytes 2359304 | tf_op jit(solution)/shard_map/ppermute | solution.py:53
  128.2 35.6 %collective-permute-start.35 = (bf16[384,1152]{1,0:T(8,128)(2,1)S(1)}, bf16[384,1152]{1,0:T(8,128)(2,1)S(1)}, u32[]{:S(2)}, u32[]{:S(2)}) collective-permute-start(bf16[384,1152]{1,0:T(8,128)(2,1)S(1)} %bitcast.433), channel_id=1, source_target_pairs={{0,4},{2,6},{4,0},{6,2},{1,5},{3,7},{5,1},{7,3},{8,12},{10,14},{12... | collective-permute-start | bytes 2654216 | tf_op jit(solution)/shard_map/ppermute | solution.py:53
  130.9 24.8 %collective-permute-start.52 = (bf16[128,1536]{1,0:T(8,128)(2,1)S(1)}, bf16[128,1536]{1,0:T(8,128)(2,1)S(1)}, u32[]{:S(2)}, u32[]{:S(2)}) collective-permute-start(bf16[128,1536]{1,0:T(8,128)(2,1)S(1)} %collective-permute-done.48), channel_id=1, source_target_pairs={{8,16},{16,24},{9,17},{17,25},{10,18},{18,26},{11,19},{19,27},{12,... | collective-permute-start | bytes 1179656 | tf_op jit(solution)/shard_map/ppermute | solution.py:100
  140.7 27.8 %collective-permute-start.54 = (bf16[128,1536]{1,0:T(8,128)(2,1)S(1)}, bf16[128,1536]{1,0:T(8,128)(2,1)S(1)}, u32[]{:S(2)}, u32[]{:S(2)}) collective-permute-start(bf16[128,1536]{1,0:T(8,128)(2,1)S(1)} %copy.88), channel_id=1, source_target_pairs={{0,1},{1,0},{2,3},{3,2},{4,5},{5,4},{6,7},{7,6},{8,9},{9,8},{10,11... | collective-permute-start | bytes 1179656 | tf_op jit(solution)/shard_map/ppermute | solution.py:53
  142.3 27.7 %collective-permute-start.55 = (bf16[128,1536]{1,0:T(8,128)(2,1)S(1)}, bf16[128,1536]{1,0:T(8,128)(2,1)S(1)}, u32[]{:S(2)}, u32[]{:S(2)}) collective-permute-start(bf16[128,1536]{1,0:T(8,128)(2,1)S(1)} %collective-permute-done.48), channel_id=1, source_target_pairs={{8,9},{9,8},{16,17},{17,16},{24,25},{25,24},{10,11},{11,10},{18,19... | collective-permute-start | bytes 1179656 | tf_op jit(solution)/shard_map/ppermute | solution.py:97
  155.7 87.9 %collective-permute-start.60 = (bf16[128,1536]{1,0:T(8,128)(2,1)S(1)}, bf16[128,1536]{1,0:T(8,128)(2,1)S(1)}, u32[]{:S(2)}, u32[]{:S(2)}) collective-permute-start(bf16[128,1536]{1,0:T(8,128)(2,1)S(1)} %collective-permute-done.49), channel_id=1, source_target_pairs={{0,1},{1,0},{8,9},{9,8},{16,17},{17,16},{2,3},{3,2},{10,11},{11,10... | collective-permute-start | bytes 1179656 | tf_op jit(solution)/shard_map/ppermute | solution.py:97
  164.6 14.7 %collective-permute-start.4 = (bf16[768,1024]{1,0:T(8,128)(2,1)S(1)}, bf16[768,1024]{1,0:T(8,128)(2,1)S(1)}, u32[]{:S(2)}, u32[]{:S(2)}) collective-permute-start(bf16[768,1024]{1,0:T(8,128)(2,1)S(1)} %pad_maximum_fusion.9), channel_id=1, source_target_pairs={{0,2},{2,0},{4,6},{6,4},{1,3},{3,1},{5,7},{7,5},{8,10},{10,8},{12,... | collective-permute-start | bytes 4718600 | tf_op jit(solution)/shard_map/ppermute | solution.py:53
  168.5 86.4 %collective-permute-start.30 = (bf16[384,2304]{1,0:T(8,128)(2,1)}, bf16[384,2304]{1,0:T(8,128)(2,1)S(1)}, u32[]{:S(2)}, u32[]{:S(2)}) collective-permute-start(bf16[384,2304]{1,0:T(8,128)(2,1)} %bitcast.50), channel_id=1, source_target_pairs={{0,4},{2,6},{4,0},{6,2},{1,5},{3,7},{5,1},{7,3},{8,12},{10,14},{12... | collective-permute-start | bytes 5308424 | tf_op jit(solution)/shard_map/ppermute | solution.py:53
  170.1 54.9 %collective-permute-start.12 = (bf16[768,768]{1,0:T(8,128)(2,1)S(1)}, bf16[768,768]{1,0:T(8,128)(2,1)S(1)}, u32[]{:S(2)}, u32[]{:S(2)}) collective-permute-start(bf16[768,768]{1,0:T(8,128)(2,1)S(1)} %pad_maximum_fusion.20), channel_id=1, source_target_pairs={{0,2},{2,0},{4,6},{6,4},{1,3},{3,1},{5,7},{7,5},{8,10},{10,8},{12,... | collective-permute-start | bytes 3538952 | tf_op jit(solution)/shard_map/ppermute | solution.py:53
  178.3 47.8 %collective-permute-start.57 = (bf16[128,1536]{1,0:T(8,128)(2,1)S(1)}, bf16[128,1536]{1,0:T(8,128)(2,1)S(1)}, u32[]{:S(2)}, u32[]{:S(2)}) collective-permute-start(bf16[128,1536]{1,0:T(8,128)(2,1)S(1)} %collective-permute-done.52), channel_id=1, source_target_pairs={{16,17},{17,16},{24,25},{25,24},{18,19},{19,18},{26,27},{27,26},{2... | collective-permute-start | bytes 1179656 | tf_op jit(solution)/shard_map/ppermute | solution.py:97
  183.9 28.4 %collective-permute-start.6 = (bf16[2,256,128]{2,1,0:T(8,128)(2,1)S(1)}, bf16[2,256,128]{2,1,0:T(8,128)(2,1)S(1)}, u32[]{:S(2)}, u32[]{:S(2)}) collective-permute-start(bf16[2,256,128]{2,1,0:T(8,128)(2,1)S(1)} %pad_maximum_fusion.30), channel_id=1, source_target_pairs={{0,4},{2,6},{4,0},{6,2},{1,5},{3,7},{5,1},{7,3},{8,12},{10,14},{12... | collective-permute-start | bytes 393224 | tf_op jit(solution)/shard_map/ppermute | solution.py:53
  225.0 101.7 %collective-permute-start.36 = (bf16[768,1152]{1,0:T(8,128)(2,1)S(1)}, bf16[768,1152]{1,0:T(8,128)(2,1)}, u32[]{:S(2)}, u32[]{:S(2)}) collective-permute-start(bf16[768,1152]{1,0:T(8,128)(2,1)S(1)} %pad_maximum_fusion.8), channel_id=1, source_target_pairs={{0,2},{2,0},{4,6},{6,4},{1,3},{3,1},{5,7},{7,5},{8,10},{10,8},{12,... | collective-permute-start | bytes 5308424 | tf_op jit(solution)/shard_map/ppermute | solution.py:53
  226.2 17.4 %collective-permute-start.59 = (bf16[128,1536]{1,0:T(8,128)(2,1)S(1)}, bf16[128,1536]{1,0:T(8,128)(2,1)S(1)}, u32[]{:S(2)}, u32[]{:S(2)}) collective-permute-start(bf16[128,1536]{1,0:T(8,128)(2,1)S(1)} %collective-permute-done.53), channel_id=1, source_target_pairs={{24,25},{25,24},{26,27},{27,26},{28,29},{29,28},{30,31},{31,30}} | collective-permute-start | bytes 1179656 | tf_op jit(solution)/shard_map/ppermute | solution.py:97
  243.7 13.6 %collective-permute-start.14 = (bf16[128,1536]{1,0:T(8,128)(2,1)S(1)}, bf16[128,1536]{1,0:T(8,128)(2,1)S(1)}, u32[]{:S(2)}, u32[]{:S(2)}) collective-permute-start(bf16[128,1536]{1,0:T(8,128)(2,1)S(1)} %get-tuple-element.26), channel_id=1, source_target_pairs={{0,8},{8,16},{16,24},{1,9},{9,17},{17,25},{2,10},{10,18},{18,26},{... | collective-permute-start | bytes 1179656 | tf_op jit(solution)/shard_map/ppermute | solution.py:100
  257.2 58.2 %collective-permute-start.31 = (bf16[768,2304]{1,0:T(8,128)(2,1)S(1)}, bf16[768,2304]{1,0:T(8,128)(2,1)S(1)}, u32[]{:S(2)}, u32[]{:S(2)}) collective-permute-start(bf16[768,2304]{1,0:T(8,128)(2,1)S(1)} %pad_maximum_fusion.2), channel_id=1, source_target_pairs={{0,2},{2,0},{4,6},{6,4},{1,3},{3,1},{5,7},{7,5},{8,10},{10,8},{12,... | collective-permute-start | bytes 10616840 | tf_op jit(solution)/shard_map/ppermute | solution.py:53
  268.3 23.3 %collective-permute-start.20 = (bf16[128,1536]{1,0:T(8,128)(2,1)S(1)}, bf16[128,1536]{1,0:T(8,128)(2,1)S(1)}, u32[]{:S(2)}, u32[]{:S(2)}) collective-permute-start(bf16[128,1536]{1,0:T(8,128)(2,1)S(1)} %get-tuple-element.26), channel_id=1, source_target_pairs={{0,1},{1,0},{2,3},{3,2},{4,5},{5,4},{6,7},{7,6},{8,9},{9,8},{10,11... | collective-permute-start | bytes 1179656 | tf_op jit(solution)/shard_map/ppermute | solution.py:53
  268.8 25.2 %collective-permute-start.21 = (bf16[128,1536]{1,0:T(8,128)(2,1)S(1)}, bf16[128,1536]{1,0:T(8,128)(2,1)S(1)}, u32[]{:S(2)}, u32[]{:S(2)}) collective-permute-start(bf16[128,1536]{1,0:T(8,128)(2,1)S(1)} %collective-permute-done.14), channel_id=1, source_target_pairs={{8,9},{9,8},{16,17},{17,16},{24,25},{25,24},{10,11},{11,10},{18,19... | collective-permute-start | bytes 1179656 | tf_op jit(solution)/shard_map/ppermute | solution.py:97
  288.0 13.9 %collective-permute-start.22 = (bf16[128,1536]{1,0:T(8,128)(2,1)S(1)}, bf16[128,1536]{1,0:T(8,128)(2,1)S(1)}, u32[]{:S(2)}, u32[]{:S(2)}) collective-permute-start(bf16[128,1536]{1,0:T(8,128)(2,1)S(1)} %collective-permute-done.17), channel_id=1, source_target_pairs={{0,1},{1,0},{2,3},{3,2},{4,5},{5,4},{6,7},{7,6}} | collective-permute-start | bytes 1179656 | tf_op jit(solution)/shard_map/ppermute | solution.py:97
  291.6 23.7 %collective-permute-start.26 = (bf16[128,1536]{1,0:T(8,128)(2,1)S(1)}, bf16[128,1536]{1,0:T(8,128)(2,1)S(1)}, u32[]{:S(2)}, u32[]{:S(2)}) collective-permute-start(bf16[128,1536]{1,0:T(8,128)(2,1)S(1)} %collective-permute-done.15), channel_id=1, source_target_pairs={{0,1},{1,0},{8,9},{9,8},{16,17},{17,16},{2,3},{3,2},{10,11},{11,10... | collective-permute-start | bytes 1179656 | tf_op jit(solution)/shard_map/ppermute | solution.py:97
  340.5 116.9 %collective-permute-start.100 = (bf16[768,1152]{1,0:T(8,128)(2,1)}, bf16[768,1152]{1,0:T(8,128)(2,1)}, u32[]{:S(2)}, u32[]{:S(2)}) collective-permute-start(bf16[768,1152]{1,0:T(8,128)(2,1)} %convolution_convert_fusion.1), channel_id=1, source_target_pairs={{0,2},{2,0},{4,6},{6,4},{1,3},{3,1},{5,7},{7,5},{8,10},{10,8},{12,... | collective-permute-start | bytes 5308424 | tf_op jit(solution)/shard_map/ppermute | solution.py:53
  354.2 18.6 %collective-permute-start.63 = (bf16[128,1536]{1,0:T(8,128)(2,1)S(1)}, bf16[128,1536]{1,0:T(8,128)(2,1)S(1)}, u32[]{:S(2)}, u32[]{:S(2)}) collective-permute-start(bf16[128,1536]{1,0:T(8,128)(2,1)S(1)} %get-tuple-element.38), channel_id=1, source_target_pairs={{0,1},{1,0},{2,3},{3,2},{4,5},{5,4},{6,7},{7,6},{8,9},{9,8},{10,11... | collective-permute-start | bytes 1179656 | tf_op jit(solution)/shard_map/ppermute | solution.py:53
  354.5 45.0 %collective-permute-start.62 = (bf16[128,1536]{1,0:T(8,128)(2,1)S(1)}, bf16[128,1536]{1,0:T(8,128)(2,1)S(1)}, u32[]{:S(2)}, u32[]{:S(2)}) collective-permute-start(bf16[128,1536]{1,0:T(8,128)(2,1)S(1)} %get-tuple-element.39), channel_id=1, source_target_pairs={{0,1},{1,0},{2,3},{3,2},{4,5},{5,4},{6,7},{7,6},{8,9},{9,8},{10,11... | collective-permute-start | bytes 1179656 | tf_op jit(solution)/shard_map/ppermute | solution.py:53
  356.2 82.8 %collective-permute-start.61 = (bf16[128,1536]{1,0:T(8,128)(2,1)S(1)}, bf16[128,1536]{1,0:T(8,128)(2,1)S(1)}, u32[]{:S(2)}, u32[]{:S(2)}) collective-permute-start(bf16[128,1536]{1,0:T(8,128)(2,1)S(1)} %get-tuple-element.36), channel_id=1, source_target_pairs={{0,1},{1,0},{2,3},{3,2},{4,5},{5,4},{6,7},{7,6},{8,9},{9,8},{10,11... | collective-permute-start | bytes 1179656 | tf_op jit(solution)/shard_map/ppermute | solution.py:53
  372.8 25.3 %collective-permute-start.40 = (bf16[128,1536]{1,0:T(8,128)(2,1)S(1)}, bf16[128,1536]{1,0:T(8,128)(2,1)S(1)}, u32[]{:S(2)}, u32[]{:S(2)}) collective-permute-start(bf16[128,1536]{1,0:T(8,128)(2,1)S(1)} %get-tuple-element.41), channel_id=1, source_target_pairs={{0,1},{1,0},{2,3},{3,2},{4,5},{5,4},{6,7},{7,6},{8,9},{9,8},{10,11... | collective-permute-start | bytes 1179656 | tf_op jit(solution)/shard_map/ppermute | solution.py:53
  374.5 37.5 %collective-permute-start.39 = (bf16[128,1536]{1,0:T(8,128)(2,1)S(1)}, bf16[128,1536]{1,0:T(8,128)(2,1)S(1)}, u32[]{:S(2)}, u32[]{:S(2)}) collective-permute-start(bf16[128,1536]{1,0:T(8,128)(2,1)S(1)} %get-tuple-element.42), channel_id=1, source_target_pairs={{0,1},{1,0},{2,3},{3,2},{4,5},{5,4},{6,7},{7,6},{8,9},{9,8},{10,11... | collective-permute-start | bytes 1179656 | tf_op jit(solution)/shard_map/ppermute | solution.py:53
  399.5 25.0 %collective-permute-start.38 = (bf16[128,1536]{1,0:T(8,128)(2,1)S(1)}, bf16[128,1536]{1,0:T(8,128)(2,1)S(1)}, u32[]{:S(2)}, u32[]{:S(2)}) collective-permute-start(bf16[128,1536]{1,0:T(8,128)(2,1)S(1)} %get-tuple-element.43), channel_id=1, source_target_pairs={{0,1},{1,0},{2,3},{3,2},{4,5},{5,4},{6,7},{7,6},{8,9},{9,8},{10,11... | collective-permute-start | bytes 1179656 | tf_op jit(solution)/shard_map/ppermute | solution.py:53
  412.1 80.0 %collective-permute-start.37 = (bf16[128,1536]{1,0:T(8,128)(2,1)S(1)}, bf16[128,1536]{1,0:T(8,128)(2,1)}, u32[]{:S(2)}, u32[]{:S(2)}) collective-permute-start(bf16[128,1536]{1,0:T(8,128)(2,1)S(1)} %get-tuple-element.40), channel_id=1, source_target_pairs={{0,1},{1,0},{2,3},{3,2},{4,5},{5,4},{6,7},{7,6},{8,9},{9,8},{10,11... | collective-permute-start | bytes 1179656 | tf_op jit(solution)/shard_map/ppermute | solution.py:53
  420.0 13.9 %collective-permute-start.42 = (bf16[128,1536]{1,0:T(8,128)(2,1)S(1)}, bf16[128,1536]{1,0:T(8,128)(2,1)S(1)}, u32[]{:S(2)}, u32[]{:S(2)}) collective-permute-start(bf16[128,1536]{1,0:T(8,128)(2,1)S(1)} %add_convert_fusion.8), channel_id=1, source_target_pairs={{0,8},{8,16},{1,9},{9,17},{2,10},{10,18},{3,11},{11,19},{4,12},{12... | collective-permute-start | bytes 1179656 | tf_op jit(solution)/shard_map/ppermute | solution.py:119
  424.5 28.3 %collective-permute-start.67 = (bf16[128,1536]{1,0:T(8,128)(2,1)S(1)}, bf16[128,1536]{1,0:T(8,128)(2,1)S(1)}, u32[]{:S(2)}, u32[]{:S(2)}) collective-permute-start(bf16[128,1536]{1,0:T(8,128)(2,1)S(1)} %get-tuple-element.32), channel_id=1, source_target_pairs={{0,8},{8,16},{16,24},{1,9},{9,17},{17,25},{2,10},{10,18},{18,26},{... | collective-permute-start | bytes 1179656 | tf_op jit(solution)/shard_map/ppermute | solution.py:119
  436.7 18.2 %collective-permute-start.70 = (bf16[128,1536]{1,0:T(8,128)(2,1)S(1)}, bf16[128,1536]{1,0:T(8,128)(2,1)S(1)}, u32[]{:S(2)}, u32[]{:S(2)}) collective-permute-start(bf16[128,1536]{1,0:T(8,128)(2,1)S(1)} %add_convert_fusion.1), channel_id=1, source_target_pairs={{8,0},{16,8},{24,16},{9,1},{17,9},{25,17},{10,2},{18,10},{26,18},{... | collective-permute-start | bytes 1179656 | tf_op jit(solution)/shard_map/ppermute | solution.py:120
  439.0 56.7 %collective-permute-start.43 = (bf16[128,1536]{1,0:T(8,128)(2,1)}, bf16[128,1536]{1,0:T(8,128)(2,1)}, u32[]{:S(2)}, u32[]{:S(2)}) collective-permute-start(bf16[128,1536]{1,0:T(8,128)(2,1)} %get-tuple-element.34), channel_id=1, source_target_pairs={{0,8},{8,16},{16,24},{1,9},{9,17},{17,25},{2,10},{10,18},{18,26},{... | collective-permute-start | bytes 1179656 | tf_op jit(solution)/shard_map/ppermute | solution.py:119
  463.6 39.2 %collective-permute-start.101 = (bf16[384,1152]{1,0:T(8,128)(2,1)}, bf16[384,1152]{1,0:T(8,128)(2,1)}, u32[]{:S(2)}, u32[]{:S(2)}) collective-permute-start(bf16[384,1152]{1,0:T(8,128)(2,1)} %slice.610), channel_id=1, source_target_pairs={{0,4},{2,6},{4,0},{6,2},{1,5},{3,7},{5,1},{7,3},{8,12},{10,14},{12... | collective-permute-start | bytes 2654216 | tf_op jit(solution)/shard_map/ppermute | solution.py:53
  466.3 29.3 %collective-permute-start.46 = (bf16[128,1536]{1,0:T(8,128)(2,1)S(1)}, bf16[128,1536]{1,0:T(8,128)(2,1)S(1)}, u32[]{:S(2)}, u32[]{:S(2)}) collective-permute-start(bf16[128,1536]{1,0:T(8,128)(2,1)S(1)} %add_convert_fusion.5), channel_id=1, source_target_pairs={{8,0},{16,8},{24,16},{9,1},{17,9},{25,17},{10,2},{18,10},{26,18},{... | collective-permute-start | bytes 1179656 | tf_op jit(solution)/shard_map/ppermute | solution.py:120
  477.3 14.8 %collective-permute-start.93 = (f32[1,1536]{1,0:T(1,128)S(1)}, f32[1,1536]{1,0:T(1,128)S(1)}, u32[]{:S(2)}, u32[]{:S(2)}) collective-permute-start(f32[1,1536]{1,0:T(1,128)S(1)} %add.605), channel_id=1, source_target_pairs={{0,8},{8,0},{16,24},{24,16},{1,9},{9,1},{17,25},{25,17},{2,10},{10... | collective-permute-start | bytes 18440 | tf_op jit(solution)/shard_map/ppermute | solution.py:53
  492.1 72.3 %collective-permute-start.95 = (bf16[768,2304]{1,0:T(8,128)(2,1)}, bf16[768,2304]{1,0:T(8,128)(2,1)}, u32[]{:S(2)}, u32[]{:S(2)}) collective-permute-start(bf16[768,2304]{1,0:T(8,128)(2,1)} %convolution_convert_fusion), channel_id=1, source_target_pairs={{0,2},{2,0},{4,6},{6,4},{1,3},{3,1},{5,7},{7,5},{8,10},{10,8},{12,... | collective-permute-start | bytes 10616840 | tf_op jit(solution)/shard_map/ppermute | solution.py:53
  498.2 33.9 %collective-permute-start.47 = (bf16[128,1536]{1,0:T(8,128)(2,1)}, bf16[128,1536]{1,0:T(8,128)(2,1)}, u32[]{:S(2)}, u32[]{:S(2)}) collective-permute-start(bf16[128,1536]{1,0:T(8,128)(2,1)} %get-tuple-element.85), channel_id=1, source_target_pairs={{0,1},{1,0},{2,3},{3,2},{4,5},{5,4},{6,7},{7,6},{8,9},{9,8},{10,11... | collective-permute-start | bytes 1179656 | tf_op jit(solution)/shard_map/ppermute | solution.py:53
  500.5 17.6 %collective-permute-start.71 = (bf16[128,1536]{1,0:T(8,128)(2,1)S(1)}, bf16[128,1536]{1,0:T(8,128)(2,1)S(1)}, u32[]{:S(2)}, u32[]{:S(2)}) collective-permute-start(bf16[128,1536]{1,0:T(8,128)(2,1)S(1)} %get-tuple-element.84), channel_id=1, source_target_pairs={{0,1},{1,0},{2,3},{3,2},{4,5},{5,4},{6,7},{7,6},{8,9},{9,8},{10,11... | collective-permute-start | bytes 1179656 | tf_op jit(solution)/shard_map/ppermute | solution.py:53
  505.6 36.5 %collective-permute-start.102 = (bf16[96,1152]{1,0:T(8,128)(2,1)}, bf16[96,1152]{1,0:T(8,128)(2,1)}, u32[]{:S(2)}, u32[]{:S(2)}) collective-permute-start(bf16[96,1152]{1,0:T(8,128)(2,1)} %get-tuple-element.70), channel_id=1, source_target_pairs={{0,8},{8,16},{16,24},{24,0},{1,9},{9,17},{17,25},{25,1},{2,10},{10... | collective-permute-start | bytes 663560 | tf_op jit(solution)/shard_map/ppermute | solution.py:48
  506.7 36.9 %collective-permute-start.103 = (bf16[96,1152]{1,0:T(8,128)(2,1)}, bf16[96,1152]{1,0:T(8,128)(2,1)}, u32[]{:S(2)}, u32[]{:S(2)}) collective-permute-start(bf16[96,1152]{1,0:T(8,128)(2,1)} %get-tuple-element.69), channel_id=1, source_target_pairs={{0,16},{8,24},{16,0},{24,8},{1,17},{9,25},{17,1},{25,9},{2,18},{10... | collective-permute-start | bytes 663560 | tf_op jit(solution)/shard_map/ppermute | solution.py:48
  518.1 27.2 %collective-permute-start.104 = (bf16[96,1152]{1,0:T(8,128)(2,1)}, bf16[96,1152]{1,0:T(8,128)(2,1)}, u32[]{:S(2)}, u32[]{:S(2)}) collective-permute-start(bf16[96,1152]{1,0:T(8,128)(2,1)} %get-tuple-element.68), channel_id=1, source_target_pairs={{0,24},{8,0},{16,8},{24,16},{1,25},{9,1},{17,9},{25,17},{2,26},{10... | collective-permute-start | bytes 663560 | tf_op jit(solution)/shard_map/ppermute | solution.py:48
  532.1 86.8 %collective-permute-start.85 = (bf16[768,768]{1,0:T(8,128)(2,1)}, bf16[768,768]{1,0:T(8,128)(2,1)}, u32[]{:S(2)}, u32[]{:S(2)}) collective-permute-start(bf16[768,768]{1,0:T(8,128)(2,1)} %convolution_convert_fusion.4), channel_id=1, source_target_pairs={{0,2},{2,0},{4,6},{6,4},{1,3},{3,1},{5,7},{7,5},{8,10},{10,8},{12,... | collective-permute-start | bytes 3538952 | tf_op jit(solution)/shard_map/ppermute | solution.py:53
  562.3 65.9 %collective-permute-start.80 = (bf16[768,1024]{1,0:T(8,128)(2,1)}, bf16[768,1024]{1,0:T(8,128)(2,1)}, u32[]{:S(2)}, u32[]{:S(2)}) collective-permute-start(bf16[768,1024]{1,0:T(8,128)(2,1)} %convolution_convert_fusion.3), channel_id=1, source_target_pairs={{0,2},{2,0},{4,6},{6,4},{1,3},{3,1},{5,7},{7,5},{8,10},{10,8},{12,... | collective-permute-start | bytes 4718600 | tf_op jit(solution)/shard_map/ppermute | solution.py:53
  564.0 19.5 %collective-permute-start.75 = (bf16[256,1536]{1,0:T(8,128)(2,1)S(1)}, bf16[256,1536]{1,0:T(8,128)(2,1)S(1)}, u32[]{:S(2)}, u32[]{:S(2)}) collective-permute-start(bf16[256,1536]{1,0:T(8,128)(2,1)S(1)} %convolution_convert_fusion.2), channel_id=1, source_target_pairs={{0,1},{1,0},{2,3},{3,2},{4,5},{5,4},{6,7},{7,6},{8,9},{9,8},{10,11... | collective-permute-start | bytes 2359304 | tf_op jit(solution)/shard_map/ppermute | solution.py:53
  576.2 81.6 %collective-permute-start.96 = (bf16[384,2304]{1,0:T(8,128)(2,1)}, bf16[384,2304]{1,0:T(8,128)(2,1)}, u32[]{:S(2)}, u32[]{:S(2)}) collective-permute-start(bf16[384,2304]{1,0:T(8,128)(2,1)} %slice.609), channel_id=1, source_target_pairs={{0,4},{2,6},{4,0},{6,2},{1,5},{3,7},{5,1},{7,3},{8,12},{10,14},{12... | collective-permute-start | bytes 5308424 | tf_op jit(solution)/shard_map/ppermute | solution.py:53
  590.4 27.3 %collective-permute-start.77 = (f32[1,2560]{1,0:T(1,128)S(1)}, f32[1,2560]{1,0:T(1,128)S(1)}, u32[]{:S(2)}, u32[]{:S(2)}) collective-permute-start(f32[1,2560]{1,0:T(1,128)S(1)} %fusion.99), channel_id=1, source_target_pairs={{0,4},{2,6},{4,0},{6,2},{1,5},{3,7},{5,1},{7,3},{8,12},{10,14},{12... | collective-permute-start | bytes 30728 | tf_op jit(solution)/shard_map/ppermute | solution.py:53
  621.6 16.6 %collective-permute-start.86 = (bf16[384,768]{1,0:T(8,128)(2,1)}, bf16[384,768]{1,0:T(8,128)(2,1)}, u32[]{:S(2)}, u32[]{:S(2)}) collective-permute-start(bf16[384,768]{1,0:T(8,128)(2,1)} %slice.612), channel_id=1, source_target_pairs={{0,4},{2,6},{4,0},{6,2},{1,5},{3,7},{5,1},{7,3},{8,12},{10,14},{12... | collective-permute-start | bytes 1769480 | tf_op jit(solution)/shard_map/ppermute | solution.py:53
  630.7 22.8 %collective-permute-start.81 = (bf16[384,1024]{1,0:T(8,128)(2,1)S(1)}, bf16[384,1024]{1,0:T(8,128)(2,1)S(1)}, u32[]{:S(2)}, u32[]{:S(2)}) collective-permute-start(bf16[384,1024]{1,0:T(8,128)(2,1)S(1)} %slice.611), channel_id=1, source_target_pairs={{0,4},{2,6},{4,0},{6,2},{1,5},{3,7},{5,1},{7,3},{8,12},{10,14},{12... | collective-permute-start | bytes 2359304 | tf_op jit(solution)/shard_map/ppermute | solution.py:53
  655.3 31.2 %collective-permute-start.83 = (bf16[96,1024]{1,0:T(8,128)(2,1)S(1)}, bf16[96,1024]{1,0:T(8,128)(2,1)S(1)}, u32[]{:S(2)}, u32[]{:S(2)}) collective-permute-start(bf16[96,1024]{1,0:T(8,128)(2,1)S(1)} %get-tuple-element.52), channel_id=1, source_target_pairs={{0,16},{8,24},{16,0},{24,8},{1,17},{9,25},{17,1},{25,9},{2,18},{10... | collective-permute-start | bytes 589832 | tf_op jit(solution)/shard_map/ppermute | solution.py:48
  656.5 30.0 %collective-permute-start.84 = (bf16[96,1024]{1,0:T(8,128)(2,1)S(1)}, bf16[96,1024]{1,0:T(8,128)(2,1)S(1)}, u32[]{:S(2)}, u32[]{:S(2)}) collective-permute-start(bf16[96,1024]{1,0:T(8,128)(2,1)S(1)} %get-tuple-element.51), channel_id=1, source_target_pairs={{0,24},{8,0},{16,8},{24,16},{1,25},{9,1},{17,9},{25,17},{2,26},{10... | collective-permute-start | bytes 589832 | tf_op jit(solution)/shard_map/ppermute | solution.py:48
  659.7 27.9 %collective-permute-start.97 = (bf16[96,2304]{1,0:T(8,128)(2,1)S(1)}, bf16[96,2304]{1,0:T(8,128)(2,1)S(1)}, u32[]{:S(2)}, u32[]{:S(2)}) collective-permute-start(bf16[96,2304]{1,0:T(8,128)(2,1)S(1)} %get-tuple-element.46), channel_id=1, source_target_pairs={{0,8},{8,16},{16,24},{24,0},{1,9},{9,17},{17,25},{25,1},{2,10},{10... | collective-permute-start | bytes 1327112 | tf_op jit(solution)/shard_map/ppermute | solution.py:48
  661.0 41.5 %collective-permute-start.98 = (bf16[96,2304]{1,0:T(8,128)(2,1)S(1)}, bf16[96,2304]{1,0:T(8,128)(2,1)S(1)}, u32[]{:S(2)}, u32[]{:S(2)}) collective-permute-start(bf16[96,2304]{1,0:T(8,128)(2,1)S(1)} %get-tuple-element.45), channel_id=1, source_target_pairs={{0,16},{8,24},{16,0},{24,8},{1,17},{9,25},{17,1},{25,9},{2,18},{10... | collective-permute-start | bytes 1327112 | tf_op jit(solution)/shard_map/ppermute | solution.py:48
  663.7 38.9 %collective-permute-start.99 = (bf16[96,2304]{1,0:T(8,128)(2,1)S(1)}, bf16[96,2304]{1,0:T(8,128)(2,1)S(1)}, u32[]{:S(2)}, u32[]{:S(2)}) collective-permute-start(bf16[96,2304]{1,0:T(8,128)(2,1)S(1)} %get-tuple-element.44), channel_id=1, source_target_pairs={{0,24},{8,0},{16,8},{24,16},{1,25},{9,1},{17,9},{25,17},{2,26},{10... | collective-permute-start | bytes 1327112 | tf_op jit(solution)/shard_map/ppermute | solution.py:48
  (143 other events, 2791.8 us)

commit v2 on v1

v2 whole, which is shorter than its diff:
```python
import jax
import jax.numpy as jnp
from jax import lax
from jax.experimental import pallas as pl
from jax.experimental.pallas import tpu as pltpu
from jax.sharding import PartitionSpec as P

HD = 128
EPS = 1e-06
THETA = 1000000.0
BF = jnp.bfloat16
F32 = jnp.float32


def angle_tables(positions):
    exponent = jnp.arange(HD // 2, dtype=F32) * (2.0 / HD)
    inverse = THETA ** (-exponent)
    phase_angle = positions.astype(F32)[:, None] * inverse[None, :]
    phase_angle = jnp.concatenate([phase_angle, phase_angle], axis=-1)
    return (jnp.cos(phase_angle), jnp.sin(phase_angle))


def rotary(vectors, cos_table, sin_table):
    half_width = vectors.shape[-1] // 2
    turned = jnp.concatenate([-vectors[..., half_width:], vectors[..., :half_width]], axis=-1)
    return vectors * cos_table + turned * sin_table


def rotary_back(gradient, cos_table, sin_table):
    scaled = gradient * sin_table
    half_width = gradient.shape[-1] // 2
    turned = jnp.concatenate([scaled[..., half_width:], -scaled[..., :half_width]], axis=-1)
    return gradient * cos_table + turned


def dot(left, right):
    return jnp.dot(left, right, preferred_element_type=F32)


def dot_nt(left, right):
    return lax.dot_general(left, right, (((1,), (1,)), ((), ())), preferred_element_type=F32)


def dot_tn(left, right):
    return lax.dot_general(left, right, (((0,), (0,)), ((), ())), preferred_element_type=F32)


def after(value, *earlier):
    return lax.optimization_barrier((value,) + earlier)[0]


def rotate(block, axis, distance):
    n = lax.axis_size(axis)
    return lax.ppermute(block, axis, [(i, (i + distance) % n) for i in range(n)])


def flip(block, axis, bit):
    n = lax.axis_size(axis)
    return lax.ppermute(block, axis, [(i, i ^ bit) for i in range(n)])


def pick(pieces, index):
    return lax.dynamic_index_in_dim(pieces, index, axis=0, keepdims=False)


def in_order(slots):
    n = len(slots)
    z = lax.axis_index("fsdp")
    if n <= 4:
        return jnp.stack([lax.select_n((z - b) % n, *slots) for b in range(n)])
    whole = jnp.zeros((n,) + slots[0].shape, slots[0].dtype)
    for k, slot in enumerate(slots):
        whole = lax.dynamic_update_index_in_dim(whole, slot, (z - k) % n, axis=0)
    return whole


def deal(blocks, axis):
    return lax.all_to_all(blocks, axis, 0, 0, tiled=True)


def gather_up(block, s):
    n = lax.axis_size("fsdp")
    return lax.ppermute(block, "fsdp", [(i, i + 1) for i in range(s - 1, n - 1)])


def gather_down(block, s):
    n = lax.axis_size("fsdp")
    return lax.ppermute(block, "fsdp", [(i, i - 1) for i in range(1, n - s + 1)])


def slots_of(own, ups, downs):
    n = lax.axis_size("fsdp")
    z = lax.axis_index("fsdp")
    return [own] + [jnp.where(z >= k, ups[k], downs[n - k]) for k in range(1, n)]


def sum_up(block, s):
    n = lax.axis_size("fsdp")
    return lax.ppermute(block.astype(BF), "fsdp", [(i, i + 1) for i in range(s)])


def sum_down(block, s):
    n = lax.axis_size("fsdp")
    return lax.ppermute(block.astype(BF), "fsdp", [(i, i - 1) for i in range(n - s, n)])


def chain_sum(sums, *earlier):
    n = len(sums)
    up, down = sums[1], sums[n - 1]
    if earlier:
        up, down = after(up, *earlier), after(down, *earlier)
    for s in range(1, n):
        up, down = sum_up(up, s), sum_down(down, s)
        if s < n - 1:
            up = sums[s + 1] + up.astype(F32)
            down = sums[n - s - 1] + down.astype(F32)
    return sums[0] + up.astype(F32) + down.astype(F32)


def split_x(total):
    half = total.shape[0] * 2 // lax.axis_size("ctx")
    return [total[:half]] + [
        total[start : start + half].astype(BF) for start in range(half, total.shape[0], half)
    ]


def join_x(parts, *earlier):
    total = parts[0]
    order = [0]
    bit = lax.axis_size("ctx") // 2
    while bit > 1:
        order = order + [j ^ bit for j in order]
        bit //= 2
    moved = [flip(part, "ctx", j) for part, j in zip(parts[1:], order[1:], strict=True)]
    if earlier:
        moved = [after(part, *earlier) for part in moved]
    for part in moved:
        total = total + part.astype(F32)
    return total


def hidden_kernel(blocks, x_ref, g_ref, *refs):
    pairs, downs = refs[:blocks], refs[blocks : 2 * blocks]
    act_ref, grad_ref, pair_ref, down_ref = refs[2 * blocks :]
    block, tile = downs[0].shape
    for b in range(blocks):
        pair_ref[b * block : (b + 1) * block, :] = pairs[b][...]
        down_ref[b * block : (b + 1) * block, :] = downs[b][...]
    chunk = min(512, x_ref.shape[0])
    for start in range(0, x_ref.shape[0], chunk):
        here = pl.ds(start, chunk)
        both = dot(x_ref[here, :], pair_ref[...])
        grad = dot(g_ref[here, :], down_ref[...])
        gate, upward = both[:, :tile], both[:, tile:]
        sigma = 1.0 / (1.0 + jnp.exp(-gate))
        silu = gate * sigma
        act_ref[here, :] = (silu * upward).astype(BF)
        grad_ref[here, :tile] = (grad * upward * sigma * (1.0 + gate * (1.0 - sigma))).astype(BF)
        grad_ref[here, tile:] = (grad * silu).astype(BF)


def hidden_pass(x, g, pairs, downs, tile):
    count, width = x.shape
    block, piece = downs[0].shape
    rows = min(1024, count)
    token = pl.BlockSpec((rows, width), lambda t, r: (r, 0))
    pair = pl.BlockSpec((block, 2 * tile), lambda t, r: (0, t))
    down = pl.BlockSpec((block, tile), lambda t, r: (0, t))
    return pl.pallas_call(
        lambda *refs: hidden_kernel(len(pairs), *refs),
        grid=(piece // tile, count // rows),
        in_specs=[token, token] + [pair] * len(pairs) + [down] * len(downs),
        out_specs=[
            pl.BlockSpec((rows, tile), lambda t, r: (r, t)),
            pl.BlockSpec((rows, 2 * tile), lambda t, r: (r, t)),
            pl.BlockSpec((width, 2 * tile), lambda t, r: (0, t)),
            pl.BlockSpec((width, tile), lambda t, r: (0, t)),
        ],
        out_shape=[
            jax.ShapeDtypeStruct((count, piece), BF),
            jax.ShapeDtypeStruct((count, 2 * piece), BF),
            jax.ShapeDtypeStruct((width, 2 * piece), BF),
            jax.ShapeDtypeStruct((width, piece), BF),
        ],
        compiler_params=pltpu.CompilerParams(vmem_limit_bytes=58 * 2**20),
        cost_estimate=pl.CostEstimate(
            flops=6 * count * width * piece,
            bytes_accessed=2 * (2 * count * width + 6 * width * piece + 3 * count * piece),
            transcendentals=count * piece,
        ),
    )(x, g, *pairs, *downs)


def add_z(total, *earlier):
    n = lax.axis_size("fsdp")
    if earlier:
        total = after(total, *earlier)
    parts = deal(total.astype(BF).reshape(n, total.shape[0] // n, total.shape[1]), "fsdp")
    return jnp.sum(parts.astype(F32), axis=0)


def sum_everywhere(vector, axes):
    for axis in axes:
        bit = 1
        while bit < lax.axis_size(axis):
            vector = vector + flip(vector, axis, bit)
            bit *= 2
    return vector


def body(
    tokens,
    cotangent,
    norm_in,
    w_qkv,
    b_qkv,
    w_out,
    norm_mid,
    w_gate_up,
    w_down,
    segments,
    positions,
):
    n, ctx_size = lax.axis_size("fsdp"), lax.axis_size("ctx")
    z, ctx, y = lax.axis_index("fsdp"), lax.axis_index("ctx"), lax.axis_index("tp")
    count, width = tokens.shape
    h = count // 2
    rows = w_qkv.shape[1]
    heads = w_qkv.shape[3] // HD - 2
    hidden = w_down.shape[2]
    piece = -(-hidden // (n * HD)) * HD
    scale = HD ** (-0.5)

    order = [0]
    bit = ctx_size // 2
    while bit:
        order = order + [j ^ bit for j in order]
        bit //= 2

    def one_hot():
        at = jnp.arange(width, dtype=jnp.int32)
        block = sum(jnp.where(at // (n * rows) == b, ctx ^ j, 0) for b, j in enumerate(order))
        layer = (at // rows) % n
        source = (layer * ctx_size + block) * rows + at % rows
        return (jnp.arange(width, dtype=jnp.int32)[:, None] == source[None, :]).astype(BF)

    def to_relative(values):
        parts = values.reshape(values.shape[0], n, ctx_size, rows)
        picked = [
            lax.dynamic_index_in_dim(parts, ctx ^ j, axis=2, keepdims=False) for j in order
        ]
        return jnp.stack(picked, axis=1).reshape(values.shape)

    def to_natural(values):
        parts = values.reshape(values.shape[0], ctx_size, n, rows)
        where = [order.index(j) for j in range(ctx_size)]
        stacked = jnp.stack([parts[:, place] for place in where], axis=1)
        natural = [
            lax.dynamic_index_in_dim(stacked, ctx ^ j, axis=1, keepdims=False)
            for j in range(ctx_size)
        ]
        return jnp.stack(natural, axis=2).reshape(values.shape)

    def own_half(values):
        return lax.dynamic_slice_in_dim(values, y * h, h, axis=0)

    def other_half(values):
        return lax.dynamic_slice_in_dim(values, (1 - y) * h, h, axis=0)

    def both_halves(own):
        other = flip(own, "tp", 1)
        return jnp.where(
            y == 0, jnp.concatenate([own, other], axis=0), jnp.concatenate([other, own], axis=0)
        )

    half_d = width // 2
    qkv_whole = lax.all_gather(w_qkv[0].reshape(rows, -1), ("fsdp", "ctx"), axis=0, tiled=True)
    out_slots = [w_out[0]] + [rotate(w_out[0], "fsdp", k) for k in range(1, n)]

    x0 = tokens.astype(F32)
    inverse_one = lax.rsqrt(jnp.mean(x0 * x0, axis=-1, keepdims=True) + EPS)
    normed_one = (x0 * inverse_one * norm_in).astype(BF)
    place = one_hot()
    placed = dot(jnp.concatenate([own_half(tokens), cotangent, normed_one]), place)
    x0_half, grad_in = placed[:h], placed[h : h + count].astype(BF)
    normed_placed = placed[h + count :].astype(BF)
    grad_half = own_half(grad_in)
    gain_two = to_relative(norm_mid)
    cos_table, sin_table = angle_tables(positions)

    tile = 3 * HD if piece % (3 * HD) == 0 else HD
    pad = n * piece - hidden
    gate_rows = jnp.pad(w_gate_up[0, :, 0], ((0, 0), (0, pad)))
    up_rows = jnp.pad(w_gate_up[0, :, 1], ((0, 0), (0, pad)))
    down_rows = jnp.pad(w_down[0], ((0, 0), (0, pad)))
    pair_out, down_out = [], []
    for index in range(n):
        columns = []
        for start in range(index * piece, (index + 1) * piece, tile):
            columns += [gate_rows[:, start : start + tile], up_rows[:, start : start + tile]]
        pair_out.append(jnp.concatenate(columns, axis=1))
        down_out.append(down_rows[:, index * piece : (index + 1) * piece])
    pair_block = deal(jnp.stack(pair_out), "fsdp").reshape(n * rows, 2 * piece)
    down_block = deal(after(jnp.stack(down_out), pair_block), "fsdp").reshape(n * rows, piece)

    def over_x(piece_rows):
        held = [piece_rows]
        bit = ctx_size // 2
        while bit > 1:
            held = held + [flip(part, "ctx", bit) for part in held]
            bit //= 2
        return held

    def over_cores(held):
        return held + [flip(part, "ctx", 1) for part in held]

    out_a = jnp.concatenate(over_x(in_order(out_slots).reshape(n * rows, -1)))
    out_b = flip(out_a, "ctx", 1)

    project = dot(normed_one, qkv_whole)
    project = project + b_qkv[0].reshape(-1)
    project = project.reshape(count, heads + 2, HD)
    queries = rotary(project[:, :heads], cos_table[:, None], sin_table[:, None]).astype(BF)
    key_local = rotary(project[:, heads], cos_table, sin_table).astype(BF)
    value_local = project[:, heads + 1].astype(BF)
    local_pair = jnp.stack([key_local, value_local])
    pairs_all = [local_pair] + [flip(local_pair, "ctx", j) for j in range(1, ctx_size)]
    pair_x = over_x(pair_block)
    grad_natural = lax.all_gather(
        after(grad_half, project), ("fsdp", "tp"), axis=0, tiled=True
    ).reshape(n, 2, h, width)
    key_rows = jnp.concatenate([p[0] for p in pairs_all], axis=0)
    value_rows = jnp.concatenate([p[1] for p in pairs_all], axis=0)
    query_index = ctx * count + jnp.arange(count, dtype=jnp.int32)
    key_index = jnp.concatenate(
        [(ctx ^ j) * count + jnp.arange(count, dtype=jnp.int32) for j in range(ctx_size)]
    )
    first_key = query_index - positions
    allowed = (key_index[None, :] <= query_index[:, None]) & (
        key_index[None, :] >= first_key[:, None]
    )

    def attention_scores():
        scores = jnp.einsum("tgd,kd->gtk", queries, key_rows, preferred_element_type=F32) * scale
        return jnp.where(allowed[None], scores, -1e30)

    scores = attention_scores()
    peak = jnp.max(scores, axis=-1, keepdims=True)
    shifted = jnp.exp(scores - peak)
    total = jnp.sum(shifted, axis=-1, keepdims=True)
    probabilities = (shifted / total).astype(BF)
    log_total = peak + jnp.log(total)
    attended = jnp.einsum("gtk,kd->tgd", probabilities, value_rows, preferred_element_type=F32)
    attended = attended.astype(BF).reshape(count, -1)
    def features(values, weight_a, weight_b):
        return jnp.concatenate([dot_nt(values, weight_a), dot_nt(values, weight_b)], axis=1)

    branch_away = features(other_half(attended), out_a, out_b).astype(BF)
    arrived = flip(branch_away, "tp", 1)
    down_x = over_x(after(down_block, branch_away))
    branch = features(own_half(attended), out_a, out_b)
    middle = x0_half + branch + arrived.astype(F32)

    inverse_two = lax.rsqrt(jnp.mean(middle * middle, axis=-1, keepdims=True) + EPS)
    normed_two = (middle * inverse_two * gain_two).astype(BF)
    ups, downs = {}, {}
    up = down = normed_two
    away_own = flip(normed_two, "tp", 1)
    swapped = []
    for step in range(1, n):
        up, down = gather_up(up, step), gather_down(down, step)
        ups[step], downs[step] = up, down
        if n == 4:
            if step == 1:
                passed = jnp.where(z == 0, down, up)
            if step == 2:
                passed = jnp.where(z == 0, down, jnp.where(z == 3, up, downs[1]))
            if step == 3:
                passed = jnp.where(
                    z == 0, down, jnp.where(z == 3, up, jnp.where(z == 1, downs[2], ups[2]))
                )
            swapped.append(flip(passed, "tp", 1))
    own_slots = slots_of(normed_two, ups, downs)
    if n == 4:
        one, two, three = swapped
        away_slots = [
            away_own,
            jnp.where(z == 0, three, one),
            jnp.where((z == 0) | (z == 3), two, three),
            jnp.where(z == 0, one, jnp.where(z == 3, three, two)),
        ]
    else:
        away_slots = [away_own] + [flip(slot, "tp", 1) for slot in own_slots[1:]]
    normed_all = jnp.concatenate(own_slots + away_slots)
    grad_slots = [pick(grad_natural, (z - k) % n) for k in range(n)]
    grad_all = jnp.concatenate(
        [pick(slot, y) for slot in grad_slots] + [pick(slot, 1 - y) for slot in grad_slots]
    )
    pair_blocks = over_cores(pair_x)
    down_blocks = over_cores(down_x)
    activated, grad_pair, pair_whole, down_whole = hidden_pass(
        normed_all, grad_all, pair_blocks, down_blocks, tile
    )

    own_tokens = n * h
    away = dot_nt(grad_pair[own_tokens:], pair_whole).astype(BF).reshape(n, h, width)
    low = z < n // 2
    early = jnp.where(low, 1, n - 1)
    if n == 4:
        y_early = flip(pick(away, early), "tp", 1)
        y_mid = flip(after(away[2], y_early), "tp", 1)
        y_late = flip(after(pick(away, n - early), y_mid), "tp", 1)
        y_own = flip(after(away[0], y_late), "tp", 1)
        crossed = [y_own, jnp.where(low, y_early, y_late), y_mid, jnp.where(low, y_late, y_early)]
    else:
        crossed = [flip(away[k], "tp", 1) for k in range(n)]
        y_early = y_mid = y_late = y_own = crossed[0]
    kept = dot_nt(grad_pair[:own_tokens], pair_whole).reshape(n, h, width)

    def term(k):
        return kept[k] + crossed[k].astype(F32)

    def turned(left, right, part, *earlier):
        columns = left[:, half_d:] if part else left[:, :half_d]
        if earlier:
            columns = after(columns, *earlier)
        return dot_tn(columns, right)

    down_core = flip(turned(grad_all, activated, 1, away).astype(BF), "ctx", 1)
    pair_core = flip(turned(normed_all, grad_pair, 1, away).astype(BF), "ctx", 1)
    down_kept = turned(grad_all, activated, 0, y_early)
    pair_kept = turned(normed_all, grad_pair, 0, y_early)
    down_total = split_x(after(down_kept, y_mid) + down_core.astype(F32))
    pair_total = split_x(after(pair_kept, y_mid) + pair_core.astype(F32))
    act_late = after(activated, *pair_total)
    result_away = dot_nt(act_late[own_tokens:], down_whole).astype(BF)

    if n == 4:
        up = sum_up(kept[1] + y_early.astype(F32), 1)
        down = sum_down(kept[3] + y_early.astype(F32), 1)
        up, down = up.astype(F32) + term(2), down.astype(F32) + term(2)
        up, down = sum_up(up, 2), sum_down(down, 2)
        up, down = up.astype(F32) + term(3), down.astype(F32) + term(1)
        up, down = after(up, *down_total, *pair_total), after(down, *down_total, *pair_total)
        up, down = sum_up(up, 3), sum_down(down, 3)
        grad_normed_two = term(0) + up.astype(F32) + down.astype(F32)
    else:
        grad_normed_two = chain_sum([term(k) for k in range(n)])
    result_crossed = flip(after(result_away, y_own), "tp", 1).reshape(n, h, width)

    scaled = grad_normed_two * gain_two
    gain_two_grad = jnp.sum(grad_normed_two * middle * inverse_two, axis=0)
    grad_middle = (
        inverse_two * scaled
        - middle * inverse_two**3 * jnp.mean(scaled * middle, axis=-1, keepdims=True)
        + grad_half.astype(F32)
    )
    out_in = both_halves(after(grad_middle.astype(BF), result_away))

    def deal_rows(total, *earlier):
        return deal(after(total.astype(BF), *earlier).reshape(n, rows, total.shape[1]), "fsdp")

    down_dealt = deal_rows(join_x(down_total, grad_normed_two))
    out_away = turned(out_in, attended, 1).astype(BF)
    out_core = flip(out_away, "ctx", 1)
    result_kept = dot_nt(after(activated, grad_middle)[:own_tokens], down_whole)
    result_kept = result_kept.reshape(n, h, width)
    result_sums = result_kept + result_crossed.astype(F32)

    out_in_late = after(out_in, out_away)
    grad_heads = dot(out_in_late[:, :half_d], out_a) + dot(out_in_late[:, half_d:], out_b)
    grad_heads = grad_heads.astype(BF).reshape(count, heads, HD)
    exact = jnp.exp(attention_scores() - log_total)
    grad_probs = jnp.einsum("tgd,kd->gtk", grad_heads, value_rows, preferred_element_type=F32)
    grad_scores = exact * (grad_probs - jnp.sum(exact * grad_probs, axis=-1, keepdims=True))
    grad_scores = grad_scores.astype(BF)
    pair_dealt = deal_rows(join_x(pair_total, grad_heads), down_dealt)
    grad_queries = (
        jnp.einsum("gtk,kd->tgd", grad_scores, key_rows, preferred_element_type=F32) * scale
    )
    grad_key_rows = (
        jnp.einsum("gtk,tgd->kd", grad_scores, queries, preferred_element_type=F32) * scale
    )
    grad_value_rows = jnp.einsum(
        "gtk,tgd->kd", exact.astype(BF), grad_heads, preferred_element_type=F32
    )
    grad_pairs = jnp.stack([grad_key_rows, grad_value_rows]).reshape(2, ctx_size, count, HD)
    grad_kv = grad_pairs[:, 0]
    moved = [flip(grad_pairs[:, j].astype(BF), "ctx", j) for j in range(1, ctx_size)]
    out_total = turned(out_in, attended, 0, *[grad_pairs]) + out_core.astype(F32)
    out_total = split_x(out_total)
    for part in moved:
        grad_kv = grad_kv + after(part, *out_total).astype(F32)
    result_rows = jnp.stack([pick(result_sums, (z - b) % n) for b in range(n)]).astype(BF)
    result_terms = deal(after(result_rows, pair_dealt), "fsdp")
    residual = (middle + jnp.sum(result_terms.astype(F32), axis=0)).astype(BF)
    grad_project = (
        jnp.concatenate(
            [
                rotary_back(grad_queries, cos_table[:, None], sin_table[:, None]),
                rotary_back(grad_kv[0], cos_table, sin_table)[:, None],
                grad_kv[1][:, None],
            ],
            axis=1,
        )
        .astype(BF)
        .reshape(count, -1)
    )
    qkv_away = turned(normed_placed, grad_project, 1).astype(BF)
    qkv_core = flip(qkv_away, "ctx", 1)
    qkv_kept = turned(normed_placed, grad_project, 0, qkv_away)
    partial_one = dot_nt(after(grad_project, qkv_kept), qkv_whole).astype(BF)
    arrived_one = flip(partial_one, "tp", 1)
    qkv_total = split_x(qkv_kept + qkv_core.astype(F32))
    out_grad = add_z(join_x(out_total), result_terms)
    qkv_joined = join_x(qkv_total)
    if n == 4:
        qkv_parts = qkv_joined.reshape(n, rows, -1)
        qkv_grad = pick(qkv_parts, z)
        for k in range(1, n):
            sent = pick(qkv_parts, (z + k) % n).astype(BF)
            qkv_grad = qkv_grad + rotate(sent, "fsdp", k).astype(F32)
    else:
        qkv_grad = add_z(qkv_joined)
    arrived_one = after(arrived_one, *qkv_total)
    output = dot_nt(both_halves(residual), place).astype(BF)

    bias_grad = jnp.sum(grad_project, axis=0, dtype=F32)
    grad_normed_one = partial_one.astype(F32) + arrived_one.astype(F32)
    scaled = grad_normed_one * norm_in
    gain_one_grad = jnp.sum(grad_normed_one * x0 * inverse_one, axis=0)
    grad_tokens = (
        inverse_one * scaled
        - x0 * inverse_one**3 * jnp.mean(scaled * x0, axis=-1, keepdims=True)
        + dot_nt(out_in, place)
    )

    def natural_columns(parts):
        whole = jnp.concatenate([parts[b] for b in range(n)], axis=1)
        return whole[:, :hidden].astype(F32)

    def every_second(parts, which):
        return jnp.concatenate(
            [
                parts[:, :, s : s + tile]
                for s in range(which * tile, 2 * piece, 2 * tile)
            ],
            axis=2,
        )

    down_grad = natural_columns(after(down_dealt, grad_project))
    pair_late = after(pair_dealt, grad_project)
    pair_grad = jnp.stack([natural_columns(every_second(pair_late, c)) for c in range(2)], axis=1)

    gain_two_pair = sum_everywhere(after(gain_two_grad[None], out_in), ("tp",))
    small = jnp.concatenate(
        [gain_one_grad[None], bias_grad[None], to_natural(gain_two_pair)], axis=1
    )
    small_all = sum_everywhere(small, ("ctx", "fsdp"))
    return (
        output,
        grad_tokens,
        small_all[:, :width],
        qkv_grad.reshape(1, rows, 1, -1),
        small_all[:, width:-width].reshape(1, 1, -1),
        out_grad[None],
        small_all[:, -width:],
        pair_grad[None],
        down_grad[None],
    )


def solution(mesh):
    rows = ("fsdp", "ctx")
    in_specs = (
        P(rows, None),
        P(rows, None),
        P(),
        P(None, rows, "tp", None),
        P(None, "tp", None),
        P(None, rows, "tp"),
        P(),
        P(None, rows, None, "tp"),
        P(None, rows, "tp"),
        P(rows),
        P(rows),
    )
    out_specs = (
        P(rows, None),
        P(rows, None),
        P(),
        P(None, rows, "tp", None),
        P(None, "tp", None),
        P(None, rows, "tp"),
        P(),
        P(None, rows, None, "tp"),
        P(None, rows, "tp"),
    )
    return jax.shard_map(body, mesh=mesh, in_specs=in_specs, out_specs=out_specs, check_vma=False)
```

time: 722 us -> 584 us (0.81); the launches traced: 708 us -> 580 us
  starting transfers between devices: 193 us -> 97 us
  waiting for transfers between devices: 299 us -> 258 us
  local copies, waits for them, and re-layouts: 71.6 us -> 44.7 us
  Pallas kernels: 0 us -> 20.5 us
  between operations: 3.72 us -> 16.6 us
    ppermute x24 -> x6, waiting for transfers between devices: 78 us -> 0.02 us  [rotate(): lax.ppermute(block, axis, [(i, (i + distance) % n) for i in range(n)])]
    ppermute x36 -> x12, starting transfers between devices: 88.5 us -> 25.5 us  [the longest x3 12.4 us: sum_up(): lax.ppermute(block.astype(BF), 'fsdp', [(i, i + 1) for i in range(s)])]
    ppermute x24 -> x6, starting transfers between devices: 52.3 us -> 13 us  [rotate(): lax.ppermute(block, axis, [(i, (i + distance) % n) for i in range(n)])]
    all_to_all x0 -> x6, starting transfers between devices: none -> 26.8 us  [deal(): return lax.all_to_all(blocks, axis, 0, 0, tiled=True)]
    all_gather x0 -> x2, waiting for transfers between devices: none -> 24.7 us  [the longest x1 24.7 us: body(): lax.all_gather(w_qkv[0].reshape(rows, -1), ('fsdp', 'ctx'), axis=0, tiled...]
    ppermute x45 -> x40, starting transfers between devices: 52.2 us -> 31.5 us  [flip(): return lax.ppermute(block, axis, [(i, i ^ bit) for i in range(n)])]
    pallas_call x0 -> x1, Pallas kernels: none -> 20.5 us  [hidden_pass(): pl.pallas_call(lambda *refs: hidden_kernel(len(pairs), *refs), grid=(piec...]
    dot_general x4 -> x11, matrix products: 19 us -> 37.9 us  [dot_nt(): lax.dot_general(left, right, (((1,), (1,)), ((), ())), preferred_element_...]
  transfers between devices with their start and end apart: 105 -> 66, of which waited for: 38 -> 22; matrix products, arithmetic and copies ran while one was open for 26% -> 28% of each run, Pallas kernels for 0% -> 0%
where the time goes in v2:
time: 584 us; the launch traced here: 580 us
  waiting for transfers between devices  258 us (44%)
  starting transfers between devices  97 us (17%)
  matrix products  81 us (14%)
  other arithmetic  61.9 us (11%)
  local copies, waits for them, and re-layouts  44.7 us (8%)
  Pallas kernels  20.5 us (4%)
  between operations  16.6 us (3%)
    ppermute x40, waiting for transfers between devices, flip(): return lax.ppermute(block, axis, [(i, i ^ bit) for i in range(n)])  154 us
    ppermute x3, waiting for transfers between devices, gather_down(): lax.ppermute(block, 'fsdp', [(i, i - 1) for i in range(1, n - s + 1)])  61.8 us
    dot_general x11, matrix products, dot_nt(): lax.dot_general(left, right, (((1,), (1,)), ((), ())), preferred_element_...  37.9 us
    ppermute x40, starting transfers between devices, flip(): return lax.ppermute(block, axis, [(i, i ^ bit) for i in range(n)])  31.5 us
    all_to_all x6, starting transfers between devices, deal(): return lax.all_to_all(blocks, axis, 0, 0, tiled=True)  26.8 us
    all_gather x1, waiting for transfers between devices, body(): lax.all_gather(w_qkv[0].reshape(rows, -1), ('fsdp', 'ctx'), axis=0, tiled...  24.7 us
    dot_general x8, matrix products, dot_tn(): lax.dot_general(left, right, (((0,), (0,)), ((), ())), preferred_element_...  20.5 us
    pallas_call x1, Pallas kernels, hidden_pass(): pl.pallas_call(lambda *refs: hidden_kernel(len(pairs), *refs), grid=(piec...  20.5 us
  transfers between devices with their start and end apart: 66, of which 22 were waited for; matrix products, arithmetic and copies ran while one was open for 28% of the time, Pallas kernels for 0%

profile of v2, /device:TPU:0, one launch (start us, length us, event | category | flops | bytes accessed | tf_op | source)
XLA Modules:
  0.0 579.6 jit_solution(15401868789742773650)
XLA Ops:
  7.2 3.1 collective-permute-start.3
  10.3 2.6 collective-permute-start.4
  14.3 4.8 fusion.138
  21.1 4.8 all-to-all-start
  28.2 5.2 fusion.145
  39.6 2.2 pad_maximum_fusion.4
  41.8 13.4 %collective-permute-done.6 = bf16[384,768]{1,0:T(8,128)(2,1)S(1)} collective-permute-done((bf16[384,768]{1,0:T(8,128)(2,1)S(1)}, bf16[384,768]{1,0:T(8,128)(2,1)S(1)}, u32[]{:S(2)}, u32[]{:S(2)}) %collective-permute-start.6) | collective-permute-done | bytes 589856 | tf_op jit(solution)/shard_map/ppermute | solution.py:59
  56.4 24.7 %all-gather.6.cloned.1.call-done = bf16[1,1536,1,1024]{3,1,2,0:T(8,128)(2,1)} async-done(((bf16[1,96,1,1024]{3,1,2,0:T(8,128)(2,1)}), bf16[1,1536,1,1024]{3,1,2,0:T(8,128)(2,1)}) %all-gather.6.cloned.1.call-update) | async-done | bytes 3145744 | tf_op jit(solution)/shard_map/all_gather | solution.py:277
  81.1 3.1 fusion.44
  89.8 3.3 collective-permute-done.1
  98.4 2.2 fusion.48
  104.1 4.2 all-to-all-start.1
  110.1 4.1 collective-permute-done.8
  118.5 4.6 collective-permute-start.9
  123.1 24.1 %collective-permute-done.10 = bf16[128,1536]{1,0:T(8,128)(2,1)} collective-permute-done((bf16[128,1536]{1,0:T(8,128)(2,1)}, bf16[128,1536]{1,0:T(8,128)(2,1)}, u32[]{:S(2)}, u32[]{:S(2)}) %collective-permute-start.10) | collective-permute-done | bytes 393248 | tf_op jit(solution)/shard_map/ppermute | solution.py:88
  151.8 32.3 %collective-permute-done.11 = bf16[128,1536]{1,0:T(8,128)(2,1)S(1)} collective-permute-done((bf16[128,1536]{1,0:T(8,128)(2,1)}, bf16[128,1536]{1,0:T(8,128)(2,1)S(1)}, u32[]{:S(2)}, u32[]{:S(2)}) %collective-permute-start.11) | collective-permute-done | bytes 393248 | tf_op jit(solution)/shard_map/ppermute | solution.py:88
  190.4 5.4 collective-permute-done.12
  195.9 1.8 select_dynamic-update-slice_fusion.5
  198.5 2.4 select_select_fusion
  202.9 6.1 %fusion.4 = bf16[1024,6,256]{2,0,1:T(8,128)(2,1)} fusion(f32[1024,256,6]{1,0,2:T(8,128)} %copy-done, f32[6,256]{1,0:T(8,128)S(1)} %log_add_fusion, pred[1024,256]{1,0:T(8,128)(4,1)S(1)} %copy-done.43), kind=kLoop, calls=%fused_computation.7 | loop fusion | flops 6291456 | bytes 9705472 | tf_op jit(solution)/shard_map/convert_element_type | solution.py:485
  209.1 19.8 %collective-permute-done.19.refs_3_ = bf16[384,2304]{1,0:T(8,128)(2,1)} collective-permute-done((bf16[384,2304]{1,0:T(8,128)(2,1)}, bf16[384,2304]{1,0:T(8,128)(2,1)}, u32[]{:S(2)}, u32[]{:S(2)}) %collective-permute-start.19) | collective-permute-done | bytes 1769504 | tf_op jit(solution)/shard_map/ppermute | solution.py:59
  229.4 14.2 %collective-permute-done.22.refs_7_ = bf16[384,1152]{1,0:T(8,128)(2,1)} collective-permute-done((bf16[384,1152]{1,0:T(8,128)(2,1)}, bf16[384,1152]{1,0:T(8,128)(2,1)}, u32[]{:S(2)}, u32[]{:S(2)}) %collective-permute-start.22) | collective-permute-done | bytes 884768 | tf_op jit(solution)/shard_map/ppermute | solution.py:59
  244.2 10.9 %collective-permute-done.18 = bf16[128,1536]{1,0:T(8,128)(2,1)S(1)} collective-permute-done((bf16[128,1536]{1,0:T(8,128)(2,1)S(1)}, bf16[128,1536]{1,0:T(8,128)(2,1)S(1)}, u32[]{:S(2)}, u32[]{:S(2)}) %collective-permute-start.18) | collective-permute-done | bytes 393248 | tf_op jit(solution)/shard_map/ppermute | solution.py:59
  257.1 1.9 fusion.136
  265.6 20.5 %shard_map.169 = (bf16[1024,1152]{1,0:T(8,128)(2,1)}, bf16[1024,2304]{1,0:T(8,128)(2,1)}, bf16[1536,2304]{1,0:T(8,128)(2,1)}, bf16[1536,1152]{1,0:T(8,128)(2,1)}) custom-call(bf16[1024,1536]{1,0:T(8,128)(2,1)} %copy-done.17, bf16[1024,1536]{1,0:T(8,128)(2,1)} %copy-done.18, bf16[384,2304]{1,0:T(8,128)(2,1)} %bitcast.46.refs_2_, ...), custom_call_target="tpu_custom_call" | custom-call | flops 10871635968 | bytes 34603008 | tf_op jit(solution)/shard_map/pallas_call | solution.py:169
  286.0 7.7 %convolution_convert_fusion.3 = bf16[512,1536]{1,0:T(8,128)(2,1)S(1)} fusion(bf16[1536,2304]{1,0:T(8,128)(2,1)} %get-tuple-element.52, bf16[1024,2304]{1,0:T(8,128)(2,1)} %get-tuple-element.51), kind=kOutput, calls=%fused_computation.41 | convolution fusion | flops 3624665088 | bytes 11010048 | tf_op jit(solution)/shard_map/dot_general | solution.py:41
  293.8 6.2 %fusion.24 = f32[512,1536]{1,0:T(8,128)S(1)} fusion(bf16[1536,2304]{1,0:T(8,128)(2,1)} %get-tuple-element.52, bf16[1024,2304]{1,0:T(8,128)(2,1)S(1)} %copy-done.88), kind=kOutput, calls=%fused_computation.47 | convolution fusion | flops 3623878656 | bytes 12582912 | tf_op jit(solution)/shard_map/dot_general | solution.py:41
  300.1 2.3 convolution_convert_fusion.1
  302.8 4.1 convolution_convert_fusion
  308.1 6.0 %collective-permute-done.25 = bf16[128,1536]{1,0:T(8,128)(2,1)S(1)} collective-permute-done((bf16[128,1536]{1,0:T(8,128)(2,1)S(1)}, bf16[128,1536]{1,0:T(8,128)(2,1)S(1)}, u32[]{:S(2)}, u32[]{:S(2)}) %collective-permute-start.25) | collective-permute-done | bytes 393248 | tf_op jit(solution)/shard_map/ppermute | solution.py:59
  314.5 5.0 collective-permute-start.29
  320.3 6.1 %fusion.147 = f32[768,2304]{1,0:T(8,128)} fusion(bf16[1024,768]{1,0:T(8,128)(2,1)S(1)} %copy-done.36, bf16[1024,2304]{1,0:T(8,128)(2,1)S(1)} %copy-done.88), kind=kOutput, calls=%fused_computation.375 | convolution fusion | flops 3623878656 | bytes 13369344 | tf_op jit(solution)/shard_map/dot_general | solution.py:45
  327.7 4.4 collective-permute-start.30
  334.6 2.3 fusion.146
  336.9 5.2 collective-permute-done.27
  347.0 4.7 convert_add_fusion
  353.7 2.9 collective-permute-start.33
  357.9 5.4 convolution_convert_fusion.2
  363.9 2.7 collective-permute-done.36
  366.6 2.0 multiply_reduce_fusion
  370.4 4.4 all-to-all-start.2
  375.5 29.3 %collective-permute-done.39 = bf16[128,1536]{1,0:T(8,128)(2,1)S(1)} collective-permute-done((bf16[128,1536]{1,0:T(8,128)(2,1)S(1)}, bf16[128,1536]{1,0:T(8,128)(2,1)S(1)}, u32[]{:S(2)}, u32[]{:S(2)}) %collective-permute-start.39) | collective-permute-done | bytes 393248 | tf_op jit(solution)/shard_map/ppermute | solution.py:59
  407.9 5.6 fusion.5
  418.5 1.9 fusion.148
  422.8 6.4 %convolution_add_fusion = bf16[512,1536]{1,0:T(8,128)(2,1)} fusion(bf16[1536,1152]{1,0:T(8,128)(2,1)} %get-tuple-element.65, bf16[512,1536]{1,0:T(8,128)(2,1)} %collective-permute-done.37, bf16[1024,1152]{1,0:T(8,128)(2,1)} %get-tuple-element.64), kind=kOutput, calls=%fused_computation.27 | convolution fusion | flops 1814298624 | bytes 7864320 | tf_op jit(solution)/shard_map/dot_general | solution.py:41
  434.6 3.1 add_convert_fusion
  437.7 5.4 all-to-all-start.3
  443.1 6.5 %collective-permute-done.57 = bf16[384,768]{1,0:T(8,128)(2,1)} collective-permute-done((bf16[384,768]{1,0:T(8,128)(2,1)}, bf16[384,768]{1,0:T(8,128)(2,1)}, u32[]{:S(2)}, u32[]{:S(2)}) %collective-permute-start.57) | collective-permute-done | bytes 589856 | tf_op jit(solution)/shard_map/ppermute | solution.py:59
  449.6 2.4 convert_add_fusion.6
  456.7 2.5 broadcast_multiply_fusion
  470.8 1.9 fusion.19
  473.6 12.2 %all-to-all-done.3 = bf16[4,96,2304]{2,1,0:T(8,128)(2,1)} async-done(((bf16[4,96,2304]{2,1,0:T(8,128)(2,1)}), bf16[4,96,2304]{2,1,0:T(8,128)(2,1)}, u32[]{:S(2)}, u32[]{:S(2)}) %all-to-all-start.3) | async-done | bytes 1769504 | tf_op jit(solution)/shard_map/all_to_all | solution.py:78
  488.1 4.4 copy.57
  492.5 4.5 all-to-all-start.4
  497.0 2.2 fusion.39
  502.2 1.9 collective-permute-start.54
  504.1 2.4 collective-permute-start.55
  508.9 27.2 %collective-permute-done.51 = f32[1,4096]{1,0:T(1,128)S(1)} collective-permute-done((f32[1,4096]{1,0:T(1,128)S(1)}, f32[1,4096]{1,0:T(1,128)S(1)}, u32[]{:S(2)}, u32[]{:S(2)}) %collective-permute-start.51) | collective-permute-done | bytes 16416 | tf_op jit(solution)/shard_map/ppermute | solution.py:59
  536.1 4.6 collective-permute-start.52
  540.7 4.9 fusion.18
  545.6 6.4 %collective-permute-done.52 = f32[1,4096]{1,0:T(1,128)S(1)} collective-permute-done((f32[1,4096]{1,0:T(1,128)S(1)}, f32[1,4096]{1,0:T(1,128)S(1)}, u32[]{:S(2)}, u32[]{:S(2)}) %collective-permute-start.52) | collective-permute-done | bytes 16416 | tf_op jit(solution)/shard_map/ppermute | solution.py:59
  552.7 3.5 all-to-all-start.5
  561.6 6.5 %collective-permute-done.41 = bf16[128,1536]{1,0:T(8,128)(2,1)S(1)} collective-permute-done((bf16[128,1536]{1,0:T(8,128)(2,1)S(1)}, bf16[128,1536]{1,0:T(8,128)(2,1)S(1)}, u32[]{:S(2)}, u32[]{:S(2)}) %collective-permute-start.41) | collective-permute-done | bytes 393248 | tf_op jit(solution)/shard_map/ppermute | solution.py:59
  568.1 3.1 fusion.22
  (437 shorter events, 121.0 us)
Async XLA Ops:
  7.2 73.9 %all-gather.6.cloned.1.call-start = ((), (), s32[]{:S(2)}) async-start(), calls=%async_computation.7 | async-start | bytes 3342336 | tf_op jit(solution)/shard_map/all_gather | solution.py:277
  7.2 28.2 %collective-permute-start.3 = (bf16[96,768]{1,0:T(8,128)(2,1)}, bf16[96,768]{1,0:T(8,128)(2,1)S(1)}, u32[]{:S(2)}, u32[]{:S(2)}) collective-permute-start(bf16[96,768]{1,0:T(8,128)(2,1)} %bitcast.342), channel_id=1, source_target_pairs={{0,8},{8,16},{16,24},{24,0},{1,9},{9,17},{17,25},{25,1},{2,10},{10... | collective-permute-start | bytes 442376 | tf_op jit(solution)/shard_map/ppermute | solution.py:54
  10.3 25.1 %collective-permute-start.4 = (bf16[96,768]{1,0:T(8,128)(2,1)}, bf16[96,768]{1,0:T(8,128)(2,1)}, u32[]{:S(2)}, u32[]{:S(2)}) collective-permute-start(bf16[96,768]{1,0:T(8,128)(2,1)} %bitcast.343), channel_id=1, source_target_pairs={{0,16},{8,24},{16,0},{24,8},{1,17},{9,25},{17,1},{25,9},{2,18},{10... | collective-permute-start | bytes 442376 | tf_op jit(solution)/shard_map/ppermute | solution.py:54
  12.9 23.2 %collective-permute-start.5 = (bf16[96,768]{1,0:T(8,128)(2,1)}, bf16[96,768]{1,0:T(8,128)(2,1)}, u32[]{:S(2)}, u32[]{:S(2)}) collective-permute-start(bf16[96,768]{1,0:T(8,128)(2,1)} %bitcast.344), channel_id=1, source_target_pairs={{0,24},{8,0},{16,8},{24,16},{1,25},{9,1},{17,9},{25,17},{2,26},{10... | collective-permute-start | bytes 442376 | tf_op jit(solution)/shard_map/ppermute | solution.py:54
  21.1 83.0 %all-to-all-start = ((bf16[4,96,2304]{2,1,0:T(8,128)(2,1)}), bf16[4,96,2304]{2,1,0:T(8,128)(2,1)}, u32[]{:S(2)}, u32[]{:S(2)}) async-start(bf16[4,96,2304]{2,1,0:T(8,128)(2,1)} %pad_maximum_fusion), calls=%async_computation | async-start | bytes 3538944 | tf_op jit(solution)/shard_map/all_to_all | solution.py:78
  37.3 18.0 %collective-permute-start.6 = (bf16[384,768]{1,0:T(8,128)(2,1)S(1)}, bf16[384,768]{1,0:T(8,128)(2,1)S(1)}, u32[]{:S(2)}, u32[]{:S(2)}) collective-permute-start(bf16[384,768]{1,0:T(8,128)(2,1)S(1)} %bitcast.329), channel_id=1, source_target_pairs={{0,4},{2,6},{4,0},{6,2},{1,5},{3,7},{5,1},{7,3},{8,12},{10,14},{12... | collective-permute-start | bytes 1769480 | tf_op jit(solution)/shard_map/ppermute | solution.py:59
  56.4 44.8 %collective-permute-start.7 = (bf16[768,768]{1,0:T(8,128)(2,1)}, bf16[768,768]{1,0:T(8,128)(2,1)S(1)}, u32[]{:S(2)}, u32[]{:S(2)}) collective-permute-start(bf16[768,768]{1,0:T(8,128)(2,1)} %pad_maximum_fusion.3), channel_id=1, source_target_pairs={{0,2},{2,0},{4,6},{6,4},{1,3},{3,1},{5,7},{7,5},{8,10},{10,8},{12,... | collective-permute-start | bytes 3538952 | tf_op jit(solution)/shard_map/ppermute | solution.py:59
  86.7 6.3 %collective-permute-start.1 = (bf16[2,256,128]{2,1,0:T(8,128)(2,1)S(1)}, bf16[2,256,128]{2,1,0:T(8,128)(2,1)S(1)}, u32[]{:S(2)}, u32[]{:S(2)}) collective-permute-start(bf16[2,256,128]{2,1,0:T(8,128)(2,1)S(1)} %pad_maximum_fusion.19), channel_id=1, source_target_pairs={{0,4},{2,6},{4,0},{6,2},{1,5},{3,7},{5,1},{7,3},{8,12},{10,14},{12... | collective-permute-start | bytes 393224 | tf_op jit(solution)/shard_map/ppermute | solution.py:59
  88.2 6.3 %collective-permute-start.2 = (bf16[2,256,128]{2,1,0:T(8,128)(2,1)S(1)}, bf16[2,256,128]{2,1,0:T(8,128)(2,1)S(1)}, u32[]{:S(2)}, u32[]{:S(2)}) collective-permute-start(bf16[2,256,128]{2,1,0:T(8,128)(2,1)S(1)} %pad_maximum_fusion.19), channel_id=1, source_target_pairs={{0,6},{2,4},{4,2},{6,0},{1,7},{3,5},{5,3},{7,1},{8,14},{10,12},{12... | collective-permute-start | bytes 393224 | tf_op jit(solution)/shard_map/ppermute | solution.py:59
  102.5 11.7 %collective-permute-start.8 = (bf16[128,1536]{1,0:T(8,128)(2,1)}, bf16[128,1536]{1,0:T(8,128)(2,1)S(1)}, u32[]{:S(2)}, u32[]{:S(2)}) collective-permute-start(bf16[128,1536]{1,0:T(8,128)(2,1)} %pad_maximum_fusion.17), channel_id=1, source_target_pairs={{0,1},{1,0},{2,3},{3,2},{4,5},{5,4},{6,7},{7,6},{8,9},{9,8},{10,11... | collective-permute-start | bytes 1179656 | tf_op jit(solution)/shard_map/ppermute | solution.py:59
  104.1 84.4 %all-to-all-start.1 = ((bf16[4,96,1152]{2,1,0:T(8,128)(2,1)}), bf16[4,96,1152]{2,1,0:T(8,128)(2,1)}, u32[]{:S(2)}, u32[]{:S(2)}) async-start(bf16[4,96,1152]{2,1,0:T(8,128)(2,1)} %pad_maximum_fusion.4), calls=%async_computation.1 | async-start | bytes 1769472 | tf_op jit(solution)/shard_map/all_to_all | solution.py:78
  108.3 150.6 %all-gather.4.cloned.1.call-start = ((), (), s32[]{:S(2)}) async-start(), calls=%async_computation.6 | async-start | bytes 3538944 | tf_op jit(solution)/shard_map/all_gather | solution.py:329
  117.2 30.0 %collective-permute-start.10 = (bf16[128,1536]{1,0:T(8,128)(2,1)}, bf16[128,1536]{1,0:T(8,128)(2,1)}, u32[]{:S(2)}, u32[]{:S(2)}) collective-permute-start(bf16[128,1536]{1,0:T(8,128)(2,1)} %get-tuple-element.102), channel_id=1, source_target_pairs={{8,0},{16,8},{24,16},{9,1},{17,9},{25,17},{10,2},{18,10},{26,18},{... | collective-permute-start | bytes 1179656 | tf_op jit(solution)/shard_map/ppermute | solution.py:88
  118.5 31.9 %collective-permute-start.9 = (bf16[128,1536]{1,0:T(8,128)(2,1)}, bf16[128,1536]{1,0:T(8,128)(2,1)S(1)}, u32[]{:S(2)}, u32[]{:S(2)}) collective-permute-start(bf16[128,1536]{1,0:T(8,128)(2,1)} %get-tuple-element.102), channel_id=1, source_target_pairs={{0,8},{8,16},{16,24},{1,9},{9,17},{17,25},{2,10},{10,18},{18,26},{... | collective-permute-start | bytes 1179656 | tf_op jit(solution)/shard_map/ppermute | solution.py:83
  147.2 36.8 %collective-permute-start.11 = (bf16[128,1536]{1,0:T(8,128)(2,1)}, bf16[128,1536]{1,0:T(8,128)(2,1)S(1)}, u32[]{:S(2)}, u32[]{:S(2)}) collective-permute-start(bf16[128,1536]{1,0:T(8,128)(2,1)} %collective-permute-done.10), channel_id=1, source_target_pairs={{8,0},{16,8},{9,1},{17,9},{10,2},{18,10},{11,3},{19,11},{12,4},{20... | collective-permute-start | bytes 1179656 | tf_op jit(solution)/shard_map/ppermute | solution.py:88
  150.4 39.4 %collective-permute-start.13 = (bf16[128,1536]{1,0:T(8,128)(2,1)S(1)}, bf16[128,1536]{1,0:T(8,128)(2,1)}, u32[]{:S(2)}, u32[]{:S(2)}) collective-permute-start(bf16[128,1536]{1,0:T(8,128)(2,1)S(1)} %collective-permute-done.9), channel_id=1, source_target_pairs={{8,16},{16,24},{9,17},{17,25},{10,18},{18,26},{11,19},{19,27},{12,... | collective-permute-start | bytes 1179656 | tf_op jit(solution)/shard_map/ppermute | solution.py:83
  184.0 11.8 %collective-permute-start.12 = (bf16[128,1536]{1,0:T(8,128)(2,1)S(1)}, bf16[128,1536]{1,0:T(8,128)(2,1)}, u32[]{:S(2)}, u32[]{:S(2)}) collective-permute-start(bf16[128,1536]{1,0:T(8,128)(2,1)S(1)} %collective-permute-done.11), channel_id=1, source_target_pairs={{8,0},{9,1},{10,2},{11,3},{12,4},{13,5},{14,6},{15,7}} | collective-permute-start | bytes 1179656 | tf_op jit(solution)/shard_map/ppermute | solution.py:88
  187.0 41.9 %collective-permute-start.19 = (bf16[384,2304]{1,0:T(8,128)(2,1)}, bf16[384,2304]{1,0:T(8,128)(2,1)}, u32[]{:S(2)}, u32[]{:S(2)}) collective-permute-start(bf16[384,2304]{1,0:T(8,128)(2,1)} %bitcast.46.refs_2_), channel_id=1, source_target_pairs={{0,4},{2,6},{4,0},{6,2},{1,5},{3,7},{5,1},{7,3},{8,12},{10,14},{12... | collective-permute-start | bytes 5308424 | tf_op jit(solution)/shard_map/ppermute | solution.py:59
  188.4 55.1 %collective-permute-start.22 = (bf16[384,1152]{1,0:T(8,128)(2,1)}, bf16[384,1152]{1,0:T(8,128)(2,1)}, u32[]{:S(2)}, u32[]{:S(2)}) collective-permute-start(bf16[384,1152]{1,0:T(8,128)(2,1)} %bitcast.52.refs_6_), channel_id=1, source_target_pairs={{0,4},{2,6},{4,0},{6,2},{1,5},{3,7},{5,1},{7,3},{8,12},{10,14},{12... | collective-permute-start | bytes 2654216 | tf_op jit(solution)/shard_map/ppermute | solution.py:59
  189.7 39.1 %collective-permute-start.15 = (bf16[128,1536]{1,0:T(8,128)(2,1)}, bf16[128,1536]{1,0:T(8,128)(2,1)S(1)}, u32[]{:S(2)}, u32[]{:S(2)}) collective-permute-start(bf16[128,1536]{1,0:T(8,128)(2,1)} %get-tuple-element.102), channel_id=1, source_target_pairs={{0,1},{1,0},{2,3},{3,2},{4,5},{5,4},{6,7},{7,6},{8,9},{9,8},{10,11... | collective-permute-start | bytes 1179656 | tf_op jit(solution)/shard_map/ppermute | solution.py:59
  189.7 8.8 %collective-permute-start.14 = (bf16[128,1536]{1,0:T(8,128)(2,1)}, bf16[128,1536]{1,0:T(8,128)(2,1)S(1)}, u32[]{:S(2)}, u32[]{:S(2)}) collective-permute-start(bf16[128,1536]{1,0:T(8,128)(2,1)} %collective-permute-done.13), channel_id=1, source_target_pairs={{16,24},{17,25},{18,26},{19,27},{20,28},{21,29},{22,30},{23,31}} | collective-permute-start | bytes 1179656 | tf_op jit(solution)/shard_map/ppermute | solution.py:83
  200.9 42.6 %collective-permute-start.16 = (bf16[128,1536]{1,0:T(8,128)(2,1)S(1)}, bf16[128,1536]{1,0:T(8,128)(2,1)S(1)}, u32[]{:S(2)}, u32[]{:S(2)}) collective-permute-start(bf16[128,1536]{1,0:T(8,128)(2,1)S(1)} %get-tuple-element.187), channel_id=1, source_target_pairs={{0,1},{1,0},{2,3},{3,2},{4,5},{5,4},{6,7},{7,6},{8,9},{9,8},{10,11... | collective-permute-start | bytes 1179656 | tf_op jit(solution)/shard_map/ppermute | solution.py:59
  202.4 41.7 %collective-permute-start.17 = (bf16[128,1536]{1,0:T(8,128)(2,1)S(1)}, bf16[128,1536]{1,0:T(8,128)(2,1)S(1)}, u32[]{:S(2)}, u32[]{:S(2)}) collective-permute-start(bf16[128,1536]{1,0:T(8,128)(2,1)S(1)} %get-tuple-element.196), channel_id=1, source_target_pairs={{0,1},{1,0},{2,3},{3,2},{4,5},{5,4},{6,7},{7,6},{8,9},{9,8},{10,11... | collective-permute-start | bytes 1179656 | tf_op jit(solution)/shard_map/ppermute | solution.py:59
  228.8 36.7 %collective-permute-start.20 = (bf16[384,2304]{1,0:T(8,128)(2,1)}, bf16[384,2304]{1,0:T(8,128)(2,1)}, u32[]{:S(2)}, u32[]{:S(2)}) collective-permute-start(bf16[384,2304]{1,0:T(8,128)(2,1)} %bitcast.46.refs_2_), channel_id=1, source_target_pairs={{0,2},{2,0},{4,6},{6,4},{1,3},{3,1},{5,7},{7,5},{8,10},{10,8},{12,... | collective-permute-start | bytes 5308424 | tf_op jit(solution)/shard_map/ppermute | solution.py:59
  228.8 36.7 %collective-permute-start.21 = (bf16[384,2304]{1,0:T(8,128)(2,1)}, bf16[384,2304]{1,0:T(8,128)(2,1)}, u32[]{:S(2)}, u32[]{:S(2)}) collective-permute-start(bf16[384,2304]{1,0:T(8,128)(2,1)} %collective-permute-done.19.refs_3_), channel_id=1, source_target_pairs={{0,2},{2,0},{4,6},{6,4},{1,3},{3,1},{5,7},{7,5},{8,10},{10,8},{12,... | collective-permute-start | bytes 5308424 | tf_op jit(solution)/shard_map/ppermute | solution.py:59
  243.5 22.0 %collective-permute-start.23 = (bf16[384,1152]{1,0:T(8,128)(2,1)}, bf16[384,1152]{1,0:T(8,128)(2,1)}, u32[]{:S(2)}, u32[]{:S(2)}) collective-permute-start(bf16[384,1152]{1,0:T(8,128)(2,1)} %bitcast.52.refs_6_), channel_id=1, source_target_pairs={{0,2},{2,0},{4,6},{6,4},{1,3},{3,1},{5,7},{7,5},{8,10},{10,8},{12,... | collective-permute-start | bytes 2654216 | tf_op jit(solution)/shard_map/ppermute | solution.py:59
  243.5 22.0 %collective-permute-start.24 = (bf16[384,1152]{1,0:T(8,128)(2,1)}, bf16[384,1152]{1,0:T(8,128)(2,1)}, u32[]{:S(2)}, u32[]{:S(2)}) collective-permute-start(bf16[384,1152]{1,0:T(8,128)(2,1)} %collective-permute-done.22.refs_7_), channel_id=1, source_target_pairs={{0,2},{2,0},{4,6},{6,4},{1,3},{3,1},{5,7},{7,5},{8,10},{10,8},{12,... | collective-permute-start | bytes 2654216 | tf_op jit(solution)/shard_map/ppermute | solution.py:59
  244.1 11.1 %collective-permute-start.18 = (bf16[128,1536]{1,0:T(8,128)(2,1)S(1)}, bf16[128,1536]{1,0:T(8,128)(2,1)S(1)}, u32[]{:S(2)}, u32[]{:S(2)}) collective-permute-start(bf16[128,1536]{1,0:T(8,128)(2,1)S(1)} %get-tuple-element.186), channel_id=1, source_target_pairs={{0,1},{1,0},{2,3},{3,2},{4,5},{5,4},{6,7},{7,6},{8,9},{9,8},{10,11... | collective-permute-start | bytes 1179656 | tf_op jit(solution)/shard_map/ppermute | solution.py:59
  302.3 41.8 %collective-permute-start.31 = (bf16[768,1152]{1,0:T(8,128)(2,1)S(1)}, bf16[768,1152]{1,0:T(8,128)(2,1)S(1)}, u32[]{:S(2)}, u32[]{:S(2)}) collective-permute-start(bf16[768,1152]{1,0:T(8,128)(2,1)S(1)} %convolution_convert_fusion.1), channel_id=1, source_target_pairs={{0,2},{2,0},{4,6},{6,4},{1,3},{3,1},{5,7},{7,5},{8,10},{10,8},{12,... | collective-permute-start | bytes 5308424 | tf_op jit(solution)/shard_map/ppermute | solution.py:59
  302.5 11.6 %collective-permute-start.25 = (bf16[128,1536]{1,0:T(8,128)(2,1)S(1)}, bf16[128,1536]{1,0:T(8,128)(2,1)S(1)}, u32[]{:S(2)}, u32[]{:S(2)}) collective-permute-start(bf16[128,1536]{1,0:T(8,128)(2,1)S(1)} %get-tuple-element.137), channel_id=1, source_target_pairs={{0,1},{1,0},{2,3},{3,2},{4,5},{5,4},{6,7},{7,6},{8,9},{9,8},{10,11... | collective-permute-start | bytes 1179656 | tf_op jit(solution)/shard_map/ppermute | solution.py:59
  307.0 40.0 %collective-permute-start.32 = (bf16[768,2304]{1,0:T(8,128)(2,1)S(1)}, bf16[768,2304]{1,0:T(8,128)(2,1)}, u32[]{:S(2)}, u32[]{:S(2)}) collective-permute-start(bf16[768,2304]{1,0:T(8,128)(2,1)S(1)} %convolution_convert_fusion), channel_id=1, source_target_pairs={{0,2},{2,0},{4,6},{6,4},{1,3},{3,1},{5,7},{7,5},{8,10},{10,8},{12,... | collective-permute-start | bytes 10616840 | tf_op jit(solution)/shard_map/ppermute | solution.py:59
  314.1 12.3 %collective-permute-start.26 = (bf16[128,1536]{1,0:T(8,128)(2,1)S(1)}, bf16[128,1536]{1,0:T(8,128)(2,1)S(1)}, u32[]{:S(2)}, u32[]{:S(2)}) collective-permute-start(bf16[128,1536]{1,0:T(8,128)(2,1)S(1)} %get-tuple-element.53), channel_id=1, source_target_pairs={{0,1},{1,0},{2,3},{3,2},{4,5},{5,4},{6,7},{7,6},{8,9},{9,8},{10,11... | collective-permute-start | bytes 1179656 | tf_op jit(solution)/shard_map/ppermute | solution.py:59
  314.5 13.0 %collective-permute-start.29 = (bf16[128,1536]{1,0:T(8,128)(2,1)S(1)}, bf16[128,1536]{1,0:T(8,128)(2,1)S(1)}, u32[]{:S(2)}, u32[]{:S(2)}) collective-permute-start(bf16[128,1536]{1,0:T(8,128)(2,1)S(1)} %get-tuple-element.111), channel_id=1, source_target_pairs={{0,8},{1,9},{2,10},{3,11},{4,12},{5,13},{6,14},{7,15}} | collective-permute-start | bytes 1179656 | tf_op jit(solution)/shard_map/ppermute | solution.py:99
  319.5 7.9 %collective-permute-start.34 = (bf16[128,1536]{1,0:T(8,128)(2,1)S(1)}, bf16[128,1536]{1,0:T(8,128)(2,1)S(1)}, u32[]{:S(2)}, u32[]{:S(2)}) collective-permute-start(bf16[128,1536]{1,0:T(8,128)(2,1)S(1)} %get-tuple-element.112), channel_id=1, source_target_pairs={{24,16},{25,17},{26,18},{27,19},{28,20},{29,21},{30,22},{31,23}} | collective-permute-start | bytes 1179656 | tf_op jit(solution)/shard_map/ppermute | solution.py:104
  327.7 16.1 %collective-permute-start.30 = (bf16[128,1536]{1,0:T(8,128)(2,1)S(1)}, bf16[128,1536]{1,0:T(8,128)(2,1)S(1)}, u32[]{:S(2)}, u32[]{:S(2)}) collective-permute-start(bf16[128,1536]{1,0:T(8,128)(2,1)S(1)} %get-tuple-element.109), channel_id=1, source_target_pairs={{0,8},{8,16},{1,9},{9,17},{2,10},{10,18},{3,11},{11,19},{4,12},{12... | collective-permute-start | bytes 1179656 | tf_op jit(solution)/shard_map/ppermute | solution.py:99
  332.1 11.7 %collective-permute-start.35 = (bf16[128,1536]{1,0:T(8,128)(2,1)S(1)}, bf16[128,1536]{1,0:T(8,128)(2,1)S(1)}, u32[]{:S(2)}, u32[]{:S(2)}) collective-permute-start(bf16[128,1536]{1,0:T(8,128)(2,1)S(1)} %get-tuple-element.110), channel_id=1, source_target_pairs={{16,8},{24,16},{17,9},{25,17},{18,10},{26,18},{19,11},{27,19},{20,... | collective-permute-start | bytes 1179656 | tf_op jit(solution)/shard_map/ppermute | solution.py:104
  332.8 9.3 %collective-permute-start.27 = (bf16[128,1536]{1,0:T(8,128)(2,1)S(1)}, bf16[128,1536]{1,0:T(8,128)(2,1)S(1)}, u32[]{:S(2)}, u32[]{:S(2)}) collective-permute-start(bf16[128,1536]{1,0:T(8,128)(2,1)S(1)} %get-tuple-element.54), channel_id=1, source_target_pairs={{0,1},{1,0},{2,3},{3,2},{4,5},{5,4},{6,7},{7,6},{8,9},{9,8},{10,11... | collective-permute-start | bytes 1179656 | tf_op jit(solution)/shard_map/ppermute | solution.py:59
  342.1 21.2 %collective-permute-start.28 = (bf16[128,1536]{1,0:T(8,128)(2,1)}, bf16[128,1536]{1,0:T(8,128)(2,1)}, u32[]{:S(2)}, u32[]{:S(2)}) collective-permute-start(bf16[128,1536]{1,0:T(8,128)(2,1)} %get-tuple-element.55), channel_id=1, source_target_pairs={{0,1},{1,0},{2,3},{3,2},{4,5},{5,4},{6,7},{7,6},{8,9},{9,8},{10,11... | collective-permute-start | bytes 1179656 | tf_op jit(solution)/shard_map/ppermute | solution.py:59
  345.5 23.8 %collective-permute-start.40 = (bf16[384,1152]{1,0:T(8,128)(2,1)}, bf16[384,1152]{1,0:T(8,128)(2,1)S(1)}, u32[]{:S(2)}, u32[]{:S(2)}) collective-permute-start(bf16[384,1152]{1,0:T(8,128)(2,1)} %fusion.134), channel_id=1, source_target_pairs={{0,4},{2,6},{4,0},{6,2},{1,5},{3,7},{5,1},{7,3},{8,12},{10,14},{12... | collective-permute-start | bytes 2654216 | tf_op jit(solution)/shard_map/ppermute | solution.py:59
  353.1 76.2 %collective-permute-start.38 = (bf16[384,2304]{1,0:T(8,128)(2,1)}, bf16[384,2304]{1,0:T(8,128)(2,1)}, u32[]{:S(2)}, u32[]{:S(2)}) collective-permute-start(bf16[384,2304]{1,0:T(8,128)(2,1)} %fusion.133), channel_id=1, source_target_pairs={{0,4},{2,6},{4,0},{6,2},{1,5},{3,7},{5,1},{7,3},{8,12},{10,14},{12... | collective-permute-start | bytes 5308424 | tf_op jit(solution)/shard_map/ppermute | solution.py:59
  353.7 10.2 %collective-permute-start.33 = (bf16[128,1536]{1,0:T(8,128)(2,1)S(1)}, bf16[128,1536]{1,0:T(8,128)(2,1)S(1)}, u32[]{:S(2)}, u32[]{:S(2)}) collective-permute-start(bf16[128,1536]{1,0:T(8,128)(2,1)S(1)} %get-tuple-element.62), channel_id=1, source_target_pairs={{0,8},{8,16},{16,24},{1,9},{9,17},{17,25},{2,10},{10,18},{18,26},{... | collective-permute-start | bytes 1179656 | tf_op jit(solution)/shard_map/ppermute | solution.py:99
  356.6 10.0 %collective-permute-start.36 = (bf16[128,1536]{1,0:T(8,128)(2,1)S(1)}, bf16[128,1536]{1,0:T(8,128)(2,1)S(1)}, u32[]{:S(2)}, u32[]{:S(2)}) collective-permute-start(bf16[128,1536]{1,0:T(8,128)(2,1)S(1)} %get-tuple-element.63), channel_id=1, source_target_pairs={{8,0},{16,8},{24,16},{9,1},{17,9},{25,17},{10,2},{18,10},{26,18},{... | collective-permute-start | bytes 1179656 | tf_op jit(solution)/shard_map/ppermute | solution.py:104
  363.3 59.3 %collective-permute-start.37 = (bf16[512,1536]{1,0:T(8,128)(2,1)}, bf16[512,1536]{1,0:T(8,128)(2,1)}, u32[]{:S(2)}, u32[]{:S(2)}) collective-permute-start(bf16[512,1536]{1,0:T(8,128)(2,1)} %convolution_convert_fusion.2), channel_id=1, source_target_pairs={{0,1},{1,0},{2,3},{3,2},{4,5},{5,4},{6,7},{7,6},{8,9},{9,8},{10,11... | collective-permute-start | bytes 4718600 | tf_op jit(solution)/shard_map/ppermute | solution.py:59
  368.9 35.8 %collective-permute-start.39 = (bf16[128,1536]{1,0:T(8,128)(2,1)S(1)}, bf16[128,1536]{1,0:T(8,128)(2,1)S(1)}, u32[]{:S(2)}, u32[]{:S(2)}) collective-permute-start(bf16[128,1536]{1,0:T(8,128)(2,1)S(1)} %convert_add_fusion.9), channel_id=1, source_target_pairs={{0,1},{1,0},{2,3},{3,2},{4,5},{5,4},{6,7},{7,6},{8,9},{9,8},{10,11... | collective-permute-start | bytes 1179656 | tf_op jit(solution)/shard_map/ppermute | solution.py:59
  370.4 67.3 %all-to-all-start.2 = ((bf16[4,96,1152]{2,1,0:T(8,128)(2,1)}), bf16[4,96,1152]{2,1,0:T(8,128)(2,1)}, u32[]{:S(2)}, u32[]{:S(2)}) async-start(bf16[4,96,1152]{2,1,0:T(8,128)(2,1)} %bitcast.58), calls=%async_computation.2 | async-start | bytes 1769472 | tf_op jit(solution)/shard_map/all_to_all | solution.py:78
  406.5 22.8 %collective-permute-start.43 = (bf16[768,768]{1,0:T(8,128)(2,1)}, bf16[768,768]{1,0:T(8,128)(2,1)}, u32[]{:S(2)}, u32[]{:S(2)}) collective-permute-start(bf16[768,768]{1,0:T(8,128)(2,1)} %convolution_convert_fusion.5), channel_id=1, source_target_pairs={{0,2},{2,0},{4,6},{6,4},{1,3},{3,1},{5,7},{7,5},{8,10},{10,8},{12,... | collective-permute-start | bytes 3538952 | tf_op jit(solution)/shard_map/ppermute | solution.py:59
  416.4 4.7 collective-permute-start.48
  420.4 31.6 %collective-permute-start.42 = (bf16[2,256,128]{2,1,0:T(8,128)(2,1)S(1)}, bf16[2,256,128]{2,1,0:T(8,128)(2,1)}, u32[]{:S(2)}, u32[]{:S(2)}) collective-permute-start(bf16[2,256,128]{2,1,0:T(8,128)(2,1)S(1)} %get-tuple-element.193), channel_id=1, source_target_pairs={{0,2},{2,0},{4,6},{6,4},{1,3},{3,1},{5,7},{7,5},{8,10},{10,8},{12,... | collective-permute-start | bytes 393224 | tf_op jit(solution)/shard_map/ppermute | solution.py:59
  421.0 31.0 %collective-permute-start.44 = (bf16[2,256,128]{2,1,0:T(8,128)(2,1)S(1)}, bf16[2,256,128]{2,1,0:T(8,128)(2,1)}, u32[]{:S(2)}, u32[]{:S(2)}) collective-permute-start(bf16[2,256,128]{2,1,0:T(8,128)(2,1)S(1)} %get-tuple-element.195), channel_id=1, source_target_pairs={{0,4},{2,6},{4,0},{6,2},{1,5},{3,7},{5,1},{7,3},{8,12},{10,14},{12... | collective-permute-start | bytes 393224 | tf_op jit(solution)/shard_map/ppermute | solution.py:59
  422.6 29.4 %collective-permute-start.45 = (bf16[2,256,128]{2,1,0:T(8,128)(2,1)S(1)}, bf16[2,256,128]{2,1,0:T(8,128)(2,1)}, u32[]{:S(2)}, u32[]{:S(2)}) collective-permute-start(bf16[2,256,128]{2,1,0:T(8,128)(2,1)S(1)} %get-tuple-element.194), channel_id=1, source_target_pairs={{0,6},{2,4},{4,2},{6,0},{1,7},{3,5},{5,3},{7,1},{8,14},{10,12},{12... | collective-permute-start | bytes 393224 | tf_op jit(solution)/shard_map/ppermute | solution.py:59
  433.1 16.5 %collective-permute-start.57 = (bf16[384,768]{1,0:T(8,128)(2,1)}, bf16[384,768]{1,0:T(8,128)(2,1)}, u32[]{:S(2)}, u32[]{:S(2)}) collective-permute-start(bf16[384,768]{1,0:T(8,128)(2,1)} %slice.706), channel_id=1, source_target_pairs={{0,4},{2,6},{4,0},{6,2},{1,5},{3,7},{5,1},{7,3},{8,12},{10,14},{12... | collective-permute-start | bytes 1769480 | tf_op jit(solution)/shard_map/ppermute | solution.py:59
  437.7 48.1 %all-to-all-start.3 = ((bf16[4,96,2304]{2,1,0:T(8,128)(2,1)}), bf16[4,96,2304]{2,1,0:T(8,128)(2,1)}, u32[]{:S(2)}, u32[]{:S(2)}) async-start(bf16[4,96,2304]{2,1,0:T(8,128)(2,1)} %bitcast.301), calls=%async_computation.3 | async-start | bytes 3538944 | tf_op jit(solution)/shard_map/all_to_all | solution.py:78
  463.4 4.4 collective-permute-start.47
  469.4 30.1 %collective-permute-start.53 = (bf16[384,1024]{1,0:T(8,128)(2,1)}, bf16[384,1024]{1,0:T(8,128)(2,1)}, u32[]{:S(2)}, u32[]{:S(2)}) collective-permute-start(bf16[384,1024]{1,0:T(8,128)(2,1)} %slice.705), channel_id=1, source_target_pairs={{0,4},{2,6},{4,0},{6,2},{1,5},{3,7},{5,1},{7,3},{8,12},{10,14},{12... | collective-permute-start | bytes 2359304 | tf_op jit(solution)/shard_map/ppermute | solution.py:59
  472.8 24.2 %collective-permute-start.46 = (bf16[256,1536]{1,0:T(8,128)(2,1)}, bf16[256,1536]{1,0:T(8,128)(2,1)}, u32[]{:S(2)}, u32[]{:S(2)}) collective-permute-start(bf16[256,1536]{1,0:T(8,128)(2,1)} %fusion.19), channel_id=1, source_target_pairs={{0,1},{1,0},{2,3},{3,2},{4,5},{5,4},{6,7},{7,6},{8,9},{9,8},{10,11... | collective-permute-start | bytes 2359304 | tf_op jit(solution)/shard_map/ppermute | solution.py:59
  492.5 60.1 %all-to-all-start.4 = ((bf16[4,128,1536]{2,1,0:T(8,128)(2,1)}), bf16[4,128,1536]{2,1,0:T(8,128)(2,1)}, u32[]{:S(2)}, u32[]{:S(2)}) async-start(bf16[4,128,1536]{2,1,0:T(8,128)(2,1)} %pad_maximum_fusion.1), calls=%async_computation.4 | async-start | bytes 3145728 | tf_op jit(solution)/shard_map/all_to_all | solution.py:78
  501.0 7.2 %collective-permute-start.50 = (f32[1,4096]{1,0:T(1,128)S(1)}, f32[1,4096]{1,0:T(1,128)S(1)}, u32[]{:S(2)}, u32[]{:S(2)}) collective-permute-start(f32[1,4096]{1,0:T(1,128)S(1)} %fusion.180), channel_id=1, source_target_pairs={{0,4},{2,6},{4,0},{6,2},{1,5},{3,7},{5,1},{7,3},{8,12},{10,14},{12... | collective-permute-start | bytes 49160 | tf_op jit(solution)/shard_map/ppermute | solution.py:59
  502.2 57.3 %collective-permute-start.54 = (bf16[96,1024]{1,0:T(8,128)(2,1)S(1)}, bf16[96,1024]{1,0:T(8,128)(2,1)S(1)}, u32[]{:S(2)}, u32[]{:S(2)}) collective-permute-start(bf16[96,1024]{1,0:T(8,128)(2,1)S(1)} %get-tuple-element.129), channel_id=1, source_target_pairs={{0,8},{8,16},{16,24},{24,0},{1,9},{9,17},{17,25},{25,1},{2,10},{10... | collective-permute-start | bytes 589832 | tf_op jit(solution)/shard_map/ppermute | solution.py:54
  504.1 55.4 %collective-permute-start.55 = (bf16[96,1024]{1,0:T(8,128)(2,1)S(1)}, bf16[96,1024]{1,0:T(8,128)(2,1)S(1)}, u32[]{:S(2)}, u32[]{:S(2)}) collective-permute-start(bf16[96,1024]{1,0:T(8,128)(2,1)S(1)} %get-tuple-element.131), channel_id=1, source_target_pairs={{0,16},{8,24},{16,0},{24,8},{1,17},{9,25},{17,1},{25,9},{2,18},{10... | collective-permute-start | bytes 589832 | tf_op jit(solution)/shard_map/ppermute | solution.py:54
  506.5 53.0 %collective-permute-start.56 = (bf16[96,1024]{1,0:T(8,128)(2,1)S(1)}, bf16[96,1024]{1,0:T(8,128)(2,1)S(1)}, u32[]{:S(2)}, u32[]{:S(2)}) collective-permute-start(bf16[96,1024]{1,0:T(8,128)(2,1)S(1)} %get-tuple-element.130), channel_id=1, source_target_pairs={{0,24},{8,0},{16,8},{24,16},{1,25},{9,1},{17,9},{25,17},{2,26},{10... | collective-permute-start | bytes 589832 | tf_op jit(solution)/shard_map/ppermute | solution.py:54
  508.2 27.8 %collective-permute-start.51 = (f32[1,4096]{1,0:T(1,128)S(1)}, f32[1,4096]{1,0:T(1,128)S(1)}, u32[]{:S(2)}, u32[]{:S(2)}) collective-permute-start(f32[1,4096]{1,0:T(1,128)S(1)} %add.522), channel_id=1, source_target_pairs={{0,8},{8,0},{16,24},{24,16},{1,9},{9,1},{17,25},{25,17},{2,10},{10... | collective-permute-start | bytes 49160 | tf_op jit(solution)/shard_map/ppermute | solution.py:59
  536.1 16.0 %collective-permute-start.52 = (f32[1,4096]{1,0:T(1,128)S(1)}, f32[1,4096]{1,0:T(1,128)S(1)}, u32[]{:S(2)}, u32[]{:S(2)}) collective-permute-start(f32[1,4096]{1,0:T(1,128)S(1)} %add.523), channel_id=1, source_target_pairs={{0,16},{8,24},{16,0},{24,8},{1,17},{9,25},{17,1},{25,9},{2,18},{10... | collective-permute-start | bytes 49160 | tf_op jit(solution)/shard_map/ppermute | solution.py:59
  552.7 18.8 %all-to-all-start.5 = ((bf16[4,96,768]{2,1,0:T(8,128)(2,1)}), bf16[4,96,768]{2,1,0:T(8,128)(2,1)S(1)}, u32[]{:S(2)}, u32[]{:S(2)}) async-start(bf16[4,96,768]{2,1,0:T(8,128)(2,1)} %bitcast.94), calls=%async_computation.5 | async-start | bytes 1179648 | tf_op jit(solution)/shard_map/all_to_all | solution.py:78
  558.0 10.1 %collective-permute-start.41 = (bf16[128,1536]{1,0:T(8,128)(2,1)S(1)}, bf16[128,1536]{1,0:T(8,128)(2,1)S(1)}, u32[]{:S(2)}, u32[]{:S(2)}) collective-permute-start(bf16[128,1536]{1,0:T(8,128)(2,1)S(1)} %add_convert_fusion.2), channel_id=1, source_target_pairs={{0,1},{1,0},{2,3},{3,2},{4,5},{5,4},{6,7},{7,6},{8,9},{9,8},{10,11... | collective-permute-start | bytes 1179656 | tf_op jit(solution)/shard_map/ppermute | solution.py:59
  (96 other events, 1344.7 us)
Sparse Core Ops, SparseCore 0:
  14.4 66.6 all-gather.5
  111.3 77.5 all-gather.3

commit v3 on v2

v3 whole, which is shorter than its diff:
```python
import jax
import jax.numpy as jnp
from jax import lax
from jax.experimental import pallas as pl
from jax.experimental.pallas import tpu as pltpu
from jax.sharding import PartitionSpec as P

HD = 128
EPS = 1e-06
THETA = 1000000.0
BF = jnp.bfloat16
F32 = jnp.float32


def angle_tables(positions):
    exponent = jnp.arange(HD // 2, dtype=F32) * (2.0 / HD)
    inverse = THETA ** (-exponent)
    phase_angle = positions.astype(F32)[:, None] * inverse[None, :]
    phase_angle = jnp.concatenate([phase_angle, phase_angle], axis=-1)
    return (jnp.cos(phase_angle), jnp.sin(phase_angle))


def rotary(vectors, cos_table, sin_table):
    half_width = vectors.shape[-1] // 2
    turned = jnp.concatenate([-vectors[..., half_width:], vectors[..., :half_width]], axis=-1)
    return vectors * cos_table + turned * sin_table


def rotary_back(gradient, cos_table, sin_table):
    scaled = gradient * sin_table
    half_width = gradient.shape[-1] // 2
    turned = jnp.concatenate([scaled[..., half_width:], -scaled[..., :half_width]], axis=-1)
    return gradient * cos_table + turned


def dot(left, right):
    return jnp.dot(left, right, preferred_element_type=F32)


def dot_nt(left, right):
    return lax.dot_general(left, right, (((1,), (1,)), ((), ())), preferred_element_type=F32)


def dot_tn(left, right):
    return lax.dot_general(left, right, (((0,), (0,)), ((), ())), preferred_element_type=F32)


def after(value, *earlier):
    return lax.optimization_barrier((value,) + earlier)[0]


def together(*values):
    return lax.optimization_barrier(values)


def segment(ready, work, *operands):
    shapes = jax.eval_shape(work, *operands)

    def skip(*operands):
        return jax.tree.map(lambda leaf: jnp.zeros(leaf.shape, leaf.dtype), shapes)

    return lax.cond(ready, work, skip, *operands)


def rotate(block, axis, distance):
    n = lax.axis_size(axis)
    return lax.ppermute(block, axis, [(i, (i + distance) % n) for i in range(n)])


def flip(block, axis, bit):
    n = lax.axis_size(axis)
    return lax.ppermute(block, axis, [(i, i ^ bit) for i in range(n)])


def pick(pieces, index):
    return lax.dynamic_index_in_dim(pieces, index, axis=0, keepdims=False)


def in_order(slots):
    n = len(slots)
    z = lax.axis_index("fsdp")
    if n <= 4:
        return jnp.stack([lax.select_n((z - b) % n, *slots) for b in range(n)])
    whole = jnp.zeros((n,) + slots[0].shape, slots[0].dtype)
    for k, slot in enumerate(slots):
        whole = lax.dynamic_update_index_in_dim(whole, slot, (z - k) % n, axis=0)
    return whole


def deal(blocks, axis):
    return lax.all_to_all(blocks, axis, 0, 0, tiled=True)


def gather_up(block, s):
    n = lax.axis_size("fsdp")
    return lax.ppermute(block, "fsdp", [(i, i + 1) for i in range(s - 1, n - 1)])


def gather_down(block, s):
    n = lax.axis_size("fsdp")
    return lax.ppermute(block, "fsdp", [(i, i - 1) for i in range(1, n - s + 1)])


def slots_of(own, ups, downs):
    n = lax.axis_size("fsdp")
    z = lax.axis_index("fsdp")
    return [own] + [jnp.where(z >= k, ups[k], downs[n - k]) for k in range(1, n)]


def sum_up(block, s):
    n = lax.axis_size("fsdp")
    return lax.ppermute(block.astype(BF), "fsdp", [(i, i + 1) for i in range(s)])


def sum_down(block, s):
    n = lax.axis_size("fsdp")
    return lax.ppermute(block.astype(BF), "fsdp", [(i, i - 1) for i in range(n - s, n)])


def chain_sum(sums, *earlier):
    n = len(sums)
    up, down = sums[1], sums[n - 1]
    if earlier:
        up, down = after(up, *earlier), after(down, *earlier)
    for s in range(1, n):
        up, down = sum_up(up, s), sum_down(down, s)
        if s < n - 1:
            up = sums[s + 1] + up.astype(F32)
            down = sums[n - s - 1] + down.astype(F32)
    return sums[0] + up.astype(F32) + down.astype(F32)


def put_rows(parts, whole):
    rows = parts[0].shape[0]
    for b, part in enumerate(parts):
        whole[b * rows : (b + 1) * rows, :] = part[...]


def hidden_step(x_ref, g_ref, pair_ref, down_ref, act_ref, grad_ref):
    tile = down_ref.shape[1]
    chunk = min(512, x_ref.shape[0])
    for start in range(0, x_ref.shape[0], chunk):
        here = pl.ds(start, chunk)
        both = dot(x_ref[here, :], pair_ref[...])
        grad = dot(g_ref[here, :], down_ref[...])
        gate, upward = both[:, :tile], both[:, tile:]
        sigma = 1.0 / (1.0 + jnp.exp(-gate))
        silu = gate * sigma
        act_ref[here, :] = (silu * upward).astype(BF)
        grad_ref[here, :tile] = (grad * upward * sigma * (1.0 + gate * (1.0 - sigma))).astype(BF)
        grad_ref[here, tile:] = (grad * silu).astype(BF)


def put_weights(parts, early, refs, pair_ref, down_ref):
    refs = list(refs)
    step = pl.program_id(0)
    for b, apart in enumerate(parts):
        down, pair = refs.pop(0), refs.pop(0)
        rows = slice(b * down.shape[0], (b + 1) * down.shape[0])
        down_ref[rows, :] = down[...]
        if not apart:
            pair_ref[rows, :] = pair[...]
            continue
        first = refs.pop(0)
        pair_ref[rows, :] = jnp.where(step < early, first[...], pair[...])


def hidden_kernel(parts, early, x_ref, g_ref, *refs):
    act_ref, grad_ref, pair_ref, down_ref = refs[-4:]
    put_weights(parts, early, refs[:-4], pair_ref, down_ref)
    hidden_step(x_ref, g_ref, pair_ref, down_ref, act_ref, grad_ref)


def hidden_kernel_four(parts, early, place_ref, *refs):
    own, ups, downs = refs[0], refs[1:4], refs[4:7]
    away_own, one, two, three, natural = refs[7:12]
    act_ref, grad_ref, pair_ref, down_ref, x_ref, g_ref, natural_ref = refs[-7:]
    z, y = place_ref[0], place_ref[1]
    h = own.shape[0]
    step = pl.program_id(0)

    def natural_rows(slot):
        index = lax.rem(z + 4 - slot % 4, 4) * 2 + lax.rem(y + slot // 4, 2)
        return pl.ds(pl.multiple_of(index * h, h), h)

    @pl.when(step == 0)
    def _():
        x_ref[:h, :] = own[...]
        for k in range(1, 4):
            x_ref[k * h : (k + 1) * h, :] = jnp.where(z >= k, ups[k - 1][...], downs[3 - k][...])
        x_ref[4 * h : 5 * h, :] = away_own[...]
        x_ref[5 * h : 6 * h, :] = jnp.where(z == 0, three[...], one[...])
        x_ref[6 * h : 7 * h, :] = jnp.where((z == 0) | (z == 3), two[...], three[...])
        last = jnp.where(z == 3, three[...], two[...])
        x_ref[7 * h :, :] = jnp.where(z == 0, one[...], last)
        for slot in range(8):
            g_ref[slot * h : (slot + 1) * h, :] = natural[natural_rows(slot), :]

    put_weights(parts, early, refs[12:-7], pair_ref, down_ref)
    hidden_step(x_ref, g_ref, pair_ref, down_ref, act_ref, grad_ref)
    for slot in range(8):
        natural_ref[natural_rows(slot), :] = act_ref[slot * h : (slot + 1) * h, :]


def hidden_pass(place, tokens, grads, blocks, early, piece, tile):
    count, width = grads.shape
    four = place is not None
    rows = count if four else min(1024, count)
    weights, weight_specs = [], []

    def at(shape, index):
        return pl.BlockSpec(shape, lambda t, r: (0, index(t)))

    for block in blocks:
        (down, d_from), (pair, p_from) = block[:2]
        depth = down.shape[0]
        base = early if len(block) > 2 else 0
        weights += [down, pair]
        weight_specs.append(at((depth, tile), lambda t, first=d_from // tile: first + t))
        weight_specs.append(
            at(
                (depth, 2 * tile),
                lambda t, first=p_from // (2 * tile), base=base: first + jnp.maximum(t - base, 0),
            )
        )
        if base:
            weights.append(block[2][0])
            weight_specs.append(
                at(
                    (depth, 2 * tile),
                    lambda t, first=block[2][1] // (2 * tile): first + jnp.minimum(t, early - 1),
                )
            )
    parts = [len(block) > 2 and early > 0 for block in blocks]
    out_specs = [
        pl.BlockSpec((rows, tile), lambda t, r: (r, t)),
        pl.BlockSpec((rows, 2 * tile), lambda t, r: (r, t)),
        pl.BlockSpec((width, 2 * tile), lambda t, r: (0, t)),
        pl.BlockSpec((width, tile), lambda t, r: (0, t)),
    ]
    out_shape = [
        jax.ShapeDtypeStruct((count, piece), BF),
        jax.ShapeDtypeStruct((count, 2 * piece), BF),
        jax.ShapeDtypeStruct((width, 2 * piece), BF),
        jax.ShapeDtypeStruct((width, piece), BF),
    ]
    if four:
        kernel, operands = hidden_kernel_four, [place] + list(tokens) + [grads]
        in_specs = [pl.BlockSpec(memory_space=pltpu.SMEM)]
        for array in operands[1:]:
            in_specs.append(
                pl.BlockSpec(array.shape, lambda t, r: (0, 0), pipeline_mode=pl.Buffered(1))
            )
        out_specs += [pl.BlockSpec((count, width), lambda t, r: (0, 0))] * 2
        out_shape += [jax.ShapeDtypeStruct((count, width), BF)] * 2
        out_specs.append(pl.BlockSpec((rows, tile), lambda t, r: (r, t)))
        out_shape.append(jax.ShapeDtypeStruct((count, piece), BF))
    else:
        kernel, operands = hidden_kernel, [tokens, grads]
        in_specs = [pl.BlockSpec((rows, width), lambda t, r: (r, 0))] * 2
    outs = pl.pallas_call(
        lambda *refs: kernel(parts, early, *refs),
        grid=(piece // tile, count // rows),
        in_specs=in_specs + weight_specs,
        out_specs=out_specs,
        out_shape=out_shape,
        compiler_params=pltpu.CompilerParams(vmem_limit_bytes=60 * 2**20),
        cost_estimate=pl.CostEstimate(
            flops=6 * count * width * piece,
            bytes_accessed=2 * (4 * count * width + 6 * width * piece + 3 * count * piece),
            transcendentals=count * piece,
        ),
    )(*operands, *weights)
    return outs if four else list(outs) + [tokens, grads, None]


def add_z(total, *earlier):
    n = lax.axis_size("fsdp")
    if earlier:
        total = after(total, *earlier)
    parts = deal(total.astype(BF).reshape(n, total.shape[0] // n, total.shape[1]), "fsdp")
    return jnp.sum(parts.astype(F32), axis=0)


def sum_everywhere(vector, axes):
    for axis in axes:
        bit = 1
        while bit < lax.axis_size(axis):
            vector = vector + flip(vector, axis, bit)
            bit *= 2
    return vector


def body(
    tokens,
    cotangent,
    norm_in,
    w_qkv,
    b_qkv,
    w_out,
    norm_mid,
    w_gate_up,
    w_down,
    segments,
    positions,
):
    n, ctx_size = lax.axis_size("fsdp"), lax.axis_size("ctx")
    z, ctx, y = lax.axis_index("fsdp"), lax.axis_index("ctx"), lax.axis_index("tp")
    count, width = tokens.shape
    h = count // 2
    rows = w_qkv.shape[1]
    heads = w_qkv.shape[3] // HD - 2
    hidden = w_down.shape[2]
    piece = -(-hidden // (n * HD)) * HD
    scale = HD ** (-0.5)

    order = [0]
    bit = ctx_size // 2
    while bit:
        order = order + [j ^ bit for j in order]
        bit //= 2

    def one_hot():
        at = jnp.arange(width, dtype=jnp.int32)
        block = sum(jnp.where(at // (n * rows) == b, ctx ^ j, 0) for b, j in enumerate(order))
        layer = (at // rows) % n
        source = (layer * ctx_size + block) * rows + at % rows
        return (jnp.arange(width, dtype=jnp.int32)[:, None] == source[None, :]).astype(BF)

    def to_relative(values):
        parts = values.reshape(values.shape[0], n, ctx_size, rows)
        picked = [
            lax.dynamic_index_in_dim(parts, ctx ^ j, axis=2, keepdims=False) for j in order
        ]
        return jnp.stack(picked, axis=1).reshape(values.shape)

    def to_natural(values):
        parts = values.reshape(values.shape[0], ctx_size, n, rows)
        where = [order.index(j) for j in range(ctx_size)]
        stacked = jnp.stack([parts[:, place] for place in where], axis=1)
        natural = [
            lax.dynamic_index_in_dim(stacked, ctx ^ j, axis=1, keepdims=False)
            for j in range(ctx_size)
        ]
        return jnp.stack(natural, axis=2).reshape(values.shape)

    def own_half(values):
        return lax.dynamic_slice_in_dim(values, y * h, h, axis=0)

    def other_half(values):
        return lax.dynamic_slice_in_dim(values, (1 - y) * h, h, axis=0)

    def both_halves(own):
        other = flip(own, "tp", 1)
        return jnp.where(
            y == 0, jnp.concatenate([own, other], axis=0), jnp.concatenate([other, own], axis=0)
        )

    half_d = width // 2
    ready = norm_in[0, 0] == norm_in[0, 0]
    qkv_whole = lax.all_gather(w_qkv[0].reshape(rows, -1), ("fsdp", "ctx"), axis=0, tiled=True)
    out_slots = [w_out[0]] + [rotate(w_out[0], "fsdp", k) for k in range(1, n)]

    tile = 3 * HD if piece % (3 * HD) == 0 else HD
    pad = n * piece - hidden

    def lay_out(w_gate_up, w_down):
        gate_rows = jnp.pad(w_gate_up[0, :, 0], ((0, 0), (0, pad)))
        up_rows = jnp.pad(w_gate_up[0, :, 1], ((0, 0), (0, pad)))
        down_rows = jnp.pad(w_down[0], ((0, 0), (0, pad)))
        pair_out, down_out = [], []
        for index in range(n):
            columns = []
            for start in range(index * piece, (index + 1) * piece, tile):
                columns += [gate_rows[:, start : start + tile], up_rows[:, start : start + tile]]
            pair_out.append(jnp.concatenate(columns, axis=1))
            down_out.append(down_rows[:, index * piece : (index + 1) * piece])
        return jnp.stack(pair_out), jnp.stack(down_out)

    pair_out, down_out = lay_out(w_gate_up, w_down)
    pair_block = deal(pair_out, "fsdp").reshape(n * rows, 2 * piece)

    def prepare(tokens, cotangent, norm_in, norm_mid, positions):
        x0 = tokens.astype(F32)
        inverse_one = lax.rsqrt(jnp.mean(x0 * x0, axis=-1, keepdims=True) + EPS)
        normed_one = (x0 * inverse_one * norm_in).astype(BF)
        place = one_hot()
        placed = dot(jnp.concatenate([own_half(tokens), cotangent, normed_one]), place)
        grad_half = own_half(placed[h : h + count].astype(BF))
        normed_placed = placed[h + count :].astype(BF)
        cos_table, sin_table = angle_tables(positions)
        gain_two = to_relative(norm_mid)
        return inverse_one, normed_one, place, placed[:h], grad_half, normed_placed, gain_two, cos_table, sin_table

    x0 = tokens.astype(F32)
    (
        inverse_one,
        normed_one,
        place,
        x0_half,
        grad_half,
        normed_placed,
        gain_two,
        cos_table,
        sin_table,
    ) = prepare(tokens, cotangent, norm_in, norm_mid, positions)

    def over_x(piece_rows):
        held = [piece_rows]
        bit = ctx_size // 2
        while bit > 1:
            held = held + [flip(part, "ctx", bit) for part in held]
            bit //= 2
        return held

    def over_cores(held):
        return held + [flip(part, "ctx", 1) for part in held]

    out_x = over_x(in_order(out_slots).reshape(n * rows, -1))
    out_a = jnp.concatenate(out_x)
    out_b = flip(out_a, "ctx", 1)

    query_index = ctx * count + jnp.arange(count, dtype=jnp.int32)
    key_index = jnp.concatenate(
        [(ctx ^ j) * count + jnp.arange(count, dtype=jnp.int32) for j in range(ctx_size)]
    )
    first_key = query_index - positions
    allowed = (key_index[None, :] <= query_index[:, None]) & (
        key_index[None, :] >= first_key[:, None]
    )
    grad_natural = lax.all_gather(grad_half, ("fsdp", "tp"), axis=0, tiled=True)

    def by_features(values, weight):
        return jnp.concatenate(
            [dot_nt(values, weight[:half_d]), dot_nt(values, weight[half_d:])], axis=1
        )

    def attention_scores(queries, key_rows):
        scores = jnp.einsum("tgd,kd->gtk", queries, key_rows, preferred_element_type=F32) * scale
        return jnp.where(allowed[None], scores, -1e30)

    def project_all(normed_one, qkv_whole):
        project = dot(normed_one, qkv_whole) + b_qkv[0].reshape(-1)
        project = project.reshape(count, heads + 2, HD)
        queries = rotary(project[:, :heads], cos_table[:, None], sin_table[:, None]).astype(BF)
        key_local = rotary(project[:, heads], cos_table, sin_table).astype(BF)
        value_local = project[:, heads + 1].astype(BF)
        local_pair = jnp.stack([key_local, value_local])
        pairs_all = [local_pair] + [flip(local_pair, "ctx", j) for j in range(1, ctx_size)]
        key_rows = jnp.concatenate([p[0] for p in pairs_all], axis=0)
        value_rows = jnp.concatenate([p[1] for p in pairs_all], axis=0)
        return queries, key_rows, value_rows

    def attend(queries, key_rows, value_rows, out_whole):
        scores = attention_scores(queries, key_rows)
        peak = jnp.max(scores, axis=-1, keepdims=True)
        shifted = jnp.exp(scores - peak)
        total = jnp.sum(shifted, axis=-1, keepdims=True)
        probabilities = (shifted / total).astype(BF)
        log_total = peak + jnp.log(total)
        attended = jnp.einsum("gtk,kd->tgd", probabilities, value_rows, preferred_element_type=F32)
        attended = attended.astype(BF).reshape(count, -1)
        branch_away = by_features(other_half(attended), out_whole).astype(BF)
        arrived = flip(branch_away, "tp", 1)
        branch = by_features(own_half(after(attended, branch_away)), out_whole)
        middle = x0_half + branch + arrived.astype(F32)
        inverse_two = lax.rsqrt(jnp.mean(middle * middle, axis=-1, keepdims=True) + EPS)
        normed_two = (middle * inverse_two * gain_two).astype(BF)
        return log_total, attended, middle, inverse_two, normed_two

    out_whole = jnp.concatenate([out_a, out_b])
    queries, key_rows, value_rows = segment(
        ready, project_all, after(normed_one, out_whole), qkv_whole
    )
    early = piece // tile // 2
    cut_at = early * 2 * tile
    down_block = deal(after(down_out, value_rows), "fsdp").reshape(n * rows, piece)
    pair_late = after(pair_block[:, cut_at:], value_rows)
    pair_x = flip(pair_late, "ctx", ctx_size // 2)
    pair_core = flip(after(pair_block, value_rows), "ctx", 1)
    log_total, attended, middle, inverse_two, normed_two = segment(
        ready, attend, queries, key_rows, value_rows, out_whole
    )

    second_out = jnp.concatenate([pair_block[:, :cut_at], down_block], axis=1)
    second_x = flip(after(second_out, normed_two), "ctx", ctx_size // 2)

    def gather_first(block):
        away_own = flip(block, "tp", 1)
        ups, downs, swapped = [block], [block], []
        for step in range(1, n - 1):
            up, down = together(gather_up(ups[-1], step), gather_down(downs[-1], step))
            ups.append(up)
            downs.append(down)
            if n == 4 and step == 1:
                swapped.append(flip(jnp.where(z == 0, down, up), "tp", 1))
        return away_own, ups[1:], downs[1:], swapped

    def gather_last(block, ups, downs):
        if n == 4:
            two = jnp.where(z == 0, downs[1], jnp.where(z == 3, ups[1], downs[0]))
            two = flip(two, "tp", 1)
        up, down = gather_up(ups[-1], n - 1), gather_down(downs[-1], n - 1)
        if n == 4:
            up, down, two = together(up, down, two)
            three = jnp.where(
                z == 0, down, jnp.where(z == 3, up, jnp.where(z == 1, downs[1], ups[1]))
            )
            return up, down, [two, flip(three, "tp", 1)]
        ups = dict(enumerate(list(ups) + [up], start=1))
        downs = dict(enumerate(list(downs) + [down], start=1))
        own_slots = slots_of(block, ups, downs)
        gathered = own_slots + [flip(slot, "tp", 1) for slot in own_slots[1:]]
        return up, down, gathered

    away_own, ups, downs, swapped = segment(ready, gather_first, normed_two)
    second_x = after(second_x, ups[-1])
    second_core = flip(second_x, "ctx", 1)
    pair_x_core = flip(after(pair_x, ups[-1]), "ctx", 1)
    down_core = flip(after(down_block, ups[-1]), "ctx", 1)
    up, down, gathered = segment(ready, gather_last, normed_two, ups, downs)
    blocks = [
        [(down_block, 0), (pair_block, 0)],
        [(second_x, cut_at), (pair_x, 0), (second_x, 0)],
        [(down_core, 0), (pair_core, 0)],
        [(second_core, cut_at), (pair_x_core, 0), (second_core, 0)],
    ]
    if n == 4:
        spot = jnp.stack([z, y]).astype(jnp.int32)
        arrivals = [normed_two, *ups, up, *downs, down, away_own, swapped[0], *gathered]
        operands = (spot, arrivals, grad_natural)
    else:
        normed_all = jnp.concatenate(gathered[:n] + [away_own] + gathered[n:])
        by_slot = grad_natural.reshape(n, 2, h, width)
        by_slot = [pick(by_slot, (z - k) % n) for k in range(n)]
        grad_all = jnp.concatenate(
            [pick(slot, y) for slot in by_slot] + [pick(slot, 1 - y) for slot in by_slot]
        )
        operands = (None, normed_all, grad_all)
    activated, grad_pair, pair_whole, down_whole, normed_all, grad_all, act_natural = hidden_pass(
        *operands, blocks, early, piece, tile
    )

    own_tokens = n * h
    ctx_half, ctx_own = width // 2, width // ctx_size

    def core_term(left, right):
        return dot_tn(left[:, ctx_half:], right).astype(BF)

    def x_terms(left, right, arrived):
        terms = []
        for start in range(ctx_own, ctx_half, ctx_own):
            term = dot_tn(left[:, start : start + ctx_own], right)
            terms.append((term + arrived[start : start + ctx_own].astype(F32)).astype(BF))
        return terms

    def to_x(terms):
        return [flip(term, "ctx", j) for term, j in zip(terms, order[1:], strict=False)]

    def own_rows(left, right, arrived, moved):
        total = dot_tn(left[:, :ctx_own], right) + arrived[:ctx_own].astype(F32)
        for part in moved:
            total = total + part.astype(F32)
        return total

    def deal_rows(total):
        return deal(total.astype(BF).reshape(n, rows, total.shape[1]), "fsdp")

    def add_rows(total):
        if n != 4:
            return add_z(total)
        parts = total.reshape(n, rows, total.shape[1])
        out = pick(parts, z)
        for k in range(1, n):
            out = out + rotate(pick(parts, (z + k) % n).astype(BF), "fsdp", k).astype(F32)
        return out

    away = by_features(grad_pair[own_tokens:], pair_whole).astype(BF).reshape(n, h, width)
    low = z < n // 2
    early = jnp.where(low, 1, n - 1)
    leaving = pick(away, early)

    def beside_first(grad_pair, activated, grad_all, pair_whole):
        kept = by_features(grad_pair[:own_tokens], pair_whole).reshape(n, h, width)
        return kept, core_term(grad_all, activated)

    def result_terms(activated, down_whole):
        return by_features(activated, down_whole).astype(BF)

    def result_order(result):
        result = result.reshape(2, n, h, width)
        by_y = jnp.where(y == 0, result, result[::-1])
        by_z = jnp.stack([by_y[:, k] for k in range(n)])
        return jnp.stack([pick(by_z, (z - b) % n) for b in range(n)]).reshape(-1, width)

    y_early = flip(leaving, "tp", 1)
    pair_leaving = segment(ready, core_term, after(normed_all, leaving), grad_pair)
    pair_core = flip(pair_leaving, "ctx", 1)
    kept, down_leaving = segment(
        ready,
        beside_first,
        after(grad_pair, pair_leaving),
        activated,
        grad_all,
        pair_whole,
    )
    if n == 4:
        y_early = after(y_early, kept)
        acc_up = (kept[1] + y_early.astype(F32)).astype(BF)
        acc_down = (kept[3] + y_early.astype(F32)).astype(BF)
        acc_up, acc_down = together(acc_up, acc_down)
        up, down = sum_up(acc_up, 1), sum_down(acc_down, 1)
        y_mid = flip(after(away[2], acc_up), "tp", 1)
        down_core = flip(after(down_leaving, acc_up), "ctx", 1)
        pair_terms = segment(
            ready, x_terms, after(normed_all, acc_up, acc_down), grad_pair, after(pair_core, kept)
        )
        pair_moved = to_x([after(term, up, down, y_mid) for term in pair_terms])

        def rest_of_sum(kept, away, y_early, y_mid, up, down, down_core, act_natural):
            acc_up = (kept[2] + y_mid.astype(F32) + up.astype(F32)).astype(BF)
            acc_down = (kept[2] + y_mid.astype(F32) + down.astype(F32)).astype(BF)
            acc_up, acc_down = together(acc_up, acc_down)
            up, down = sum_up(acc_up, 2), sum_down(acc_down, 2)
            y_late = flip(after(pick(away, n - early), acc_up), "tp", 1)
            by_z = result_terms(after(act_natural, acc_up, acc_down), down_whole)
            up, down, y_late = together(up, down, y_late, by_z)[:3]
            crossed_three = jnp.where(low, y_late, y_early).astype(F32)
            crossed_one = jnp.where(low, y_early, y_late).astype(F32)
            acc_up = (kept[3] + crossed_three + up.astype(F32)).astype(BF)
            acc_down = (kept[1] + crossed_one + down.astype(F32)).astype(BF)
            acc_up, acc_down = together(acc_up, acc_down)
            up, down = sum_up(acc_up, 3), sum_down(acc_down, 3)
            y_own = flip(after(away[0], acc_up), "tp", 1)
            down_terms = x_terms(after(grad_all, acc_up, acc_down), activated, down_core)
            up, down, y_own = together(up, down, y_own, *down_terms)[:3]
            total = kept[0] + y_own.astype(F32) + up.astype(F32) + down.astype(F32)
            return total, by_z, down_terms

        grad_normed_two, by_z, down_terms = segment(
            ready,
            rest_of_sum,
            kept,
            away,
            y_early,
            y_mid,
            after(up, *pair_terms),
            down,
            down_core,
            act_natural,
        )
    else:
        crossed = [flip(away[k], "tp", 1) for k in range(n)]
        grad_normed_two = chain_sum([kept[k] + crossed[k].astype(F32) for k in range(n)])
        by_z = result_order(result_terms(activated, down_whole))
        down_core, pair_core = flip(down_leaving, "ctx", 1), flip(pair_leaving, "ctx", 1)
        pair_terms = x_terms(normed_all, grad_pair, pair_core)
        pair_moved = to_x(pair_terms)
        down_terms = x_terms(grad_all, activated, down_core)

    scaled = grad_normed_two * gain_two
    gain_two_grad = jnp.sum(grad_normed_two * middle * inverse_two, axis=0)
    grad_middle = (
        inverse_two * scaled
        - middle * inverse_two**3 * jnp.mean(scaled * middle, axis=-1, keepdims=True)
        + grad_half.astype(F32)
    )
    middle_half = grad_middle.astype(BF)

    result_sum = lax.psum_scatter(
        by_z, ("fsdp", "tp"), scatter_dimension=0, tiled=True
    )

    out_other = flip(middle_half, "tp", 1)

    def pair_rows(normed_all, grad_pair, pair_core, pair_moved):
        return own_rows(normed_all, grad_pair, pair_core, pair_moved).astype(BF)

    pair_total = segment(
        ready, pair_rows, after(normed_all, middle_half), grad_pair, pair_core, pair_moved
    )
    if n == 4:
        parts = pair_total.reshape(n, rows, 2 * piece)
        pair_dealt = {0: pick(parts, z)}
        for k in (1, 3):
            pair_dealt[k] = rotate(after(pick(parts, (z + k) % n), out_other), "fsdp", k)
    down_moved = to_x([after(term, pair_total, out_other) for term in down_terms])

    def attend_back(own, other, out_whole, queries, key_rows, value_rows, log_total):
        out_in = jnp.where(y == 0, jnp.concatenate([own, other]), jnp.concatenate([other, own]))
        grad_heads = dot(out_in[:, :half_d], out_whole[:half_d])
        grad_heads = grad_heads + dot(out_in[:, half_d:], out_whole[half_d:])
        grad_heads = grad_heads.astype(BF).reshape(count, heads, HD)
        exact = jnp.exp(attention_scores(queries, key_rows) - log_total)
        grad_probs = jnp.einsum("tgd,kd->gtk", grad_heads, value_rows, preferred_element_type=F32)
        grad_scores = exact * (grad_probs - jnp.sum(exact * grad_probs, axis=-1, keepdims=True))
        grad_scores = grad_scores.astype(BF)
        grad_queries = (
            jnp.einsum("gtk,kd->tgd", grad_scores, key_rows, preferred_element_type=F32) * scale
        )
        grad_key_rows = (
            jnp.einsum("gtk,tgd->kd", grad_scores, queries, preferred_element_type=F32) * scale
        )
        grad_value_rows = jnp.einsum(
            "gtk,tgd->kd", exact.astype(BF), grad_heads, preferred_element_type=F32
        )
        grad_pairs = jnp.stack([grad_key_rows, grad_value_rows]).reshape(2, ctx_size, count, HD)
        sent = [grad_pairs[:, j].astype(BF) for j in range(1, ctx_size)]
        return out_in, grad_queries, grad_pairs[:, 0], sent, core_term(out_in, attended)

    out_in, grad_queries, grad_kv, sent, out_leaving = segment(
        ready,
        attend_back,
        middle_half,
        after(out_other, pair_total),
        out_whole,
        queries,
        key_rows,
        value_rows,
        log_total,
    )
    first_way = [*down_moved] + ([pair_dealt[1], pair_dealt[3]] if n == 4 else [])
    moved = [flip(after(part, *first_way), "ctx", j) for j, part in enumerate(sent, start=1)]
    if n == 4:
        pair_dealt[2] = rotate(after(pick(parts, (z + 2) % n), *sent), "fsdp", 2)
        last_way = [pair_dealt[2]]
    else:
        pair_dealt = deal_rows(after(pair_total, *sent))
        last_way = []

    out_core = flip(after(out_leaving, *first_way), "ctx", 1)

    def down_rows(grad_all, activated, down_core, down_moved):
        return own_rows(grad_all, activated, down_core, down_moved).astype(BF)

    down_total = segment(
        ready, down_rows, after(grad_all, *sent), activated, down_core, down_moved
    )
    out_terms = x_terms(out_in, attended, after(out_core, *moved, down_total))
    out_moved = to_x(out_terms)
    if n == 4:
        parts = down_total.reshape(n, rows, piece)
        down_dealt = [pick(parts, z)]
        down_dealt += [rotate(pick(parts, (z + k) % n), "fsdp", k) for k in range(1, n)]
    else:
        down_dealt = deal_rows(down_total)

    def project_back(grad_queries, grad_kv, moved, normed_placed, qkv_whole):
        for part in moved:
            grad_kv = grad_kv + part.astype(F32)
        grad_project = (
            jnp.concatenate(
                [
                    rotary_back(grad_queries, cos_table[:, None], sin_table[:, None]),
                    rotary_back(grad_kv[0], cos_table, sin_table)[:, None],
                    grad_kv[1][:, None],
                ],
                axis=1,
            )
            .astype(BF)
            .reshape(count, -1)
        )
        away = core_term(normed_placed, grad_project)
        arrived = flip(away, "ctx", 1)
        partial_one = dot_nt(after(grad_project, away), qkv_whole).astype(BF)
        terms = x_terms(normed_placed, grad_project, after(arrived, partial_one))
        return grad_project, partial_one, arrived, terms

    grad_project, partial_one, qkv_core, qkv_terms = segment(
        ready,
        project_back,
        grad_queries,
        grad_kv,
        [after(part, *out_terms, *last_way, down_total) for part in moved],
        normed_placed,
        qkv_whole,
    )
    down_there = down_dealt[1:] if n == 4 else []
    qkv_moved = to_x([after(term, *down_there) for term in qkv_terms])
    arrived_one = flip(after(partial_one, *qkv_terms), "tp", 1)

    def natural_columns(parts):
        whole = jnp.concatenate([parts[b] for b in range(n)], axis=1)
        return whole[:, :hidden].astype(F32)

    out_total = own_rows(
        after(out_in, *qkv_terms), attended, out_core, [after(p, *qkv_terms) for p in out_moved]
    )
    out_parts = out_total.reshape(n, rows, -1)
    if n == 4:
        out_dealt = [rotate(pick(out_parts, (z + k) % n).astype(BF), "fsdp", k) for k in range(1, n)]
        out_grad = pick(out_parts, z)
        for part in out_dealt:
            out_grad = out_grad + part.astype(F32)
    else:
        out_dealt = []
        out_grad = add_z(out_total)

    def beside_x(grad_project, out_in, result_sum):
        bias_grad = jnp.sum(grad_project, axis=0, dtype=F32)
        residual = (middle + result_sum.astype(F32)).astype(BF)
        return bias_grad, dot_nt(out_in, place), residual

    bias_grad, middle_natural, residual = segment(
        ready, beside_x, after(grad_project, out_total), out_in, result_sum
    )
    residual_other = flip(residual, "tp", 1)
    qkv_moved = [after(part, bias_grad, *out_dealt) for part in qkv_moved]
    qkv_total = own_rows(normed_placed, grad_project, qkv_core, qkv_moved)
    qkv_grad = add_rows(qkv_total)
    arrived_one = after(arrived_one, qkv_total)

    def beside_z(residual, residual_other, pair_dealt, down_dealt):
        first, second = [residual, residual_other], [residual_other, residual]
        whole = jnp.where(y == 0, jnp.concatenate(first), jnp.concatenate(second))
        if n == 4:
            pair_dealt = in_order([pair_dealt[k] for k in range(n)])
            down_dealt = in_order(down_dealt)
        pair_grad = [natural_columns(every_second(pair_dealt, c)) for c in range(2)]
        output = dot_nt(whole, place).astype(BF)
        return output, jnp.stack(pair_grad, axis=1), natural_columns(down_dealt)

    def every_second(parts, which):
        return jnp.concatenate(
            [parts[:, :, s : s + tile] for s in range(which * tile, 2 * piece, 2 * tile)], axis=2
        )

    output, pair_grad, down_grad = segment(
        ready, beside_z, after(residual, qkv_total), residual_other, pair_dealt, down_dealt
    )
    grad_normed_one = partial_one.astype(F32) + arrived_one.astype(F32)
    scaled = grad_normed_one * norm_in
    gain_one_grad = jnp.sum(grad_normed_one * x0 * inverse_one, axis=0)
    grad_tokens = (
        inverse_one * scaled
        - x0 * inverse_one**3 * jnp.mean(scaled * x0, axis=-1, keepdims=True)
        + middle_natural
    )

    gain_two_pair = sum_everywhere(after(gain_two_grad[None], *sent), ("tp",))
    small = jnp.concatenate(
        [gain_one_grad[None], bias_grad[None], to_natural(gain_two_pair)], axis=1
    )
    small_all = sum_everywhere(small, ("ctx", "fsdp"))
    return (
        output,
        grad_tokens,
        small_all[:, :width],
        qkv_grad.reshape(1, rows, 1, -1),
        small_all[:, width:-width].reshape(1, 1, -1),
        out_grad[None],
        small_all[:, -width:],
        pair_grad[None],
        down_grad[None],
    )


def solution(mesh):
    rows = ("fsdp", "ctx")
    in_specs = (
        P(rows, None),
        P(rows, None),
        P(),
        P(None, rows, "tp", None),
        P(None, "tp", None),
        P(None, rows, "tp"),
        P(),
        P(None, rows, None, "tp"),
        P(None, rows, "tp"),
        P(rows),
        P(rows),
    )
    out_specs = (
        P(rows, None),
        P(rows, None),
        P(),
        P(None, rows, "tp", None),
        P(None, "tp", None),
        P(None, rows, "tp"),
        P(),
        P(None, rows, None, "tp"),
        P(None, rows, "tp"),
    )
    return jax.shard_map(body, mesh=mesh, in_specs=in_specs, out_specs=out_specs, check_vma=False)
```

time: 584 us -> 551 us (0.943); the launches traced: 580 us -> 540 us
  waiting for transfers between devices: 258 us -> 173 us
  matrix products: 81 us -> 116 us
  other arithmetic: 61.9 us -> 71.7 us
  starting transfers between devices: 97 us -> 90.9 us
    ppermute x40 -> x39, waiting for transfers between devices: 154 us -> 87.3 us  [flip(): return lax.ppermute(block, axis, [(i, i ^ bit) for i in range(n)])]
    ppermute x3, waiting for transfers between devices: 61.8 us -> 17.9 us  [gather_down(): lax.ppermute(block, 'fsdp', [(i, i - 1) for i in range(1, n - s + 1)])]
    dot_general x8 -> x12, matrix products: 20.5 us -> 44.9 us  [dot_tn(): lax.dot_general(left, right, (((0,), (0,)), ((), ())), preferred_element_...]
    all_to_all x6 -> x2, starting transfers between devices: 26.8 us -> 8.07 us  [deal(): return lax.all_to_all(blocks, axis, 0, 0, tiled=True)]
    cond x0 -> x37, local copies, waits for them, and re-layouts: none -> 16.8 us
    all_gather x1, waiting for transfers between devices: 24.7 us -> 40.2 us  [body(): lax.all_gather(w_qkv[0].reshape(rows, -1), ('fsdp', 'ctx'), axis=0, tiled...]
    ppermute x6 -> x15, waiting for transfers between devices: 0.02 us -> 14.1 us  [rotate(): lax.ppermute(block, axis, [(i, (i + distance) % n) for i in range(n)])]
    all_to_all x6 -> x2, waiting for transfers between devices: 12.5 us -> 0.01 us  [deal(): return lax.all_to_all(blocks, axis, 0, 0, tiled=True)]
  transfers between devices with their start and end apart: 66 -> 71, of which waited for: 22 -> 25; matrix products, arithmetic and copies ran while one was open for 28% -> 34% of each run, Pallas kernels for 0% -> 0%
where the time goes in v3:
time: 551 us; the launch traced here: 540 us
  waiting for transfers between devices  173 us (31%)
  matrix products  116 us (21%)
  starting transfers between devices  90.9 us (16%)
  other arithmetic  71.7 us (13%)
  local copies, waits for them, and re-layouts  46.8 us (8%)
  Pallas kernels  23.2 us (4%)
  between operations  16.1 us (3%)
    ppermute x39, waiting for transfers between devices, flip(): return lax.ppermute(block, axis, [(i, i ^ bit) for i in range(n)])  87.3 us
    dot_general x12, matrix products, dot_tn(): lax.dot_general(left, right, (((0,), (0,)), ((), ())), preferred_element_...  44.9 us
    dot_general x13, matrix products, dot_nt(): lax.dot_general(left, right, (((1,), (1,)), ((), ())), preferred_element_...  43.9 us
    all_gather x1, waiting for transfers between devices, body(): lax.all_gather(w_qkv[0].reshape(rows, -1), ('fsdp', 'ctx'), axis=0, tiled...  40.2 us
    ppermute x39, starting transfers between devices, flip(): return lax.ppermute(block, axis, [(i, i ^ bit) for i in range(n)])  33 us
    ppermute x15, starting transfers between devices, rotate(): lax.ppermute(block, axis, [(i, (i + distance) % n) for i in range(n)])  24.1 us
    pallas_call x1, Pallas kernels, hidden_pass(): pl.pallas_call(lambda *refs: kernel(parts, early, *refs), grid=(piece //...  23.2 us
    ppermute x3, waiting for transfers between devices, gather_down(): lax.ppermute(block, 'fsdp', [(i, i - 1) for i in range(1, n - s + 1)])  17.9 us
  transfers between devices with their start and end apart: 71, of which 25 were waited for; matrix products, arithmetic and copies ran while one was open for 34% of the time, Pallas kernels for 0%

profile of v3, /device:TPU:0, one launch (start us, length us, event | category | flops | bytes accessed | tf_op | source)
XLA Modules:
  0.0 540.1 jit_solution(5315124550300162580)
XLA Ops:
  7.2 3.1 collective-permute-start.21
  10.3 2.6 collective-permute-start.22
  14.3 4.8 fusion.204
  21.0 3.7 all-to-all-start.1
  26.1 5.2 fusion.207
  41.5 40.2 %all-gather.6.cloned.1.call-done = bf16[1,1536,1,1024]{3,1,2,0:T(8,128)(2,1)} async-done(((bf16[1,96,1,1024]{3,1,2,0:T(8,128)(2,1)}), bf16[1,1536,1,1024]{3,1,2,0:T(8,128)(2,1)}) %all-gather.6.cloned.1.call-update) | async-done | bytes 3145744 | tf_op jit(solution)/shard_map/all_gather | solution.py:361
  81.7 12.0 %conditional.14 = (bf16[256,6,128]{2,1,0:T(8,128)(2,1)S(1)}, bf16[1024,128]{1,0:T(8,128)(2,1)S(1)}, bf16[1024,128]{1,0:T(8,128)(2,1)S(1)}) conditional(s32[]{:T(128)} %bitcast.70, () %tuple.191, (bf16[256,1536]{1,0:T(8,128)(2,1)}, bf16[1536,1024]{1,0:T(8,128)(2,1)}, f32[1,1,1024]{2,1,0:T(1,128)S(1)}, f32[256,128]{1,0:T(8,128)S(1)}, ...), branch_computations={%region_1.2_spmd, %region_2.3_spmd} | conditional | flops 809025536 | bytes 16191632 | solution.py:62
  81.7 3.1 fusion
  88.3 3.9 collective-permute-done.11
  93.8 4.4 all-to-all-start
  104.3 33.0 %conditional.15 = (f32[6,256,1]{1,0,2:T(8,128)S(1)}, bf16[256,768]{0,1:T(8,128)(2,1)S(1)}, f32[128,1536]{1,0:T(8,128)}, f32[128,1]{0,1:T(1,128)S(1)}, bf16[128,1...) conditional(s32[]{:T(128)} %bitcast.70, () %tuple.190, (pred[256,1024]{0,1:T(8,128)(4,1)}, ...), branch_computations={%region_3.4_spmd, %region_4.8_spmd} | conditional | flops 1431108608 | bytes 37164804 | solution.py:62
  108.8 2.8 fusion.8
  121.5 12.3 %collective-permute-done.13 = bf16[128,1536]{1,0:T(8,128)(2,1)S(1)} collective-permute-done((bf16[128,1536]{1,0:T(8,128)(2,1)S(1)}, bf16[128,1536]{1,0:T(8,128)(2,1)S(1)}, u32[]{:S(2)}, u32[]{:S(2)}) %collective-permute-start.13) | collective-permute-done | bytes 393248 | tf_op jit(solution)/shard_map/cond/branch_1_fun/ppermute | solution.py:72
  142.2 37.5 %conditional.16 = (bf16[128,1536]{1,0:T(8,128)(2,1)}, bf16[128,1536]{1,0:T(8,128)(2,1)}, bf16[128,1536]{1,0:T(8,128)(2,1)}, bf16[128,1536]{1,0:T(8,128)(2,1)}, b...) conditional(s32[]{:T(128)} %bitcast.70, () %tuple.196, (bf16[128,1536]{1,0:T(8,128)(2,1)S(1)}, ...), branch_computations={%region_8.9_spmd, %region_9.10_spmd} | conditional | flops 196609 | bytes 10617130 | solution.py:62
  142.2 4.5 collective-permute-start.1
  150.6 10.8 %collective-permute-done.1 = bf16[128,1536]{1,0:T(8,128)(2,1)} collective-permute-done((bf16[128,1536]{1,0:T(8,128)(2,1)S(1)}, bf16[128,1536]{1,0:T(8,128)(2,1)}, u32[]{:S(2)}, u32[]{:S(2)}) %collective-permute-start.1) | collective-permute-done | bytes 393248 | tf_op jit(solution)/shard_map/cond/branch_1_fun/ppermute | solution.py:96
  169.0 10.7 %collective-permute-done.4 = bf16[128,1536]{1,0:T(8,128)(2,1)} collective-permute-done((bf16[128,1536]{1,0:T(8,128)(2,1)}, bf16[128,1536]{1,0:T(8,128)(2,1)}, u32[]{:S(2)}, u32[]{:S(2)}) %collective-permute-start.4) | collective-permute-done | bytes 393248 | tf_op jit(solution)/shard_map/cond/branch_1_fun/ppermute | solution.py:101
  181.1 24.7 %conditional.17 = (bf16[128,1536]{1,0:T(8,128)(2,1)}, bf16[128,1536]{1,0:T(8,128)(2,1)}, bf16[128,1536]{1,0:T(8,128)(2,1)}, bf16[128,1536]{1,0:T(8,128)(2,1)}) conditional(s32[]{:T(128)} %bitcast.70, () %tuple.198, (bf16[128,1536]{1,0:T(8,128)(2,1)}, bf16[128,1536]{1,0:T(8,128)(2,1)}, s32[]{:T(128)}, bf16[128,1536]{1,0:T(8,128)(2,1)}) %tuple.199), branch_computations={%region_10.11_spmd, %region_11.12_spmd} | conditional | flops 983043 | bytes 9830624 | solution.py:62
  186.6 4.7 collective-permute-done.8
  191.3 4.9 collective-permute-done.7
  197.8 7.6 %collective-permute-done.9 = bf16[128,1536]{1,0:T(8,128)(2,1)} collective-permute-done((bf16[128,1536]{1,0:T(8,128)(2,1)S(1)}, bf16[128,1536]{1,0:T(8,128)(2,1)}, u32[]{:S(2)}, u32[]{:S(2)}) %collective-permute-start.9) | collective-permute-done | bytes 393248 | tf_op jit(solution)/shard_map/cond/branch_1_fun/ppermute | solution.py:72
  207.5 3.8 collective-permute-done.29.refs_19_
  211.3 3.6 collective-permute-done.28.refs_18_
  215.0 23.2 %shard_map.170 = (bf16[1024,1152]{1,0:T(8,128)(2,1)}, bf16[1024,2304]{1,0:T(8,128)(2,1)}, bf16[1536,2304]{1,0:T(8,128)(2,1)}, bf16[1536,1152]{1,0:T(8,128)(2,1)}...) custom-call(s32[2]{0:T(128)} %pad_add_fusion.1.refs_0_, ...), custom_call_target="tpu_custom_call" | custom-call | flops 10871635968 | bytes 40894464 | tf_op jit(solution)/shard_map/pallas_call | solution.py:261
  238.2 4.9 fusion.151
  243.1 4.0 fusion.146
  248.2 7.7 %conditional.18 = (bf16[768,2304]{1,0:T(8,128)(2,1)}) conditional(s32[]{:T(128)} %bitcast.70, () %tuple.207, (bf16[1024,1536]{1,0:T(8,128)(2,1)S(1)}, bf16[1024,2304]{1,0:T(8,128)(2,1)}) %tuple.407), branch_computations={%region_12.13_spmd, %region_13.14_spmd} | conditional | flops 3625648128 | bytes 9830408 | solution.py:62
  248.2 7.7 %convolution_convert_fusion.2 = bf16[768,2304]{1,0:T(8,128)(2,1)} fusion(bf16[1024,2304]{1,0:T(8,128)(2,1)} %get-tuple-element.283, bf16[1024,1536]{1,0:T(8,128)(2,1)S(1)} %get-tuple-element.282), kind=kOutput, calls=%fused_computation.58 | convolution fusion | flops 3625648128 | bytes 9830400 | tf_op jit(solution)/shard_map/cond/branch_1_fun/dot_general | solution.py:45
  256.3 14.8 %conditional.19 = (f32[4,128,1536]{2,1,0:T(8,128)S(1)}, bf16[768,1152]{1,0:T(8,128)(2,1)}) conditional(s32[]{:T(128)} %bitcast.70, () %tuple.195, (bf16[1024,2304]{1,0:T(8,128)(2,1)}, bf16[1536,2304]{1,0:T(8,128)(2,1)}, bf16[1024,1536]{1,0:T(8,128)(2,1)}, bf16[1024,1152]{1,0:T(8,128)(2,1)}) %tuple.211), branch_computations={%region_14.15_spmd, %region_15.16_spmd} | conditional | flops 5437489152 | bytes 77267048 | solution.py:62
  256.5 4.9 fusion.28
  261.4 3.7 fusion.30
  267.7 3.5 convolution_convert_fusion.3
  280.7 6.4 %conditional.20 = (bf16[384,2304]{1,0:T(8,128)(2,1)}) conditional(s32[]{:T(128)} %bitcast.70, () %tuple.215, (bf16[1024,1536]{1,0:T(8,128)(2,1)}, bf16[1024,2304]{1,0:T(8,128)(2,1)}, bf16[768,2304]{1,0:T(8,128)(2,1)}) %tuple.218), branch_computations={%region_16.17_spmd, %region_17.18_spmd} | conditional | flops 1814593536 | bytes 9043976 | solution.py:62
  280.7 6.4 %fusion.35 = bf16[384,2304]{1,0:T(8,128)(2,1)} fusion(bf16[1024,2304]{1,0:T(8,128)(2,1)} %get-tuple-element.289, bf16[768,2304]{1,0:T(8,128)(2,1)} %get-tuple-element.290, bf16[1024,1536]{1,0:T(8,128)(2,1)} %get-tuple-element.288), kind=kOutput, calls=%fused_computation.70 | convolution fusion | flops 1814593536 | bytes 9043968 | tf_op jit(solution)/shard_map/cond/branch_1_fun/dot_general | solution.py:45
  288.0 37.7 %conditional.21 = (f32[128,1536]{1,0:T(8,128)}, bf16[1024,1536]{0,1:T(8,128)(2,1)}, bf16[384,1152]{1,0:T(8,128)(2,1)}) conditional(s32[]{:T(128)} %bitcast.70, () %tuple.194, (f32[4,128,1536]{2,1,0:T(8,128)S(1)}, pred[]{:T(512)}, bf16[128,1536]{1,0:T(8,128)(2,1)}, bf16[128,1536]{1,0:T(8,128)(2,1)}, bf16[128,1536]{1,0:T(8,128)(2,1)}, ...), branch_computations={%region_18.19_spmd, %region_19.20_spmd} | conditional | flops 4544151552 | bytes 76087696 | solution.py:62
  296.1 4.6 fusion.42
  306.6 6.8 %collective-permute-start.17 = (bf16[128,1536]{1,0:T(8,128)(2,1)S(1)}, bf16[128,1536]{1,0:T(8,128)(2,1)S(1)}, u32[]{:S(2)}, u32[]{:S(2)}) collective-permute-start(bf16[128,1536]{1,0:T(8,128)(2,1)S(1)} %get-tuple-element.308), channel_id=1, source_target_pairs={{0,8},{8,16},{16,24},{1,9},{9,17},{17,25},{2,10},{10,18},{18,26},{... | collective-permute-start | bytes 1179656 | tf_op jit(solution)/shard_map/cond/branch_1_fun/ppermute | solution.py:112
  315.5 3.5 fusion.37
  319.1 3.0 collective-permute-done.19
  322.1 2.6 collective-permute-done.18
  325.7 4.6 copy.66
  338.5 30.6 %collective-permute-done.39 = bf16[384,2304]{1,0:T(8,128)(2,1)} collective-permute-done((bf16[384,2304]{1,0:T(8,128)(2,1)S(1)}, bf16[384,2304]{1,0:T(8,128)(2,1)}, u32[]{:S(2)}, u32[]{:S(2)}) %collective-permute-start.39) | collective-permute-done | bytes 1769504 | tf_op jit(solution)/shard_map/ppermute | solution.py:72
  369.0 8.6 %conditional.22 = (bf16[384,2304]{1,0:T(8,128)(2,1)}, bf16[4,96,2304]{2,1,0:T(8,128)(2,1)S(1)}) conditional(s32[]{:T(128)} %bitcast.70, () %tuple.222, (bf16[1024,1536]{1,0:T(8,128)(2,1)}, bf16[1024,2304]{1,0:T(8,128)(2,1)}, bf16[768,2304]{1,0:T(8,128)(2,1)}, bf16[384,2304]{1,0:T(8,128)(2,1)}) %tuple.225), branch_computations={%region_21.22_spmd, %region_22.23_spmd} | conditional | flops 1816363008 | bytes 14352400 | solution.py:62
  369.0 7.1 %fusion.56 = bf16[384,2304]{1,0:T(8,128)(2,1)} fusion(bf16[1024,2304]{1,0:T(8,128)(2,1)} %get-tuple-element.319, bf16[384,2304]{1,0:T(8,128)(2,1)} %get-tuple-element.321, bf16[768,2304]{1,0:T(8,128)(2,1)} %get-tuple-element.320, bf16[1024,1536]{1,0:T(8,128)(2,1)} %get-tuple-element.318), kind=kOutput, calls=%fused_computation.98 | convolution fusion | flops 1816363008 | bytes 10813440 | tf_op jit(solution)/shard_map/cond/branch_1_fun/dot_general | solution.py:45
  382.1 25.6 %conditional.23 = (bf16[256,1536]{1,0:T(8,128)(2,1)}, f32[256,6,128]{2,0,1:T(8,128)S(1)}, f32[2,256,128]{2,1,0:T(8,128)}, bf16[2,256,128]{2,1,0:T(8,128)(2,1)}, ...) conditional(s32[]{:T(128)} %bitcast.70, () %tuple.189, ...), branch_computations={%region_23.24_spmd, %region_24.26_spmd} | conditional | flops 2948004352 | bytes 80902296 | solution.py:62
  388.7 4.4 fusion.59
  393.1 2.9 fusion.60
  396.0 2.7 fusion.62
  410.2 5.1 fusion.122
  422.1 5.1 conditional.24
  422.1 3.8 fusion.83
  437.5 11.1 %collective-permute-done.47 = bf16[96,2304]{1,0:T(8,128)(2,1)} collective-permute-done((bf16[96,2304]{1,0:T(8,128)(2,1)}, bf16[96,2304]{1,0:T(8,128)(2,1)}, u32[]{:S(2)}, u32[]{:S(2)}) %collective-permute-start.47) | collective-permute-done | bytes 442400 | tf_op jit(solution)/shard_map/ppermute | solution.py:67
  448.6 13.0 %conditional.25 = (bf16[256,1024]{1,0:T(8,128)(2,1)}, bf16[256,1536]{1,0:T(8,128)(2,1)}, bf16[768,1024]{0,1:T(8,128)(2,1)}, bf16[384,1024]{0,1:T(8,128)(2,1)}, f32[256,1536]{1,0:T(8,128)S(1)}) conditional(s32[]{:T(128)} %bitcast.70, () %tuple.188, (f32[256,128]{1,0:T(8,128)S(1)}, f32[256,6,128]{2,0,1:T(8,128)S(1)}, f32[256,128]{1,0:T(8,128)S(1)}, ...), branch_computations={%region_28.29_spmd, %region_29.30_spmd} | conditional | flops 1415266304 | bytes 39583852 | solution.py:62
  455.3 3.0 fusion.202
  458.9 2.8 fusion.85
  471.3 3.8 collective-permute-start.55
  476.7 6.4 %conditional.26 = (f32[1024]{0:T(1024)S(1)}, f32[256,1536]{1,0:T(8,128)S(1)}, bf16[128,1536]{1,0:T(8,128)(2,1)S(1)}) conditional(s32[]{:T(128)} %bitcast.70, () %tuple.187, (bf16[256,1024]{1,0:T(8,128)(2,1)}, bf16[256,1536]{1,0:T(8,128)(2,1)}, bf16[1536,1536]{1,0:T(8,128)(2,1)}, bf16[128,1536]{1,0:T(8,128)(2,1)}, f32[128,1536]{1,0:T(8,128)}) %tuple.247), branch_computations={%region_31.32_spmd, %region_32.34_spmd} | conditional | flops 1209072640 | bytes 10752052 | solution.py:62
  476.8 4.0 fusion.208
  493.1 2.7 collective-permute-start.63
  499.0 11.7 %collective-permute-done.61 = f32[1,4096]{1,0:T(1,128)S(1)} collective-permute-done((f32[1,4096]{1,0:T(1,128)S(1)}, f32[1,4096]{1,0:T(1,128)S(1)}, u32[]{:S(2)}, u32[]{:S(2)}) %collective-permute-start.61) | collective-permute-done | bytes 16416 | tf_op jit(solution)/shard_map/ppermute | solution.py:72
  511.4 2.8 fusion.141
  517.8 13.8 %conditional.27 = (bf16[256,1536]{1,0:T(8,128)(2,1)}, f32[1,96,4480]{2,1,0:T(8,128)}, f32[1,96,2,4480]{3,2,1,0:T(2,128)S(1)}) conditional(s32[]{:T(128)} %bitcast.70, () %tuple.186, (s32[]{:T(128)}, bf16[128,1536]{1,0:T(8,128)(2,1)S(1)}, bf16[128,1536]{1,0:T(8,128)(2,1)S(1)}, bf16[1536,1536]{1,0:T(8,128)(2,1)}, bf16[4,96,2304]{2,1,0:T(8,128)(2,1)}, ...), branch_computations={%region_34.35_spmd, %region_35.36_spmd} | conditional | flops 1236307968 | bytes 47039200 | solution.py:62
  521.1 2.7 copy.82
  526.5 5.1 convolution_convert_fusion.7
  (402 shorter events, 195.4 us)
Async XLA Ops:
  7.2 74.5 %all-gather.6.cloned.1.call-start = ((), (), s32[]{:S(2)}) async-start(), calls=%async_computation.5 | async-start | bytes 3342336 | tf_op jit(solution)/shard_map/all_gather | solution.py:361
  7.2 29.6 %collective-permute-start.21 = (bf16[96,768]{1,0:T(8,128)(2,1)}, bf16[96,768]{1,0:T(8,128)(2,1)}, u32[]{:S(2)}, u32[]{:S(2)}) collective-permute-start(bf16[96,768]{1,0:T(8,128)(2,1)} %bitcast.420), channel_id=1, source_target_pairs={{0,8},{8,16},{16,24},{24,0},{1,9},{9,17},{17,25},{25,1},{2,10},{10... | collective-permute-start | bytes 442376 | tf_op jit(solution)/shard_map/ppermute | solution.py:67
  10.3 26.5 %collective-permute-start.22 = (bf16[96,768]{1,0:T(8,128)(2,1)}, bf16[96,768]{1,0:T(8,128)(2,1)}, u32[]{:S(2)}, u32[]{:S(2)}) collective-permute-start(bf16[96,768]{1,0:T(8,128)(2,1)} %bitcast.421), channel_id=1, source_target_pairs={{0,16},{8,24},{16,0},{24,8},{1,17},{9,25},{17,1},{25,9},{2,18},{10... | collective-permute-start | bytes 442376 | tf_op jit(solution)/shard_map/ppermute | solution.py:67
  12.9 23.9 %collective-permute-start.23 = (bf16[96,768]{1,0:T(8,128)(2,1)}, bf16[96,768]{1,0:T(8,128)(2,1)}, u32[]{:S(2)}, u32[]{:S(2)}) collective-permute-start(bf16[96,768]{1,0:T(8,128)(2,1)} %bitcast.422), channel_id=1, source_target_pairs={{0,24},{8,0},{16,8},{24,16},{1,25},{9,1},{17,9},{25,17},{2,26},{10... | collective-permute-start | bytes 442376 | tf_op jit(solution)/shard_map/ppermute | solution.py:67
  21.0 72.7 %all-to-all-start.1 = ((bf16[4,96,2304]{2,1,0:T(8,128)(2,1)}), bf16[4,96,2304]{2,1,0:T(8,128)(2,1)S(1)}, u32[]{:S(2)}, u32[]{:S(2)}) async-start(bf16[4,96,2304]{2,1,0:T(8,128)(2,1)} %pad_maximum_fusion.21), calls=%async_computation.1 | async-start | bytes 3538944 | tf_op jit(solution)/shard_map/all_to_all | solution.py:91
  24.8 182.7 %all-gather.4.cloned.1.call-start = ((), (), s32[]{:S(2)}) async-start(), calls=%async_computation.3 | async-start | bytes 3538944 | tf_op jit(solution)/shard_map/all_gather | solution.py:431
  38.9 59.3 %collective-permute-start.24 = (bf16[384,768]{1,0:T(8,128)(2,1)}, bf16[384,768]{1,0:T(8,128)(2,1)}, u32[]{:S(2)}, u32[]{:S(2)}) collective-permute-start(bf16[384,768]{1,0:T(8,128)(2,1)} %bitcast.77), channel_id=1, source_target_pairs={{0,4},{2,6},{4,0},{6,2},{1,5},{3,7},{5,1},{7,3},{8,12},{10,14},{12... | collective-permute-start | bytes 1769480 | tf_op jit(solution)/shard_map/ppermute | solution.py:72
  85.9 6.3 %collective-permute-start.11 = (bf16[2,256,128]{2,1,0:T(8,128)(2,1)S(1)}, bf16[2,256,128]{2,1,0:T(8,128)(2,1)S(1)}, u32[]{:S(2)}, u32[]{:S(2)}) collective-permute-start(bf16[2,256,128]{2,1,0:T(8,128)(2,1)S(1)} %pad_maximum_fusion.2), channel_id=1, source_target_pairs={{0,4},{2,6},{4,0},{6,2},{1,5},{3,7},{5,1},{7,3},{8,12},{10,14},{12... | collective-permute-start | bytes 393224 | tf_op jit(solution)/shard_map/cond/branch_1_fun/ppermute | solution.py:72
  87.4 6.3 %collective-permute-start.12 = (bf16[2,256,128]{2,1,0:T(8,128)(2,1)S(1)}, bf16[2,256,128]{2,1,0:T(8,128)(2,1)S(1)}, u32[]{:S(2)}, u32[]{:S(2)}) collective-permute-start(bf16[2,256,128]{2,1,0:T(8,128)(2,1)S(1)} %pad_maximum_fusion.2), channel_id=1, source_target_pairs={{0,6},{2,4},{4,2},{6,0},{1,7},{3,5},{5,3},{7,1},{8,14},{10,12},{12... | collective-permute-start | bytes 393224 | tf_op jit(solution)/shard_map/cond/branch_1_fun/ppermute | solution.py:72
  93.8 43.5 %all-to-all-start = ((bf16[4,96,1152]{2,1,0:T(8,128)(2,1)}), bf16[4,96,1152]{2,1,0:T(8,128)(2,1)}, u32[]{:S(2)}, u32[]{:S(2)}) async-start(bf16[4,96,1152]{2,1,0:T(8,128)(2,1)} %pad_maximum_fusion.24), calls=%async_computation | async-start | bytes 1769472 | tf_op jit(solution)/shard_map/all_to_all | solution.py:91
  98.2 378.6 %reduce-scatter.2.cloned.1.call-start = ((), (), s32[]{:S(2)}) async-start(), calls=%async_computation.4 | async-start | bytes 3538944 | tf_op jit(solution)/shard_map/reduce_scatter | solution.py:670
  115.4 18.3 %collective-permute-start.13 = (bf16[128,1536]{1,0:T(8,128)(2,1)S(1)}, bf16[128,1536]{1,0:T(8,128)(2,1)S(1)}, u32[]{:S(2)}, u32[]{:S(2)}) collective-permute-start(bf16[128,1536]{1,0:T(8,128)(2,1)S(1)} %pad_maximum_fusion.3), channel_id=1, source_target_pairs={{0,1},{1,0},{2,3},{3,2},{4,5},{5,4},{6,7},{7,6},{8,9},{9,8},{10,11... | collective-permute-start | bytes 1179656 | tf_op jit(solution)/shard_map/cond/branch_1_fun/ppermute | solution.py:72
  139.9 66.0 %collective-permute-start.26 = (bf16[384,1920]{1,0:T(8,128)(2,1)}, bf16[384,1920]{1,0:T(8,128)(2,1)}, u32[]{:S(2)}, u32[]{:S(2)}) collective-permute-start(bf16[384,1920]{1,0:T(8,128)(2,1)} %pad_maximum_fusion.22), channel_id=1, source_target_pairs={{0,4},{2,6},{4,0},{6,2},{1,5},{3,7},{5,1},{7,3},{8,12},{10,14},{12... | collective-permute-start | bytes 4423688 | tf_op jit(solution)/shard_map/ppermute | solution.py:72
  142.2 19.2 %collective-permute-start.1 = (bf16[128,1536]{1,0:T(8,128)(2,1)S(1)}, bf16[128,1536]{1,0:T(8,128)(2,1)}, u32[]{:S(2)}, u32[]{:S(2)}) collective-permute-start(bf16[128,1536]{1,0:T(8,128)(2,1)S(1)} %get-tuple-element.269), channel_id=1, source_target_pairs={{0,8},{8,16},{16,24},{1,9},{9,17},{17,25},{2,10},{10,18},{18,26},{... | collective-permute-start | bytes 1179656 | tf_op jit(solution)/shard_map/cond/branch_1_fun/ppermute | solution.py:96
  146.8 17.0 %collective-permute-start.2 = (bf16[128,1536]{1,0:T(8,128)(2,1)S(1)}, bf16[128,1536]{1,0:T(8,128)(2,1)}, u32[]{:S(2)}, u32[]{:S(2)}) collective-permute-start(bf16[128,1536]{1,0:T(8,128)(2,1)S(1)} %get-tuple-element.269), channel_id=1, source_target_pairs={{8,0},{16,8},{24,16},{9,1},{17,9},{25,17},{10,2},{18,10},{26,18},{... | collective-permute-start | bytes 1179656 | tf_op jit(solution)/shard_map/cond/branch_1_fun/ppermute | solution.py:101
  148.1 31.6 %collective-permute-start = (bf16[128,1536]{1,0:T(8,128)(2,1)S(1)}, bf16[128,1536]{1,0:T(8,128)(2,1)}, u32[]{:S(2)}, u32[]{:S(2)}) collective-permute-start(bf16[128,1536]{1,0:T(8,128)(2,1)S(1)} %get-tuple-element.269), channel_id=1, source_target_pairs={{0,1},{1,0},{2,3},{3,2},{4,5},{5,4},{6,7},{7,6},{8,9},{9,8},{10,11... | collective-permute-start | bytes 1179656 | tf_op jit(solution)/shard_map/cond/branch_1_fun/ppermute | solution.py:72
  165.2 14.5 %collective-permute-start.4 = (bf16[128,1536]{1,0:T(8,128)(2,1)}, bf16[128,1536]{1,0:T(8,128)(2,1)}, u32[]{:S(2)}, u32[]{:S(2)}) collective-permute-start(bf16[128,1536]{1,0:T(8,128)(2,1)} %collective-permute-done.2), channel_id=1, source_target_pairs={{8,0},{16,8},{9,1},{17,9},{10,2},{18,10},{11,3},{19,11},{12,4},{20... | collective-permute-start | bytes 1179656 | tf_op jit(solution)/shard_map/cond/branch_1_fun/ppermute | solution.py:101
  167.5 12.2 %collective-permute-start.5 = (bf16[128,1536]{1,0:T(8,128)(2,1)S(1)}, bf16[128,1536]{1,0:T(8,128)(2,1)}, u32[]{:S(2)}, u32[]{:S(2)}) collective-permute-start(bf16[128,1536]{1,0:T(8,128)(2,1)S(1)} %broadcast_select_fusion), channel_id=1, source_target_pairs={{0,1},{1,0},{2,3},{3,2},{4,5},{5,4},{6,7},{7,6},{8,9},{9,8},{10,11... | collective-permute-start | bytes 1179656 | tf_op jit(solution)/shard_map/cond/branch_1_fun/ppermute | solution.py:72
  179.7 26.7 %collective-permute-start.27 = (bf16[384,1536]{1,0:T(8,128)(2,1)}, bf16[384,1536]{1,0:T(8,128)(2,1)}, u32[]{:S(2)}, u32[]{:S(2)}) collective-permute-start(bf16[384,1536]{1,0:T(8,128)(2,1)} %slice.561), channel_id=1, source_target_pairs={{0,4},{2,6},{4,0},{6,2},{1,5},{3,7},{5,1},{7,3},{8,12},{10,14},{12... | collective-permute-start | bytes 3538952 | tf_op jit(solution)/shard_map/ppermute | solution.py:72
  182.3 9.0 %collective-permute-start.8 = (bf16[128,1536]{1,0:T(8,128)(2,1)S(1)}, bf16[128,1536]{1,0:T(8,128)(2,1)}, u32[]{:S(2)}, u32[]{:S(2)}) collective-permute-start(bf16[128,1536]{1,0:T(8,128)(2,1)S(1)} %select_select_fusion.1), channel_id=1, source_target_pairs={{0,1},{1,0},{2,3},{3,2},{4,5},{5,4},{6,7},{7,6},{8,9},{9,8},{10,11... | collective-permute-start | bytes 1179656 | tf_op jit(solution)/shard_map/cond/branch_1_fun/ppermute | solution.py:72
  183.9 7.4 %collective-permute-start.6 = (bf16[128,1536]{1,0:T(8,128)(2,1)}, bf16[128,1536]{1,0:T(8,128)(2,1)}, u32[]{:S(2)}, u32[]{:S(2)}) collective-permute-start(bf16[128,1536]{1,0:T(8,128)(2,1)} %get-tuple-element.275), channel_id=1, source_target_pairs={{16,24},{17,25},{18,26},{19,27},{20,28},{21,29},{22,30},{23,31}} | collective-permute-start | bytes 1179656 | tf_op jit(solution)/shard_map/cond/branch_1_fun/ppermute | solution.py:96
  185.3 10.9 %collective-permute-start.7 = (bf16[128,1536]{1,0:T(8,128)(2,1)}, bf16[128,1536]{1,0:T(8,128)(2,1)}, u32[]{:S(2)}, u32[]{:S(2)}) collective-permute-start(bf16[128,1536]{1,0:T(8,128)(2,1)} %get-tuple-element.276), channel_id=1, source_target_pairs={{8,0},{9,1},{10,2},{11,3},{12,4},{13,5},{14,6},{15,7}} | collective-permute-start | bytes 1179656 | tf_op jit(solution)/shard_map/cond/branch_1_fun/ppermute | solution.py:101
  197.4 8.0 %collective-permute-start.9 = (bf16[128,1536]{1,0:T(8,128)(2,1)S(1)}, bf16[128,1536]{1,0:T(8,128)(2,1)}, u32[]{:S(2)}, u32[]{:S(2)}) collective-permute-start(bf16[128,1536]{1,0:T(8,128)(2,1)S(1)} %select_select_fusion), channel_id=1, source_target_pairs={{0,1},{1,0},{2,3},{3,2},{4,5},{5,4},{6,7},{7,6},{8,9},{9,8},{10,11... | collective-permute-start | bytes 1179656 | tf_op jit(solution)/shard_map/cond/branch_1_fun/ppermute | solution.py:72
  205.9 9.1 %collective-permute-start.30 = (bf16[384,1920]{1,0:T(8,128)(2,1)}, bf16[384,1920]{1,0:T(8,128)(2,1)}, u32[]{:S(2)}, u32[]{:S(2)}) collective-permute-start(bf16[384,1920]{1,0:T(8,128)(2,1)} %collective-permute-done.26.refs_15_.refs_17_), channel_id=1, source_target_pairs={{0,2},{2,0},{4,6},{6,4},{1,3},{3,1},{5,7},{7,5},{8,10},{10,8},{12,... | collective-permute-start | bytes 4423688 | tf_op jit(solution)/shard_map/ppermute | solution.py:72
  206.4 8.6 %collective-permute-start.31 = (bf16[384,1536]{1,0:T(8,128)(2,1)}, bf16[384,1536]{1,0:T(8,128)(2,1)}, u32[]{:S(2)}, u32[]{:S(2)}) collective-permute-start(bf16[384,1536]{1,0:T(8,128)(2,1)} %collective-permute-done.27.refs_16_), channel_id=1, source_target_pairs={{0,2},{2,0},{4,6},{6,4},{1,3},{3,1},{5,7},{7,5},{8,10},{10,8},{12,... | collective-permute-start | bytes 3538952 | tf_op jit(solution)/shard_map/ppermute | solution.py:72
  206.5 8.5 %collective-permute-start.28 = (bf16[384,1152]{1,0:T(8,128)(2,1)}, bf16[384,1152]{1,0:T(8,128)(2,1)}, u32[]{:S(2)}, u32[]{:S(2)}) collective-permute-start(bf16[384,1152]{1,0:T(8,128)(2,1)} %bitcast.90.refs_13_), channel_id=1, source_target_pairs={{0,2},{2,0},{4,6},{6,4},{1,3},{3,1},{5,7},{7,5},{8,10},{10,8},{12,... | collective-permute-start | bytes 2654216 | tf_op jit(solution)/shard_map/ppermute | solution.py:72
  255.8 24.9 %collective-permute-start.35 = (bf16[768,2304]{1,0:T(8,128)(2,1)}, bf16[768,2304]{1,0:T(8,128)(2,1)}, u32[]{:S(2)}, u32[]{:S(2)}) collective-permute-start(bf16[768,2304]{1,0:T(8,128)(2,1)} %get-tuple-element.882), channel_id=1, source_target_pairs={{0,2},{2,0},{4,6},{6,4},{1,3},{3,1},{5,7},{7,5},{8,10},{10,8},{12,... | collective-permute-start | bytes 10616840 | tf_op jit(solution)/shard_map/ppermute | solution.py:72
  256.0 15.2 %collective-permute-start.32 = (bf16[128,1536]{1,0:T(8,128)(2,1)}, bf16[128,1536]{1,0:T(8,128)(2,1)}, u32[]{:S(2)}, u32[]{:S(2)}) collective-permute-start(bf16[128,1536]{1,0:T(8,128)(2,1)} %fusion.160), channel_id=1, source_target_pairs={{0,1},{1,0},{2,3},{3,2},{4,5},{5,4},{6,7},{7,6},{8,9},{9,8},{10,11... | collective-permute-start | bytes 1179656 | tf_op jit(solution)/shard_map/ppermute | solution.py:72
  273.3 14.7 %collective-permute-start.37 = (bf16[768,1152]{1,0:T(8,128)(2,1)}, bf16[768,1152]{1,0:T(8,128)(2,1)}, u32[]{:S(2)}, u32[]{:S(2)}) collective-permute-start(bf16[768,1152]{1,0:T(8,128)(2,1)} %get-tuple-element.509), channel_id=1, source_target_pairs={{0,2},{2,0},{4,6},{6,4},{1,3},{3,1},{5,7},{7,5},{8,10},{10,8},{12,... | collective-permute-start | bytes 5308424 | tf_op jit(solution)/shard_map/ppermute | solution.py:72
  274.1 13.0 %collective-permute-start.34 = (bf16[128,1536]{1,0:T(8,128)(2,1)}, bf16[128,1536]{1,0:T(8,128)(2,1)}, u32[]{:S(2)}, u32[]{:S(2)}) collective-permute-start(bf16[128,1536]{1,0:T(8,128)(2,1)} %get-tuple-element.500), channel_id=1, source_target_pairs={{0,8},{1,9},{2,10},{3,11},{4,12},{5,13},{6,14},{7,15}} | collective-permute-start | bytes 1179656 | tf_op jit(solution)/shard_map/ppermute | solution.py:112
  276.3 11.7 %collective-permute-start.33 = (bf16[128,1536]{1,0:T(8,128)(2,1)}, bf16[128,1536]{1,0:T(8,128)(2,1)}, u32[]{:S(2)}, u32[]{:S(2)}) collective-permute-start(bf16[128,1536]{1,0:T(8,128)(2,1)} %pad_maximum_fusion.26), channel_id=1, source_target_pairs={{0,1},{1,0},{2,3},{3,2},{4,5},{5,4},{6,7},{7,6},{8,9},{9,8},{10,11... | collective-permute-start | bytes 1179656 | tf_op jit(solution)/shard_map/ppermute | solution.py:72
  278.0 10.0 %collective-permute-start.36 = (bf16[128,1536]{1,0:T(8,128)(2,1)}, bf16[128,1536]{1,0:T(8,128)(2,1)}, u32[]{:S(2)}, u32[]{:S(2)}) collective-permute-start(bf16[128,1536]{1,0:T(8,128)(2,1)} %get-tuple-element.502), channel_id=1, source_target_pairs={{24,16},{25,17},{26,18},{27,19},{28,20},{29,21},{30,22},{31,23}} | collective-permute-start | bytes 1179656 | tf_op jit(solution)/shard_map/ppermute | solution.py:117
  290.3 14.6 %collective-permute-start.14 = (bf16[128,1536]{1,0:T(8,128)(2,1)}, bf16[128,1536]{1,0:T(8,128)(2,1)}, u32[]{:S(2)}, u32[]{:S(2)}) collective-permute-start(bf16[128,1536]{1,0:T(8,128)(2,1)} %get-tuple-element.296), channel_id=1, source_target_pairs={{0,8},{8,16},{1,9},{9,17},{2,10},{10,18},{3,11},{11,19},{4,12},{12... | collective-permute-start | bytes 1179656 | tf_op jit(solution)/shard_map/cond/branch_1_fun/ppermute | solution.py:112
  293.7 11.2 %collective-permute-start.16 = (bf16[128,1536]{1,0:T(8,128)(2,1)S(1)}, bf16[128,1536]{1,0:T(8,128)(2,1)S(1)}, u32[]{:S(2)}, u32[]{:S(2)}) collective-permute-start(bf16[128,1536]{1,0:T(8,128)(2,1)S(1)} %get-tuple-element.300), channel_id=1, source_target_pairs={{0,1},{1,0},{2,3},{3,2},{4,5},{5,4},{6,7},{7,6},{8,9},{9,8},{10,11... | collective-permute-start | bytes 1179656 | tf_op jit(solution)/shard_map/cond/branch_1_fun/ppermute | solution.py:72
  295.4 9.5 %collective-permute-start.15 = (bf16[128,1536]{1,0:T(8,128)(2,1)}, bf16[128,1536]{1,0:T(8,128)(2,1)S(1)}, u32[]{:S(2)}, u32[]{:S(2)}) collective-permute-start(bf16[128,1536]{1,0:T(8,128)(2,1)} %get-tuple-element.297), channel_id=1, source_target_pairs={{16,8},{24,16},{17,9},{25,17},{18,10},{26,18},{19,11},{27,19},{20,... | collective-permute-start | bytes 1179656 | tf_op jit(solution)/shard_map/cond/branch_1_fun/ppermute | solution.py:117
  306.6 15.5 %collective-permute-start.17 = (bf16[128,1536]{1,0:T(8,128)(2,1)S(1)}, bf16[128,1536]{1,0:T(8,128)(2,1)S(1)}, u32[]{:S(2)}, u32[]{:S(2)}) collective-permute-start(bf16[128,1536]{1,0:T(8,128)(2,1)S(1)} %get-tuple-element.308), channel_id=1, source_target_pairs={{0,8},{8,16},{16,24},{1,9},{9,17},{17,25},{2,10},{10,18},{18,26},{... | collective-permute-start | bytes 1179656 | tf_op jit(solution)/shard_map/cond/branch_1_fun/ppermute | solution.py:112
  313.4 8.7 %collective-permute-start.19 = (bf16[128,1536]{1,0:T(8,128)(2,1)S(1)}, bf16[128,1536]{1,0:T(8,128)(2,1)S(1)}, u32[]{:S(2)}, u32[]{:S(2)}) collective-permute-start(bf16[128,1536]{1,0:T(8,128)(2,1)S(1)} %get-tuple-element.310), channel_id=1, source_target_pairs={{0,1},{1,0},{2,3},{3,2},{4,5},{5,4},{6,7},{7,6},{8,9},{9,8},{10,11... | collective-permute-start | bytes 1179656 | tf_op jit(solution)/shard_map/cond/branch_1_fun/ppermute | solution.py:72
  314.2 10.4 %collective-permute-start.18 = (bf16[128,1536]{1,0:T(8,128)(2,1)S(1)}, bf16[128,1536]{1,0:T(8,128)(2,1)S(1)}, u32[]{:S(2)}, u32[]{:S(2)}) collective-permute-start(bf16[128,1536]{1,0:T(8,128)(2,1)S(1)} %get-tuple-element.309), channel_id=1, source_target_pairs={{8,0},{16,8},{24,16},{9,1},{17,9},{25,17},{10,2},{18,10},{26,18},{... | collective-permute-start | bytes 1179656 | tf_op jit(solution)/shard_map/cond/branch_1_fun/ppermute | solution.py:117
  331.9 37.2 %collective-permute-start.39 = (bf16[384,2304]{1,0:T(8,128)(2,1)S(1)}, bf16[384,2304]{1,0:T(8,128)(2,1)}, u32[]{:S(2)}, u32[]{:S(2)}) collective-permute-start(bf16[384,2304]{1,0:T(8,128)(2,1)S(1)} %copy-done.29), channel_id=1, source_target_pairs={{0,4},{2,6},{4,0},{6,2},{1,5},{3,7},{5,1},{7,3},{8,12},{10,14},{12... | collective-permute-start | bytes 5308424 | tf_op jit(solution)/shard_map/ppermute | solution.py:72
  336.7 40.9 %collective-permute-start.38 = (bf16[128,1536]{1,0:T(8,128)(2,1)S(1)}, bf16[128,1536]{1,0:T(8,128)(2,1)}, u32[]{:S(2)}, u32[]{:S(2)}) collective-permute-start(bf16[128,1536]{1,0:T(8,128)(2,1)S(1)} %add_convert_fusion.3), channel_id=1, source_target_pairs={{0,1},{1,0},{2,3},{3,2},{4,5},{5,4},{6,7},{7,6},{8,9},{9,8},{10,11... | collective-permute-start | bytes 1179656 | tf_op jit(solution)/shard_map/ppermute | solution.py:72
  377.7 32.4 %collective-permute-start.40 = (bf16[384,1152]{1,0:T(8,128)(2,1)}, bf16[384,1152]{1,0:T(8,128)(2,1)}, u32[]{:S(2)}, u32[]{:S(2)}) collective-permute-start(bf16[384,1152]{1,0:T(8,128)(2,1)} %get-tuple-element.521), channel_id=1, source_target_pairs={{0,4},{2,6},{4,0},{6,2},{1,5},{3,7},{5,1},{7,3},{8,12},{10,14},{12... | collective-permute-start | bytes 2654216 | tf_op jit(solution)/shard_map/ppermute | solution.py:72
  379.4 30.1 %collective-permute-start.42 = (bf16[96,2304]{1,0:T(8,128)(2,1)}, bf16[96,2304]{1,0:T(8,128)(2,1)}, u32[]{:S(2)}, u32[]{:S(2)}) collective-permute-start(bf16[96,2304]{1,0:T(8,128)(2,1)} %get-tuple-element.524), channel_id=1, source_target_pairs={{0,24},{8,0},{16,8},{24,16},{1,25},{9,1},{17,9},{25,17},{2,26},{10... | collective-permute-start | bytes 1327112 | tf_op jit(solution)/shard_map/ppermute | solution.py:67
  380.6 29.5 %collective-permute-start.41 = (bf16[96,2304]{1,0:T(8,128)(2,1)}, bf16[96,2304]{1,0:T(8,128)(2,1)}, u32[]{:S(2)}, u32[]{:S(2)}) collective-permute-start(bf16[96,2304]{1,0:T(8,128)(2,1)} %get-tuple-element.523), channel_id=1, source_target_pairs={{0,8},{8,16},{16,24},{24,0},{1,9},{9,17},{17,25},{25,1},{2,10},{10... | collective-permute-start | bytes 1327112 | tf_op jit(solution)/shard_map/ppermute | solution.py:67
  407.7 9.8 %collective-permute-start.58 = (f32[1,1536]{1,0:T(1,128)}, f32[1,1536]{1,0:T(1,128)}, u32[]{:S(2)}, u32[]{:S(2)}) collective-permute-start(f32[1,1536]{1,0:T(1,128)} %broadcast_in_dim.111), channel_id=1, source_target_pairs={{0,1},{1,0},{2,3},{3,2},{4,5},{5,4},{6,7},{7,6},{8,9},{9,8},{10,11... | collective-permute-start | bytes 18440 | tf_op jit(solution)/shard_map/ppermute | solution.py:72
  410.1 18.4 %collective-permute-start.44 = (bf16[768,768]{1,0:T(8,128)(2,1)}, bf16[768,768]{1,0:T(8,128)(2,1)}, u32[]{:S(2)}, u32[]{:S(2)}) collective-permute-start(bf16[768,768]{1,0:T(8,128)(2,1)} %get-tuple-element.528), channel_id=1, source_target_pairs={{0,2},{2,0},{4,6},{6,4},{1,3},{3,1},{5,7},{7,5},{8,10},{10,8},{12,... | collective-permute-start | bytes 3538952 | tf_op jit(solution)/shard_map/ppermute | solution.py:72
  415.3 33.2 %collective-permute-start.47 = (bf16[96,2304]{1,0:T(8,128)(2,1)}, bf16[96,2304]{1,0:T(8,128)(2,1)}, u32[]{:S(2)}, u32[]{:S(2)}) collective-permute-start(bf16[96,2304]{1,0:T(8,128)(2,1)} %get-tuple-element.536), channel_id=1, source_target_pairs={{0,16},{8,24},{16,0},{24,8},{1,17},{9,25},{17,1},{25,9},{2,18},{10... | collective-permute-start | bytes 1327112 | tf_op jit(solution)/shard_map/ppermute | solution.py:67
  419.6 7.7 %collective-permute-start.46 = (bf16[2,256,128]{2,1,0:T(8,128)(2,1)}, bf16[2,256,128]{2,1,0:T(8,128)(2,1)}, u32[]{:S(2)}, u32[]{:S(2)}) collective-permute-start(bf16[2,256,128]{2,1,0:T(8,128)(2,1)} %get-tuple-element.532), channel_id=1, source_target_pairs={{0,6},{2,4},{4,2},{6,0},{1,7},{3,5},{5,3},{7,1},{8,14},{10,12},{12... | collective-permute-start | bytes 393224 | tf_op jit(solution)/shard_map/ppermute | solution.py:72
  420.6 8.0 %collective-permute-start.45 = (bf16[2,256,128]{2,1,0:T(8,128)(2,1)}, bf16[2,256,128]{2,1,0:T(8,128)(2,1)}, u32[]{:S(2)}, u32[]{:S(2)}) collective-permute-start(bf16[2,256,128]{2,1,0:T(8,128)(2,1)} %get-tuple-element.530), channel_id=1, source_target_pairs={{0,4},{2,6},{4,0},{6,2},{1,5},{3,7},{5,1},{7,3},{8,12},{10,14},{12... | collective-permute-start | bytes 393224 | tf_op jit(solution)/shard_map/ppermute | solution.py:72
  421.3 7.2 %collective-permute-start.43 = (bf16[2,256,128]{2,1,0:T(8,128)(2,1)}, bf16[2,256,128]{2,1,0:T(8,128)(2,1)}, u32[]{:S(2)}, u32[]{:S(2)}) collective-permute-start(bf16[2,256,128]{2,1,0:T(8,128)(2,1)} %get-tuple-element.525), channel_id=1, source_target_pairs={{0,2},{2,0},{4,6},{6,4},{1,3},{3,1},{5,7},{7,5},{8,10},{10,8},{12,... | collective-permute-start | bytes 393224 | tf_op jit(solution)/shard_map/ppermute | solution.py:72
  430.9 37.9 %collective-permute-start.48 = (bf16[384,768]{1,0:T(8,128)(2,1)}, bf16[384,768]{1,0:T(8,128)(2,1)}, u32[]{:S(2)}, u32[]{:S(2)}) collective-permute-start(bf16[384,768]{1,0:T(8,128)(2,1)} %fusion.156), channel_id=1, source_target_pairs={{0,4},{2,6},{4,0},{6,2},{1,5},{3,7},{5,1},{7,3},{8,12},{10,14},{12... | collective-permute-start | bytes 1769480 | tf_op jit(solution)/shard_map/ppermute | solution.py:72
  433.0 28.6 %collective-permute-start.49 = (bf16[96,1152]{1,0:T(8,128)(2,1)}, bf16[96,1152]{1,0:T(8,128)(2,1)}, u32[]{:S(2)}, u32[]{:S(2)}) collective-permute-start(bf16[96,1152]{1,0:T(8,128)(2,1)} %get-tuple-element.729), channel_id=1, source_target_pairs={{0,8},{8,16},{16,24},{24,0},{1,9},{9,17},{17,25},{25,1},{2,10},{10... | collective-permute-start | bytes 663560 | tf_op jit(solution)/shard_map/ppermute | solution.py:67
  434.0 27.6 %collective-permute-start.50 = (bf16[96,1152]{1,0:T(8,128)(2,1)}, bf16[96,1152]{1,0:T(8,128)(2,1)}, u32[]{:S(2)}, u32[]{:S(2)}) collective-permute-start(bf16[96,1152]{1,0:T(8,128)(2,1)} %get-tuple-element.728), channel_id=1, source_target_pairs={{0,16},{8,24},{16,0},{24,8},{1,17},{9,25},{17,1},{25,9},{2,18},{10... | collective-permute-start | bytes 663560 | tf_op jit(solution)/shard_map/ppermute | solution.py:67
  434.6 27.1 %collective-permute-start.51 = (bf16[96,1152]{1,0:T(8,128)(2,1)}, bf16[96,1152]{1,0:T(8,128)(2,1)}, u32[]{:S(2)}, u32[]{:S(2)}) collective-permute-start(bf16[96,1152]{1,0:T(8,128)(2,1)} %get-tuple-element.727), channel_id=1, source_target_pairs={{0,24},{8,0},{16,8},{24,16},{1,25},{9,1},{17,9},{25,17},{2,26},{10... | collective-permute-start | bytes 663560 | tf_op jit(solution)/shard_map/ppermute | solution.py:67
  464.0 21.6 %collective-permute-start.52 = (bf16[384,1024]{1,0:T(8,128)(2,1)}, bf16[384,1024]{1,0:T(8,128)(2,1)}, u32[]{:S(2)}, u32[]{:S(2)}) collective-permute-start(bf16[384,1024]{1,0:T(8,128)(2,1)} %copy.68), channel_id=1, source_target_pairs={{0,4},{2,6},{4,0},{6,2},{1,5},{3,7},{5,1},{7,3},{8,12},{10,14},{12... | collective-permute-start | bytes 2359304 | tf_op jit(solution)/shard_map/ppermute | solution.py:72
  468.3 19.6 %collective-permute-start.57 = (bf16[256,1536]{1,0:T(8,128)(2,1)}, bf16[256,1536]{1,0:T(8,128)(2,1)}, u32[]{:S(2)}, u32[]{:S(2)}) collective-permute-start(bf16[256,1536]{1,0:T(8,128)(2,1)} %get-tuple-element.557), channel_id=1, source_target_pairs={{0,1},{1,0},{2,3},{3,2},{4,5},{5,4},{6,7},{7,6},{8,9},{9,8},{10,11... | collective-permute-start | bytes 2359304 | tf_op jit(solution)/shard_map/ppermute | solution.py:72
  471.3 11.8 %collective-permute-start.53 = (bf16[96,768]{1,0:T(8,128)(2,1)}, bf16[96,768]{1,0:T(8,128)(2,1)}, u32[]{:S(2)}, u32[]{:S(2)}) collective-permute-start(bf16[96,768]{1,0:T(8,128)(2,1)} %get-tuple-element.726), channel_id=1, source_target_pairs={{0,8},{8,16},{16,24},{24,0},{1,9},{9,17},{17,25},{25,1},{2,10},{10... | collective-permute-start | bytes 442376 | tf_op jit(solution)/shard_map/ppermute | solution.py:67
  471.3 14.2 %collective-permute-start.54 = (bf16[96,768]{1,0:T(8,128)(2,1)}, bf16[96,768]{1,0:T(8,128)(2,1)}, u32[]{:S(2)}, u32[]{:S(2)}) collective-permute-start(bf16[96,768]{1,0:T(8,128)(2,1)} %get-tuple-element.725), channel_id=1, source_target_pairs={{0,16},{8,24},{16,0},{24,8},{1,17},{9,25},{17,1},{25,9},{2,18},{10... | collective-permute-start | bytes 442376 | tf_op jit(solution)/shard_map/ppermute | solution.py:67
  471.3 14.2 %collective-permute-start.55 = (bf16[96,768]{1,0:T(8,128)(2,1)}, bf16[96,768]{1,0:T(8,128)(2,1)}, u32[]{:S(2)}, u32[]{:S(2)}) collective-permute-start(bf16[96,768]{1,0:T(8,128)(2,1)} %get-tuple-element.724), channel_id=1, source_target_pairs={{0,24},{8,0},{16,8},{24,16},{1,25},{9,1},{17,9},{25,17},{2,26},{10... | collective-permute-start | bytes 442376 | tf_op jit(solution)/shard_map/ppermute | solution.py:67
  491.7 6.5 %collective-permute-start.60 = (f32[1,4096]{1,0:T(1,128)S(1)}, f32[1,4096]{1,0:T(1,128)S(1)}, u32[]{:S(2)}, u32[]{:S(2)}) collective-permute-start(f32[1,4096]{1,0:T(1,128)S(1)} %fusion.242), channel_id=1, source_target_pairs={{0,4},{2,6},{4,0},{6,2},{1,5},{3,7},{5,1},{7,3},{8,12},{10,14},{12... | collective-permute-start | bytes 49160 | tf_op jit(solution)/shard_map/ppermute | solution.py:72
  493.1 23.6 %collective-permute-start.63 = (bf16[96,1024]{1,0:T(8,128)(2,1)S(1)}, bf16[96,1024]{1,0:T(8,128)(2,1)S(1)}, u32[]{:S(2)}, u32[]{:S(2)}) collective-permute-start(bf16[96,1024]{1,0:T(8,128)(2,1)S(1)} %get-tuple-element.721), channel_id=1, source_target_pairs={{0,8},{8,16},{16,24},{24,0},{1,9},{9,17},{17,25},{25,1},{2,10},{10... | collective-permute-start | bytes 589832 | tf_op jit(solution)/shard_map/ppermute | solution.py:67
  495.8 20.9 %collective-permute-start.64 = (bf16[96,1024]{1,0:T(8,128)(2,1)S(1)}, bf16[96,1024]{1,0:T(8,128)(2,1)S(1)}, u32[]{:S(2)}, u32[]{:S(2)}) collective-permute-start(bf16[96,1024]{1,0:T(8,128)(2,1)S(1)} %get-tuple-element.723), channel_id=1, source_target_pairs={{0,16},{8,24},{16,0},{24,8},{1,17},{9,25},{17,1},{25,9},{2,18},{10... | collective-permute-start | bytes 589832 | tf_op jit(solution)/shard_map/ppermute | solution.py:67
  496.0 20.7 %collective-permute-start.65 = (bf16[96,1024]{1,0:T(8,128)(2,1)S(1)}, bf16[96,1024]{1,0:T(8,128)(2,1)S(1)}, u32[]{:S(2)}, u32[]{:S(2)}) collective-permute-start(bf16[96,1024]{1,0:T(8,128)(2,1)S(1)} %get-tuple-element.722), channel_id=1, source_target_pairs={{0,24},{8,0},{16,8},{24,16},{1,25},{9,1},{17,9},{25,17},{2,26},{10... | collective-permute-start | bytes 589832 | tf_op jit(solution)/shard_map/ppermute | solution.py:67
  498.2 12.5 %collective-permute-start.61 = (f32[1,4096]{1,0:T(1,128)S(1)}, f32[1,4096]{1,0:T(1,128)S(1)}, u32[]{:S(2)}, u32[]{:S(2)}) collective-permute-start(f32[1,4096]{1,0:T(1,128)S(1)} %add.495), channel_id=1, source_target_pairs={{0,8},{8,0},{16,24},{24,16},{1,9},{9,1},{17,25},{25,17},{2,10},{10... | collective-permute-start | bytes 49160 | tf_op jit(solution)/shard_map/ppermute | solution.py:72
  498.3 19.5 %collective-permute-start.56 = (bf16[128,1536]{1,0:T(8,128)(2,1)S(1)}, bf16[128,1536]{1,0:T(8,128)(2,1)S(1)}, u32[]{:S(2)}, u32[]{:S(2)}) collective-permute-start(bf16[128,1536]{1,0:T(8,128)(2,1)S(1)} %get-tuple-element.554), channel_id=1, source_target_pairs={{0,1},{1,0},{2,3},{3,2},{4,5},{5,4},{6,7},{7,6},{8,9},{9,8},{10,11... | collective-permute-start | bytes 1179656 | tf_op jit(solution)/shard_map/ppermute | solution.py:72
  (70 other events, 620.3 us)
Sparse Core Ops, SparseCore 0:
  14.4 67.2 all-gather.5
  84.5 76.2 all-gather.3
  330.5 82.0 reduce-scatter.1
